TPU v7x, 512 devices: a whole 4x8x8 slice. The times are simulated.
512 devices in a mesh: sweep: 16 (over x, y_lo), azim: 32 (over y_hi, z, core).
Axes of the slice: x: 4, y: 8 (y_hi: 2, y_lo: 4; y = y_hi * 4 + y_lo), z: 8, core: 2. Of those that a mesh axis runs over, the one named last changes fastest.
Arguments:
- latents: bfloat16 [32, 8, 1024, 512], P('sweep', None, 'azim'), may hold values from -6 to 6
- cotangent: bfloat16 [32, 8, 1024, 512], P('sweep', None, 'azim'), may hold values from -6 to 6
- conv_kernel: float32 [9, 512], replicated, may hold values from -2 to 2
- conv_bias: float32 [512], replicated, may hold values from -3 to 3
- norm_gain: float32 [512], replicated, may hold values from 0.25 to 1.75
- w_query: bfloat16 [512, 256], replicated, may hold values from -2 to 2
- w_key: bfloat16 [512, 256], replicated, may hold values from -2 to 2
- w_value: bfloat16 [512, 256], replicated, may hold values from -0.25 to 0.25
- w_output: bfloat16 [512, 256], replicated, may hold values from -0.375 to 0.375
Outputs:
- grad_latents: float32 [32, 8, 1024, 512], P('sweep', None, 'azim')
- grad_kernel: float32 [9, 512], replicated
- grad_bias: float32 [512], replicated
- grad_gain: float32 [512], replicated
- grad_query: float32 [512, 256], P('azim')
- grad_key: float32 [512, 256], P('azim')
- grad_value: float32 [512, 256], P('azim')
- grad_output: float32 [512, 256], P('azim')
All inputs are finite; a program needn't handle non-finite values.
Results may differ from a plain program's by a relative error of at most 0.01.
The roundings to bfloat16 on the way count: a program that leaves them out, or rounds other values in their place, can miss the bound.
Values may be sent and summed in bfloat16 or wider, within the bound.
No kernel may reach another device: no remote copies, remote signals or barrier semaphores. Data moves between devices by JAX's collectives and lax.ppermute only.
A program may use at most 64 MiB of HBM per device.

v0:
```python
import math

import jax
import jax.numpy as jnp
from jax import lax
from jax.sharding import PartitionSpec as P

DH = 64


EPS = 1e-06


def extended(value, sides, width):
    for axis, dim in sides:
        size, length = (lax.axis_size(axis), value.shape[dim])
        up = [(i, (i + 1) % size) for i in range(size)]
        down = [(j, i) for i, j in up]
        last = lax.slice_in_dim(value, length - width, length, axis=dim)
        leading = lax.slice_in_dim(value, 0, width, axis=dim)
        before = lax.ppermute(last, axis, up)
        after = lax.ppermute(leading, axis, down)
        value = jnp.concatenate([before, value, after], axis=dim)
    return value


def silu_slope(value):
    sigmoid_val = jax.nn.sigmoid(value)
    return sigmoid_val * (1.0 + value * (1.0 - sigmoid_val))


def outer_sum(left, right):
    return lax.dot_general(
        left, right, (((0,), (0,)), ((), ())), preferred_element_type=jnp.float32
    )


def attend(y_block, cot_block, w_query, w_key, w_value, w_output, norm_gain):
    sweeps, pixels, channels = y_block.shape
    heads = w_query.shape[1] // DH
    scale = 1.0 / math.sqrt(DH)
    y_float = y_block.astype(jnp.float32)
    root = jnp.sqrt(jnp.mean(y_float * y_float, axis=-1, keepdims=True) + EPS)
    inverse = 1.0 / root
    normed = (y_float * inverse * norm_gain).astype(jnp.bfloat16)
    rows = normed.reshape(sweeps * pixels, channels)
    query = jnp.dot(rows, w_query, preferred_element_type=jnp.float32).astype(jnp.bfloat16)
    key = jnp.dot(rows, w_key, preferred_element_type=jnp.float32).astype(jnp.bfloat16)
    value = jnp.dot(rows, w_value, preferred_element_type=jnp.float32).astype(jnp.bfloat16)
    query4 = query.reshape(sweeps, pixels, heads, DH)
    key4 = key.reshape(sweeps, pixels, heads, DH)
    value4 = value.reshape(sweeps, pixels, heads, DH)
    scores = jnp.einsum("tphd,uphd->phtu", query4, key4, preferred_element_type=jnp.float32) * scale
    row_max = jnp.max(scores, axis=-1, keepdims=True)
    expon = jnp.exp(scores - row_max)
    probs = expon / jnp.sum(expon, axis=-1, keepdims=True)
    probs_low = probs.astype(jnp.bfloat16)
    attended = jnp.einsum(
        "phtu,uphd->tphd", probs_low, value4, preferred_element_type=jnp.float32
    ).astype(jnp.bfloat16)
    attended_rows = attended.reshape(sweeps * pixels, heads * DH)
    cot_rows = cot_block.reshape(sweeps * pixels, channels)
    grad_output = outer_sum(cot_rows, attended_rows)
    grad_attended = jnp.dot(cot_rows, w_output, preferred_element_type=jnp.float32).astype(
        jnp.bfloat16
    )
    grad_att4 = grad_attended.reshape(sweeps, pixels, heads, DH)
    grad_probs = jnp.einsum(
        "tphd,uphd->phtu", grad_att4, value4, preferred_element_type=jnp.float32
    )
    grad_scores = (
        probs * (grad_probs - jnp.sum(probs * grad_probs, axis=-1, keepdims=True)) * scale
    ).astype(jnp.bfloat16)
    grad_v = jnp.einsum(
        "phtu,tphd->uphd", probs_low, grad_att4, preferred_element_type=jnp.float32
    ).astype(jnp.bfloat16)
    grad_q = jnp.einsum(
        "phtu,uphd->tphd", grad_scores, key4, preferred_element_type=jnp.float32
    ).astype(jnp.bfloat16)
    grad_k = jnp.einsum(
        "phtu,tphd->uphd", grad_scores, query4, preferred_element_type=jnp.float32
    ).astype(jnp.bfloat16)
    grad_q = grad_q.reshape(sweeps * pixels, heads * DH)
    grad_k = grad_k.reshape(sweeps * pixels, heads * DH)
    grad_v = grad_v.reshape(sweeps * pixels, heads * DH)
    grad_query = outer_sum(rows, grad_q)
    grad_key = outer_sum(rows, grad_k)
    grad_value = outer_sum(rows, grad_v)
    stacked_grads = jnp.concatenate([grad_q, grad_k, grad_v], axis=-1)
    stacked_weights = jnp.concatenate([w_query, w_key, w_value], axis=-1)
    grad_normed = lax.dot_general(
        stacked_grads, stacked_weights, (((1,), (1,)), ((), ())), preferred_element_type=jnp.float32
    )
    grad_normed = grad_normed.reshape(sweeps, pixels, channels)
    grad_gain = jnp.sum(grad_normed * y_float * inverse, axis=(0, 1))
    gained = grad_normed * norm_gain
    grad_attn = (
        inverse
        * (
            gained
            - y_float * jnp.mean(gained * y_float, axis=-1, keepdims=True) * inverse * inverse
        )
    ).astype(jnp.bfloat16)
    return (grad_attn, grad_query, grad_key, grad_value, grad_output, grad_gain)


def on_device(
    latents, cotangent, conv_kernel, conv_bias, norm_gain, w_query, w_key, w_value, w_output
):
    sweep_local, height, azim_local, channels = latents.shape
    groups = lax.axis_size("sweep")
    strips = lax.axis_size("azim")
    pixels_each = height * azim_local // groups
    framed = extended(latents, (("azim", 2),), 1)
    activation = jnp.pad(jax.nn.silu(framed.astype(jnp.float32)), ((0, 0), (1, 1), (0, 0), (0, 0)))
    conv_sum = jnp.zeros(latents.shape, jnp.float32)
    for row_tap in range(3):
        for col_tap in range(3):
            conv_sum = (
                conv_sum
                + conv_kernel[3 * row_tap + col_tap]
                * activation[:, row_tap : row_tap + height, col_tap : col_tap + azim_local]
            )
    y_local = (latents.astype(jnp.float32) + conv_sum + conv_bias).astype(jnp.bfloat16)
    y_split = y_local.reshape(sweep_local, groups, pixels_each, channels)
    cot_split = cotangent.reshape(sweep_local, groups, pixels_each, channels)
    y_pix, cot_pix = (
        lax.all_to_all(y_split, "sweep", split_axis=1, concat_axis=0, tiled=True),
        lax.all_to_all(cot_split, "sweep", split_axis=1, concat_axis=0, tiled=True),
    )
    total_sweeps = sweep_local * groups
    y_pix = y_pix.reshape(total_sweeps, pixels_each, channels)
    cot_pix = cot_pix.reshape(total_sweeps, pixels_each, channels)
    grad_attn, grad_query, grad_key, grad_value, grad_output, grad_gain = attend(
        y_pix, cot_pix, w_query, w_key, w_value, w_output, norm_gain
    )
    returned = lax.all_to_all(
        grad_attn.reshape(total_sweeps, 1, pixels_each, channels),
        "sweep",
        split_axis=0,
        concat_axis=1,
        tiled=True,
    )
    returned = returned.reshape(sweep_local, height, azim_local, channels)
    grad_y = cotangent.astype(jnp.float32) + returned.astype(jnp.float32)
    framed_grad = extended(grad_y, (("azim", 2),), 1)
    framed_grad = jnp.pad(framed_grad, ((0, 0), (1, 1), (0, 0), (0, 0)))
    grad_act = jnp.zeros(grad_y.shape, jnp.float32)
    taps = []
    for row_tap in range(3):
        for col_tap in range(3):
            weight = conv_kernel[3 * row_tap + col_tap]
            grad_act = (
                grad_act
                + weight
                * framed_grad[
                    :, 2 - row_tap : 2 - row_tap + height, 2 - col_tap : 2 - col_tap + azim_local
                ]
            )
            taps.append(
                jnp.sum(
                    grad_y
                    * activation[:, row_tap : row_tap + height, col_tap : col_tap + azim_local],
                    axis=(0, 1, 2),
                )
            )
    latent_float = latents.astype(jnp.float32)
    grad_latents = grad_y + grad_act * silu_slope(latent_float)
    predivide = 1.0 / math.sqrt(total_sweeps * height * azim_local * strips)
    tap_terms = jnp.stack(taps) * predivide
    bias_terms = jnp.sum(grad_y, axis=(0, 1, 2)) * predivide
    gain_terms = grad_gain * predivide
    query_terms = grad_query * predivide
    key_terms = grad_key * predivide
    value_terms = grad_value * predivide
    output_terms = grad_output * predivide
    summed = lax.psum((query_terms, key_terms, value_terms, output_terms), ("sweep", "azim"))
    rows_each = channels // strips
    start = lax.axis_index("azim") * rows_each
    shares = tuple((lax.dynamic_slice_in_dim(whole, start, rows_each, 0) for whole in summed))
    grad_kernel, grad_bias, gain_total = lax.psum(
        (tap_terms, bias_terms, gain_terms), ("sweep", "azim")
    )
    return (
        grad_latents,
        grad_kernel,
        grad_bias,
        gain_total,
        shares[0],
        shares[1],
        shares[2],
        shares[3],
    )


def solution(mesh):
    in_specs = (
        P("sweep", None, "azim", None),
        P("sweep", None, "azim", None),
        P(),
        P(),
        P(),
        P(),
        P(),
        P(),
        P(),
    )
    out_specs = (
        P("sweep", None, "azim", None),
        P(),
        P(),
        P(),
        P("azim", None),
        P("azim", None),
        P("azim", None),
        P("azim", None),
    )
    return jax.shard_map(
        on_device, mesh=mesh, in_specs=in_specs, out_specs=out_specs, check_vma=False
    )
```

profile of v0, /device:TPU:1, one launch (start us, length us, event | category | flops | bytes accessed | tf_op | source)
XLA Modules:
  0.0 400.9 jit_solution(8135872142558860999)
XLA Ops:
  7.2 1.9 copy.68
  9.1 8.1 %all-to-all-start.1 = ((bf16[2,16,16,512]{3,2,0,1:T(8,128)(2,1)}), bf16[2,16,16,512]{3,2,0,1:T(8,128)(2,1)S(1)}, u32[]{:S(2)}, u32[]{:S(2)}) async-start(bf16[2,16,16,512]{3,2,0,1:T(8,128)(2,1)} %copy.68), calls=%async_computation.1 | async-start | bytes 1048576 | tf_op jit(solution)/shard_map/all_to_all | solution.py:129
  17.4 4.8 %collective-permute-start = (bf16[2,8,1,512]{3,2,1,0:T(2,128)(2,1)S(1)}, bf16[2,8,1,512]{3,2,1,0:T(2,128)(2,1)S(1)}, u32[]{:S(2)}, u32[]{:S(2)}) collective-permute-start(bf16[2,8,1,512]{3,2,1,0:T(2,128)(2,1)S(1)} %get-tuple-element.62), channel_id=1, source_target_pairs={{0,1},{1,2},{2,3},{3,4},{4,5},{5,6},{6,7},{7,8},{8,9},{9,10},{10,1... | collective-permute-start | bytes 49160 | tf_op jit(solution)/shard_map/ppermute | solution.py:21
  22.2 1.9 collective-permute-start.1
  24.2 3.6 collective-permute-done.1
  29.9 2.8 all-to-all-done.1
  32.7 4.6 %all-to-all-start = ((bf16[2,16,16,512]{3,2,0,1:T(8,128)(2,1)}), bf16[2,16,16,512]{3,2,0,1:T(8,128)(2,1)S(1)}, u32[]{:S(2)}, u32[]{:S(2)}) async-start(bf16[2,16,16,512]{3,2,0,1:T(8,128)(2,1)} %copy.65), calls=%async_computation | async-start | bytes 1048576 | tf_op jit(solution)/shard_map/all_to_all | solution.py:128
  38.7 9.8 %all-to-all-done = bf16[2,16,16,512]{3,2,0,1:T(8,128)(2,1)S(1)} async-done(((bf16[2,16,16,512]{3,2,0,1:T(8,128)(2,1)}), bf16[2,16,16,512]{3,2,0,1:T(8,128)(2,1)S(1)}, u32[]{:S(2)}, u32[]{:S(2)}) %all-to-all-start) | async-done | bytes 524320 | tf_op jit(solution)/shard_map/all_to_all | solution.py:128
  49.0 1.2 convolution_convert_fusion.7
  55.9 3.2 fusion.93
  59.1 2.9 fusion.67
  62.0 1.3 fusion.13
  63.3 3.9 fusion.12
  67.2 3.9 fusion.14
  71.1 2.6 fusion.15
  74.3 1.3 copy.73
  76.6 1.3 copy.75
  79.0 1.3 copy.77
  81.6 2.2 convolution_multiply_fusion.4
  83.8 1.7 fusion.40
  87.9 4.2 %all-to-all-start.2 = ((bf16[32,1,16,512]{3,2,1,0:T(8,128)(2,1)}), bf16[32,1,16,512]{3,2,1,0:T(8,128)(2,1)}, u32[]{:S(2)}, u32[]{:S(2)}) async-start(bf16[32,1,16,512]{3,2,1,0:T(8,128)(2,1)} %multiply_convert_fusion), calls=%async_computation.2 | async-start | bytes 1048576 | tf_op jit(solution)/shard_map/all_to_all | solution.py:137
  92.4 2.1 convolution_multiply_fusion.3
  94.5 2.1 convolution_multiply_fusion.2
  97.8 5.5 %all-to-all-done.2 = bf16[32,1,16,512]{3,2,1,0:T(8,128)(2,1)} async-done(((bf16[32,1,16,512]{3,2,1,0:T(8,128)(2,1)}), bf16[32,1,16,512]{3,2,1,0:T(8,128)(2,1)}, u32[]{:S(2)}, u32[]{:S(2)}) %all-to-all-start.2) | async-done | bytes 524320 | tf_op jit(solution)/shard_map/all_to_all | solution.py:137
  104.6 1.3 multiply_reduce_fusion
  106.0 14.5 %collective-permute-start.2 = (f32[2,8,1,512]{3,2,1,0:T(1,128)S(1)}, f32[2,8,1,512]{3,2,1,0:T(1,128)S(1)}, u32[]{:S(2)}, u32[]{:S(2)}) collective-permute-start(f32[2,8,1,512]{3,2,1,0:T(1,128)S(1)} %get-tuple-element.60), channel_id=1, source_target_pairs={{0,1},{1,2},{2,3},{3,4},{4,5},{5,6},{6,7},{7,8},{8,9},{9,10},{10,1... | collective-permute-start | bytes 98312 | tf_op jit(solution)/shard_map/ppermute | solution.py:21
  120.5 2.5 collective-permute-start.3
  123.1 104.7 %all-reduce.2 = (f32[9,512]{1,0:T(8,128)}, f32[512]{0:T(512)}, f32[512]{0:T(512)}) all-reduce(f32[9,512]{1,0:T(8,128)S(1)} %broadcast_multiply_fusion, f32[512]{0:T(512)S(1)} %broadcast_multiply_fusion.2, f32[512]{0:T(512)S(1)} %broadcast_multiply_fusion.1), channel_id=1, replica_groups=mesh['sweep'=16,'azim'=32] {'sweep','azim'}, use_global_device_ids=true, to_apply=%region_14.15 | all-reduce | flops 5632 | bytes 45056 | tf_op jit(solution)/shard_map/psum | solution.py:181
  228.0 2.3 fusion.25
  230.3 159.4 %all-reduce.6.cloned.1.call-done = (f32[512,256]{1,0:T(8,128)}, f32[512,256]{1,0:T(8,128)}, f32[512,256]{1,0:T(8,128)}, f32[512,256]{0,1:T(8,128)}) async-done(((f32[512,256]{1,0:T(8,128)}, f32[512,256]{1,0:T(8,128)}, f32[512,256]{1,0:T(8,128)}, f32[512,256]{0,1:T(8,128)}), (f32[512,256]{1,0:T(8,128)}, f32[512,256]{1,0:T(8,128)}, f32[512,256]{1,0:T(8,128)}, ...) | async-done | bytes 2097168 | tf_op jit(solution)/shard_map/psum | solution.py:177
  391.4 1.3 constant_dynamic-slice_fusion.3
  392.7 1.3 constant_dynamic-slice_fusion.1
  (80 shorter events, 20.9 us)
Async XLA Ops:
  7.2 30.1 %copy-start = (bf16[512,256]{1,0:T(8,128)(2,1)S(1)}, bf16[512,256]{1,0:T(8,128)(2,1)}, u32[]{:S(2)}) copy-start(bf16[512,256]{1,0:T(8,128)(2,1)} %param.17) | copy-start | bytes 786436
  7.2 10.1 %copy-start.1 = (bf16[2,8,32,512]{3,2,1,0:T(8,128)(2,1)S(1)}, bf16[2,8,32,512]{3,2,1,0:T(8,128)(2,1)}, u32[]{:S(2)}) copy-start(bf16[2,8,32,512]{3,2,1,0:T(8,128)(2,1)} %param.9) | copy-start | bytes 1572868
  7.2 16.9 %copy-start.16 = (f32[9,512]{1,0:T(8,128)S(1)}, f32[9,512]{1,0:T(8,128)}, u32[]{:S(2)}) copy-start(f32[9,512]{1,0:T(8,128)} %param.11) | copy-start | bytes 55300
  9.1 19.0 %copy-start.17 = (f32[512]{0:T(512)S(1)}, f32[512]{0:T(512)}, u32[]{:S(2)}) copy-start(f32[512]{0:T(512)} %param.12) | copy-start | bytes 6148
  9.1 23.5 %all-to-all-start.1 = ((bf16[2,16,16,512]{3,2,0,1:T(8,128)(2,1)}), bf16[2,16,16,512]{3,2,0,1:T(8,128)(2,1)S(1)}, u32[]{:S(2)}, u32[]{:S(2)}) async-start(bf16[2,16,16,512]{3,2,0,1:T(8,128)(2,1)} %copy.68), calls=%async_computation.1 | async-start | bytes 1048576 | tf_op jit(solution)/shard_map/all_to_all | solution.py:129
  17.4 6.8 %collective-permute-start = (bf16[2,8,1,512]{3,2,1,0:T(2,128)(2,1)S(1)}, bf16[2,8,1,512]{3,2,1,0:T(2,128)(2,1)S(1)}, u32[]{:S(2)}, u32[]{:S(2)}) collective-permute-start(bf16[2,8,1,512]{3,2,1,0:T(2,128)(2,1)S(1)} %get-tuple-element.62), channel_id=1, source_target_pairs={{0,1},{1,2},{2,3},{3,4},{4,5},{5,6},{6,7},{7,8},{8,9},{9,10},{10,1... | collective-permute-start | bytes 49160 | tf_op jit(solution)/shard_map/ppermute | solution.py:21
  22.2 5.5 %collective-permute-start.1 = (bf16[2,8,1,512]{3,2,1,0:T(2,128)(2,1)S(1)}, bf16[2,8,1,512]{3,2,1,0:T(2,128)(2,1)S(1)}, u32[]{:S(2)}, u32[]{:S(2)}) collective-permute-start(bf16[2,8,1,512]{3,2,1,0:T(2,128)(2,1)S(1)} %get-tuple-element.63), channel_id=1, source_target_pairs={{1,0},{2,1},{3,2},{4,3},{5,4},{6,5},{7,6},{8,7},{9,8},{10,9},{11,1... | collective-permute-start | bytes 49160 | tf_op jit(solution)/shard_map/ppermute | solution.py:22
  29.9 18.9 %copy-start.15 = (f32[512]{0:T(512)S(1)}, f32[512]{0:T(512)}, u32[]{:S(2)}) copy-start(f32[512]{0:T(512)} %param.13) | copy-start | bytes 6148
  32.7 16.0 %copy-start.2 = (bf16[2,16,16,512]{3,2,0,1:T(8,128)(2,1)}, bf16[2,16,16,512]{3,2,0,1:T(8,128)(2,1)S(1)}, u32[]{:S(2)}) copy-start(bf16[2,16,16,512]{3,2,0,1:T(8,128)(2,1)S(1)} %all-to-all-done.1) | copy-start | bytes 1572868
  32.7 15.8 %all-to-all-start = ((bf16[2,16,16,512]{3,2,0,1:T(8,128)(2,1)}), bf16[2,16,16,512]{3,2,0,1:T(8,128)(2,1)S(1)}, u32[]{:S(2)}, u32[]{:S(2)}) async-start(bf16[2,16,16,512]{3,2,0,1:T(8,128)(2,1)} %copy.65), calls=%async_computation | async-start | bytes 1048576 | tf_op jit(solution)/shard_map/all_to_all | solution.py:128
  55.9 3.2 copy-start.5
  59.1 2.9 copy-start.6
  59.1 2.9 copy-start.18
  71.1 2.6 copy-start.11
  81.4 2.4 copy-start.7
  81.4 2.4 copy-start.8
  81.4 2.4 copy-start.9
  81.4 2.4 copy-start.12
  81.4 2.4 copy-start.13
  81.4 2.4 copy-start.14
  85.6 1.2 copy-start.10
  87.9 15.4 %all-to-all-start.2 = ((bf16[32,1,16,512]{3,2,1,0:T(8,128)(2,1)}), bf16[32,1,16,512]{3,2,1,0:T(8,128)(2,1)}, u32[]{:S(2)}, u32[]{:S(2)}) async-start(bf16[32,1,16,512]{3,2,1,0:T(8,128)(2,1)} %multiply_convert_fusion), calls=%async_computation.2 | async-start | bytes 1048576 | tf_op jit(solution)/shard_map/all_to_all | solution.py:137
  92.2 4.5 %copy-start.3 = (bf16[2,16,16,512]{3,2,0,1:T(8,128)(2,1)S(1)}, bf16[2,16,16,512]{3,2,0,1:T(8,128)(2,1)}, u32[]{:S(2)}) copy-start(bf16[2,16,16,512]{3,2,0,1:T(8,128)(2,1)} %copy-done.2) | copy-start | bytes 1572868
  92.2 297.5 %all-reduce.6.cloned.1.call-start = ((), (), s32[]{:S(2)}) async-start(), calls=%async_computation.3 | async-start | bytes 4194304 | tf_op jit(solution)/shard_map/psum | solution.py:177
  103.3 1.3 copy-start.4
  106.0 121.7 %collective-permute-start.2 = (f32[2,8,1,512]{3,2,1,0:T(1,128)S(1)}, f32[2,8,1,512]{3,2,1,0:T(1,128)S(1)}, u32[]{:S(2)}, u32[]{:S(2)}) collective-permute-start(f32[2,8,1,512]{3,2,1,0:T(1,128)S(1)} %get-tuple-element.60), channel_id=1, source_target_pairs={{0,1},{1,2},{2,3},{3,4},{4,5},{5,6},{6,7},{7,8},{8,9},{9,10},{10,1... | collective-permute-start | bytes 98312 | tf_op jit(solution)/shard_map/ppermute | solution.py:21
  120.5 107.3 %collective-permute-start.3 = (f32[2,8,1,512]{3,2,1,0:T(1,128)S(1)}, f32[2,8,1,512]{3,2,1,0:T(1,128)S(1)}, u32[]{:S(2)}, u32[]{:S(2)}) collective-permute-start(f32[2,8,1,512]{3,2,1,0:T(1,128)S(1)} %get-tuple-element.61), channel_id=1, source_target_pairs={{1,0},{2,1},{3,2},{4,3},{5,4},{6,5},{7,6},{8,7},{9,8},{10,9},{11,1... | collective-permute-start | bytes 98312 | tf_op jit(solution)/shard_map/ppermute | solution.py:22
Sparse Core Ops, SparseCore 0:
  98.5 291.1 all-reduce.5
where the time goes:
time: 402 us; the launch traced here: 401 us
  waiting for transfers between devices  181 us (45%)
  blocking collectives  105 us (26%)
  starting transfers between devices  40.9 us (10%)
  matrix products  30.9 us (8%)
  local copies, waits for them, and re-layouts  20.7 us (5%)
  between operations  14.4 us (4%)
  other arithmetic  8.26 us (2%)
    psum x1, waiting for transfers between devices, on_device(): lax.psum((query_terms, key_terms, value_terms, output_terms), ('sweep', '...  159 us
    psum x1, blocking collectives, on_device(): lax.psum((tap_terms, bias_terms, gain_terms), ('sweep', 'azim'))  105 us
    ppermute x2, starting transfers between devices, extended(): before = lax.ppermute(last, axis, up)  19.3 us
    all_to_all x1, waiting for transfers between devices, on_device(): lax.all_to_all(y_split, 'sweep', split_axis=1, concat_axis=0, tiled=True)  9.79 us
    all_to_all x1, starting transfers between devices, on_device(): lax.all_to_all(cot_split, 'sweep', split_axis=1, concat_axis=0, tiled=True)  8.12 us
  transfers between devices with their start and end apart: 8, of which 5 were waited for; matrix products, arithmetic and copies ran while one was open for 4% of the time, Pallas kernels for 0%

commit v1 on v0

v1 whole, which is shorter than its diff:
```python
import functools
import math

import jax
import jax.numpy as jnp
from jax import lax
from jax.experimental import pallas as pl
from jax.experimental.pallas import tpu as pltpu
from jax.sharding import PartitionSpec as P

DH = 64
EPS = 1e-06
F32 = jnp.float32
BF16 = jnp.bfloat16
MASKED = -1e30

SL, H, WL, C = 2, 8, 32, 512
GROUPS = 16
PX = 16
HD = 256
LANES = 128
PARTS = C // LANES


def params(mib):
    return pltpu.CompilerParams(vmem_limit_bytes=mib * 1024 * 1024)


def call(kernel, outs, mib, flops=0, moved=0, scratch=(), smem=0):
    vmem = pl.BlockSpec(memory_space=pltpu.VMEM)

    def run(*args):
        specs = [pl.BlockSpec(memory_space=pltpu.SMEM)] * smem + [vmem] * (len(args) - smem)
        return pl.pallas_call(
            kernel,
            out_shape=outs,
            in_specs=specs,
            out_specs=jax.tree.map(lambda _: vmem, outs),
            scratch_shapes=list(scratch),
            compiler_params=params(mib),
            cost_estimate=pl.CostEstimate(
                flops=flops, bytes_accessed=moved, transcendentals=0
            ),
        )(*args)

    return run


def struct(shape, dtype):
    return jax.ShapeDtypeStruct(shape, dtype)


def silu(value):
    return value / (1.0 + jnp.exp(-value))


def nt(left, right):
    return lax.dot_general(left, right, (((1,), (1,)), ((), ())), preferred_element_type=F32)


def tn(left, right):
    return lax.dot_general(left, right, (((0,), (0,)), ((), ())), preferred_element_type=F32)


def nn(left, right):
    return lax.dot_general(left, right, (((1,), (0,)), ((), ())), preferred_element_type=F32)


def lanes_of(part):
    return pl.ds(pl.multiple_of(part * LANES, LANES), LANES)


def row_index(rows):
    return lax.broadcasted_iota(jnp.int32, (rows, LANES), 0)


def row_shifts(value):
    at = lax.broadcasted_iota(jnp.int32, value.shape, 0)
    below = jnp.where(at == 0, 0.0, pltpu.roll(value, 1, 0))
    above = jnp.where(at == H - 1, 0.0, pltpu.roll(value, H - 1, 0))
    return below, value, above


def forward_kernel(lat, cot, left, right, taps, bias, out, edge_l, edge_r):
    for s in range(SL):
        shifted = row_shifts(silu(left[0, s].astype(F32)))
        edge_l[s] = sum(taps[3 * a : 3 * a + 1, :] * shifted[a] for a in range(3))
        shifted = row_shifts(silu(right[0, s].astype(F32)))
        edge_r[s] = sum(taps[3 * a + 2 : 3 * a + 3, :] * shifted[a] for a in range(3))
    rows = row_index(WL)

    @pl.loop(0, SL * PARTS)
    def _(step):
        s = step // PARTS
        here = lanes_of(step % PARTS)
        tap = [taps[t : t + 1, here] for t in range(9)]
        base = bias[:, here]
        values = [lat[s, h, :, here].astype(F32) for h in range(H)]
        acts = [silu(v) for v in values]
        for h in range(H):
            cols = []
            for b in range(3):
                terms = [
                    tap[3 * a + b] * acts[h + a - 1] for a in range(3) if 0 <= h + a - 1 < H
                ]
                cols.append(functools.reduce(jnp.add, terms))
            from_left = jnp.where(
                rows == 0, edge_l[s, h : h + 1, here], pltpu.roll(cols[0], 1, 0)
            )
            from_right = jnp.where(
                rows == WL - 1, edge_r[s, h : h + 1, here], pltpu.roll(cols[2], WL - 1, 0)
            )
            y = (values[h] + (cols[1] + from_left + from_right) + base).astype(BF16)
            out[2 * h, 0, s, :, here] = y[:PX]
            out[2 * h + 1, 0, s, :, here] = y[PX:]
            moved = cot[s, h, :, here]
            out[2 * h, 1, s, :, here] = moved[:PX]
            out[2 * h + 1, 1, s, :, here] = moved[PX:]


def pair_up(first, second):
    low = lax.broadcasted_iota(jnp.int32, first.shape, 1) < 4
    return (
        jnp.where(low, first, pltpu.roll(second, 4, 1)),
        jnp.where(low, pltpu.roll(first, 4, 1), second),
    )


def attend_kernel(
    recv, w_query, w_key, w_value, w_output, gain,
    out, normed, stacked, attended, cot, gain_sum,
    y_rows, inv_rows, qkv, gatt, gnorm,
):
    rows_each = GROUPS * 8
    scale = 1.0 / math.sqrt(DH)
    for tile in range(2):
        y_two = [
            recv[:, 0, s].astype(F32)[:, 8 * tile : 8 * tile + 8, :] for s in range(SL)
        ]
        cot_two = [
            recv[:, 1, s].astype(F32)[:, 8 * tile : 8 * tile + 8, :] for s in range(SL)
        ]
        for half, (y, c) in enumerate(zip(pair_up(*y_two), pair_up(*cot_two))):
            at = pl.ds((2 * tile + half) * rows_each, rows_each)
            y = y.reshape(rows_each, C)
            inverse = lax.rsqrt(jnp.sum(y * y, axis=-1, keepdims=True) * (1.0 / C) + EPS)
            y_rows[at, :] = y
            inv_rows[at, :] = jnp.broadcast_to(inverse, (rows_each, LANES))
            normed[at, :] = (y * inverse * gain[...]).astype(BF16)
            cot[at, :] = c.reshape(rows_each, C).astype(BF16)
    for index, weight in enumerate((w_query, w_key, w_value)):
        qkv[:, index * HD : (index + 1) * HD] = nn(normed[...], weight[...]).astype(BF16)
    gatt[...] = nn(cot[...], w_output[...]).astype(BF16)

    square = (rows_each, rows_each)
    same = (lax.broadcasted_iota(jnp.int32, square, 0) % 4) == (
        lax.broadcasted_iota(jnp.int32, square, 1) % 4
    )
    lane = lax.broadcasted_iota(jnp.int32, (rows_each, LANES), 1)

    def split(value):
        zero = jnp.zeros_like(value)
        return jnp.concatenate(
            [jnp.where(lane < DH, value, zero), jnp.where(lane >= DH, value, zero)], axis=0
        )

    for group in range(4):
        at = pl.ds(group * rows_each, rows_each)
        for pair in range(2):
            def part(index):
                return qkv[at, pl.ds(index * HD + pair * LANES, LANES)]

            lanes = pl.ds(pair * LANES, LANES)
            query, key, value = part(0), part(1), part(2)
            grad_att = gatt[at, lanes]
            key2, value2 = split(key), split(value)
            scores = nt(query, key2)
            grad_probs = nt(grad_att, value2)
            lows, grads = [], []
            for head in range(2):
                cut = slice(head * rows_each, (head + 1) * rows_each)
                score = jnp.where(same, scores[:, cut] * scale, MASKED)
                expon = jnp.exp(score - jnp.max(score, axis=-1, keepdims=True))
                probs = expon * (1.0 / jnp.sum(expon, axis=-1, keepdims=True))
                gp = grad_probs[:, cut]
                weighted = probs * gp
                total = jnp.sum(weighted, axis=-1, keepdims=True)
                lows.append(probs.astype(BF16))
                grads.append(((weighted - probs * total) * scale).astype(BF16))
            attended[at, lanes] = nn(jnp.concatenate(lows, axis=1), value2).astype(BF16)
            grad_q = nn(jnp.concatenate(grads, axis=1), key2)
            grad_k = tn(jnp.concatenate(grads, axis=0), split(query))
            grad_v = tn(jnp.concatenate(lows, axis=0), split(grad_att))
            for index, grad in enumerate((grad_q, grad_k, grad_v)):
                stacked[at, pl.ds(index * HD + pair * LANES, LANES)] = grad.astype(BF16)

    gnorm[...] = (
        nt(stacked[:, :HD], w_query[...])
        + nt(stacked[:, HD : 2 * HD], w_key[...])
        + nt(stacked[:, 2 * HD :], w_value[...])
    )
    total = jnp.zeros((8, C), F32)
    for tile in range(2):
        halves = []
        for half in range(2):
            at = pl.ds((2 * tile + half) * rows_each, rows_each)
            y = y_rows[at, :]
            inverse = inv_rows[at, :][:, :1]
            grad = gnorm[at, :]
            total = total + jnp.sum((grad * y * inverse).reshape(GROUPS, 8, C), axis=0)
            gained = grad * gain[...]
            mean = jnp.sum(gained * y, axis=-1, keepdims=True) * (1.0 / C)
            result = inverse * (gained - y * (mean * inverse * inverse))
            halves.append(result.reshape(GROUPS, 8, C))
        for s, whole in enumerate(pair_up(*halves)):
            out[:, s, 8 * tile : 8 * tile + 8, :] = whole.astype(BF16)
    gain_sum[...] = jnp.sum(total, axis=0, keepdims=True)


def weights_kernel(predivide, core, normed, stacked, attended, cot, out):
    mine = core[0]
    for m in range(4):
        if m < 3:
            whole = tn(normed[...], stacked[:, m * HD : (m + 1) * HD])
        else:
            whole = tn(cot[...], attended[...])
        tiles = (whole * predivide).reshape(16, 2, 2, 8, HD)
        for which in range(2):
            slot = (mine + which) % 2
            for high in range(2):
                for side in range(2):
                    piece = tiles[:, which, high, :, side * LANES : (side + 1) * LANES]
                    out[slot, 4 * m + 2 * high + side] = piece.reshape(LANES, LANES).astype(BF16)


def taps_kernel(predivide, lat, left, right, cot, ret, gain_sum, kept, got, out, edge_l, edge_r, tiles):
    tiles[...] = jnp.zeros_like(tiles)
    for s in range(SL):
        edge_l[s] = silu(left[0, s].astype(F32))
        edge_r[s] = silu(right[0, s].astype(F32))
    rows = row_index(WL)

    @pl.loop(0, PARTS)
    def _(part):
        here = lanes_of(part)
        sums = [jnp.zeros((8, LANES), F32) for _ in range(10)]
        for s in range(SL):
            grads, cols = [], []
            for h in range(H):
                back = jnp.concatenate(
                    [ret[2 * h, s, :, here].astype(F32), ret[2 * h + 1, s, :, here].astype(F32)],
                    axis=0,
                )
                grads.append(cot[s, h, :, here].astype(F32) + back)
                act = silu(lat[s, h, :, here].astype(F32))
                cols.append(
                    (
                        jnp.where(rows == 0, edge_l[s, h : h + 1, here], pltpu.roll(act, 1, 0)),
                        act,
                        jnp.where(
                            rows == WL - 1, edge_r[s, h : h + 1, here], pltpu.roll(act, WL - 1, 0)
                        ),
                    )
                )
            for h in range(H):
                for a in range(3):
                    if 0 <= h + a - 1 < H:
                        for b in range(3):
                            term = (grads[h] * cols[h + a - 1][b]).reshape(4, 8, LANES)
                            sums[3 * a + b] = sums[3 * a + b] + jnp.sum(term, axis=0)
                sums[9] = sums[9] + jnp.sum(grads[h].reshape(4, 8, LANES), axis=0)
        for r in range(10):
            tiles[4 * part + r // 3, pl.ds(r % 3, 1), :] = jnp.sum(sums[r], axis=0, keepdims=True)
        tiles[4 * part + 3, pl.ds(1, 1), :] = gain_sum[:, here]

    whole = tiles[...] * predivide
    high = whole.astype(BF16).astype(F32)
    out[:, LANES:, :] = jnp.concatenate([high, whole - high], axis=1).astype(BF16)
    out[:, :LANES, :] = (kept[0].astype(F32) + got[...].astype(F32)).astype(BF16)


def latents_kernel(lat, cot, ret, left, right, back_l, back_r, taps, out, edge_l, edge_r):
    for s in range(SL):
        below, here, above = row_shifts(left[1, s].astype(F32) + back_l[s].astype(F32))
        edge_l[s] = taps[2:3, :] * above + taps[5:6, :] * here + taps[8:9, :] * below
        below, here, above = row_shifts(right[1, s].astype(F32) + back_r[s].astype(F32))
        edge_r[s] = taps[0:1, :] * above + taps[3:4, :] * here + taps[6:7, :] * below
    rows = row_index(WL)

    @pl.loop(0, SL * PARTS)
    def _(step):
        s = step // PARTS
        here = lanes_of(step % PARTS)
        tap = [taps[t : t + 1, here] for t in range(9)]
        grads = []
        for h in range(H):
            back = jnp.concatenate(
                [ret[2 * h, s, :, here].astype(F32), ret[2 * h + 1, s, :, here].astype(F32)],
                axis=0,
            )
            grads.append(cot[s, h, :, here].astype(F32) + back)
        for h in range(H):
            cols = []
            for b in range(3):
                terms = [
                    tap[3 * a + b] * grads[h - a + 1] for a in range(3) if 0 <= h - a + 1 < H
                ]
                cols.append(functools.reduce(jnp.add, terms))
            from_left = jnp.where(
                rows == 0, edge_l[s, h : h + 1, here], pltpu.roll(cols[2], 1, 0)
            )
            from_right = jnp.where(
                rows == WL - 1, edge_r[s, h : h + 1, here], pltpu.roll(cols[0], WL - 1, 0)
            )
            total = cols[1] + from_left + from_right
            value = lat[s, h, :, here].astype(F32)
            sig = 1.0 / (1.0 + jnp.exp(-value))
            out[s, h, :, here] = grads[h] + total * (sig * (1.0 + value * (1.0 - sig)))


def second_kernel(core, recv, out):
    total = jnp.sum(recv[...].astype(F32), axis=0)
    weights = total[:LANES].reshape(16, 8, LANES)
    taps = total[LANES : LANES + 8] + total[LANES + 8 :]
    high = taps.astype(BF16).astype(F32)
    low = taps - high
    at = lax.broadcasted_iota(jnp.int32, (8, LANES), 0)
    both = jnp.where(at < 4, high, pltpu.roll(low, 4, 0))
    for which in range(2):
        own = jnp.where(core[0] == which, 1.0, 0.0)
        for z in range(16):
            out[2 * z + which] = jnp.concatenate([weights[z] * own, both], axis=0).astype(BF16)


def third_kernel(recv, out):
    total = jnp.sum(recv[...].astype(F32), axis=0)
    both = total[8:]
    taps = both + pltpu.roll(both, 4, 0)
    result = jnp.concatenate([total[:8], taps], axis=0)
    for s in range(GROUPS):
        out[s] = result


def unpack_kernel(recv, kernel_out, bias_out, gain_out, *outs):
    for part in range(PARTS):
        here = slice(part * LANES, (part + 1) * LANES)
        for r in range(11):
            row = recv[4 * part + r // 3, 8 + r % 3 : 9 + r % 3, :]
            if r < 9:
                kernel_out[r : r + 1, here] = row
            elif r == 9:
                bias_out[:, here] = row
            else:
                gain_out[:, here] = row
    for m in range(4):
        for high in range(2):
            for side in range(2):
                outs[m][8 * high : 8 * high + 8, side * LANES : (side + 1) * LANES] = recv[
                    4 * m + 2 * high + side, :8, :
                ]


def on_device(
    latents, cotangent, conv_kernel, conv_bias, norm_gain, w_query, w_key, w_value, w_output
):
    strips = lax.axis_size("azim")
    groups = lax.axis_size("sweep")
    up = [(i, (i + 1) % strips) for i in range(strips)]
    down = [(j, i) for i, j in up]
    pair = [(i, i ^ 1) for i in range(strips)]
    core = (lax.axis_index("azim") % 2).astype(jnp.int32).reshape(1)
    predivide = 1.0 / math.sqrt(SL * groups * H * WL * strips)
    bias_row = conv_bias.reshape(1, C)
    gain_row = norm_gain.reshape(1, C)
    edge = pltpu.VMEM((SL, H, C), F32)

    last = jnp.stack([latents[:, :, WL - 1, :], cotangent[:, :, WL - 1, :]])
    first = jnp.stack([latents[:, :, 0, :], cotangent[:, :, 0, :]])
    left = lax.ppermute(last, "azim", up)
    right = lax.ppermute(first, "azim", down)

    sent = call(
        forward_kernel,
        struct((GROUPS, 2, SL, PX, C), BF16),
        16,
        flops=10_000_000,
        moved=2_000_000,
        scratch=[edge, edge],
    )(latents, cotangent, left, right, conv_kernel, bias_row)
    recv = lax.all_to_all(sent, "sweep", split_axis=0, concat_axis=0, tiled=True)

    rows = GROUPS * SL * PX
    grad_attn, normed, stacked, attended, cot_rows, gain_sum = call(
        attend_kernel,
        (
            struct((GROUPS, SL, PX, C), BF16),
            struct((rows, C), BF16),
            struct((rows, 3 * HD), BF16),
            struct((rows, HD), BF16),
            struct((rows, C), BF16),
            struct((1, C), F32),
        ),
        32,
        flops=2_000_000_000,
        moved=6_000_000,
        scratch=[
            pltpu.VMEM((rows, C), F32),
            pltpu.VMEM((rows, LANES), F32),
            pltpu.VMEM((rows, 3 * HD), BF16),
            pltpu.VMEM((rows, HD), BF16),
            pltpu.VMEM((rows, C), F32),
        ],
    )(recv, w_query, w_key, w_value, w_output, gain_row)
    ret = lax.all_to_all(grad_attn, "sweep", split_axis=0, concat_axis=0, tiled=True)

    halves = call(
        functools.partial(weights_kernel, predivide),
        struct((2, GROUPS, LANES, LANES), BF16),
        24,
        flops=600_000_000,
        moved=4_000_000,
        smem=1,
    )(core, normed, stacked, attended, cot_rows)
    got = lax.ppermute(halves[1], "azim", pair)

    back_last = ret[1::2, :, PX - 1, :].transpose(1, 0, 2)
    back_first = ret[0::2, :, 0, :].transpose(1, 0, 2)
    back_l = lax.ppermute(back_last, "azim", up)
    back_r = lax.ppermute(back_first, "azim", down)

    first_sent = call(
        functools.partial(taps_kernel, predivide),
        struct((GROUPS, LANES + 16, LANES), BF16),
        16,
        flops=10_000_000,
        moved=3_000_000,
        scratch=[edge, edge, pltpu.VMEM((GROUPS, 8, LANES), F32)],
    )(latents, left, right, cotangent, ret, gain_sum, halves, got)
    first_recv = lax.all_to_all(first_sent, "sweep", split_axis=0, concat_axis=0, tiled=True)

    grad_latents = call(
        latents_kernel,
        struct((SL, H, WL, C), F32),
        16,
        flops=10_000_000,
        moved=4_000_000,
        scratch=[edge, edge],
    )(latents, cotangent, ret, left, right, back_l, back_r, conv_kernel)

    second_sent = call(
        second_kernel, struct((strips, 16, LANES), BF16), 16, moved=1_000_000, smem=1
    )(core, first_recv)
    second_recv = lax.all_to_all(second_sent, "azim", split_axis=0, concat_axis=0, tiled=True)
    third_sent = call(third_kernel, struct((GROUPS, 16, LANES), F32), 16, moved=300_000)(
        second_recv
    )
    third_recv = lax.all_to_all(third_sent, "sweep", split_axis=0, concat_axis=0, tiled=True)
    share = struct((C // strips, HD), F32)
    line = struct((1, C), F32)
    grad_kernel, grad_bias, grad_gain, *shares = call(
        unpack_kernel,
        (struct((9, C), F32), line, line, share, share, share, share),
        16,
        moved=300_000,
    )(third_recv)
    return (
        grad_latents,
        grad_kernel,
        grad_bias.reshape(C),
        grad_gain.reshape(C),
        shares[0],
        shares[1],
        shares[2],
        shares[3],
    )


def solution(mesh):
    image = P("sweep", None, "azim", None)
    share = P("azim", None)
    return jax.shard_map(
        on_device,
        mesh=mesh,
        in_specs=(image, image, P(), P(), P(), P(), P(), P(), P()),
        out_specs=(image, P(), P(), P(), share, share, share, share),
        check_vma=False,
    )
```

time: 402 us -> 148 us (0.37)
  the two profiles are of different devices: /device:TPU:1 before, /device:TPU:2 now
where the time goes in v1:
time: 148 us; the launch traced here: 147 us
  blocking collectives  66.6 us (45%)
  starting transfers between devices  42.8 us (29%)
  waiting for transfers between devices  15.9 us (11%)
  Pallas kernels  13.8 us (9%)
  local copies, waits for them, and re-layouts  6.84 us (5%)
    all_to_all x1, blocking collectives, on_device(): lax.all_to_all(second_sent, 'azim', split_axis=0, concat_axis=0, tiled=True)  23.4 us
    all_to_all x1, blocking collectives, on_device(): lax.all_to_all(sent, 'sweep', split_axis=0, concat_axis=0, tiled=True)  22.1 us
    all_to_all x1, blocking collectives, on_device(): lax.all_to_all(first_sent, 'sweep', split_axis=0, concat_axis=0, tiled=True)  21.1 us
    ppermute x1, starting transfers between devices, on_device(): right = lax.ppermute(first, 'azim', down)  15.6 us
    pallas_call x8, Pallas kernels, run(): pl.pallas_call(kernel, out_shape=outs, in_specs=specs, out_specs=jax.tree...  13.8 us
    ppermute x1, starting transfers between devices, on_device(): back_r = lax.ppermute(back_first, 'azim', down)  9.66 us
    ppermute x1, waiting for transfers between devices, on_device(): left = lax.ppermute(last, 'azim', up)  9.56 us
    all_to_all x1, starting transfers between devices, on_device(): lax.all_to_all(grad_attn, 'sweep', split_axis=0, concat_axis=0, tiled=True)  6.07 us
  transfers between devices with their start and end apart: 7, of which 4 were waited for; matrix products, arithmetic and copies ran while one was open for 0% of the time, Pallas kernels for 2%

profile of v1, /device:TPU:2, one launch (start us, length us, event | category | flops | bytes accessed | tf_op | source)
XLA Modules:
  0.0 146.8 jit_solution(12911715325631441326)
XLA Ops:
  0.6 1.1 fusion.1
  1.7 1.0 fusion.2
  2.8 15.6 %collective-permute-start.1 = (bf16[2,2,8,512]{3,2,1,0:T(8,128)(2,1)S(1)}, bf16[2,2,8,512]{3,2,1,0:T(8,128)(2,1)S(1)}, u32[]{:S(2)}, u32[]{:S(2)}) collective-permute-start(bf16[2,2,8,512]{3,2,1,0:T(8,128)(2,1)S(1)} %pad_maximum_fusion.1), channel_id=1, source_target_pairs={{1,0},{2,1},{3,2},{4,3},{5,4},{6,5},{7,6},{8,7},{9,8},{10,9},{11,1... | collective-permute-start | bytes 98312 | tf_op jit(solution)/shard_map/ppermute | solution.py:380
  18.5 0.0 copy-start.8
  18.5 1.9 %collective-permute-start = (bf16[2,2,8,512]{3,2,1,0:T(8,128)(2,1)S(1)}, bf16[2,2,8,512]{3,2,1,0:T(8,128)(2,1)S(1)}, u32[]{:S(2)}, u32[]{:S(2)}) collective-permute-start(bf16[2,2,8,512]{3,2,1,0:T(8,128)(2,1)S(1)} %pad_maximum_fusion), channel_id=1, source_target_pairs={{0,1},{1,2},{2,3},{3,4},{4,5},{5,6},{6,7},{7,8},{8,9},{9,10},{10,1... | collective-permute-start | bytes 98312 | tf_op jit(solution)/shard_map/ppermute | solution.py:379
  20.4 9.6 %collective-permute-done.left = bf16[2,2,8,512]{3,2,1,0:T(8,128)(2,1)S(1)} collective-permute-done((bf16[2,2,8,512]{3,2,1,0:T(8,128)(2,1)S(1)}, bf16[2,2,8,512]{3,2,1,0:T(8,128)(2,1)S(1)}, u32[]{:S(2)}, u32[]{:S(2)}) %collective-permute-start) | collective-permute-done | bytes 32800 | tf_op jit(solution)/shard_map/ppermute | solution.py:379
  30.0 0.0 copy-start.1
  30.0 1.0 copy-done.1
  31.1 1.2 shard_map.152
  32.3 22.1 %all_to_all.25.recv = bf16[16,2,2,16,512]{4,3,2,1,0:T(8,128)(2,1)S(1)} all-to-all(bf16[16,2,2,16,512]{4,3,2,1,0:T(8,128)(2,1)S(1)} %shard_map.152), channel_id=1, replica_groups=mesh['sweep'=16,'azim'=32] {'sweep'}, dimensions={0} | all-to-all | bytes 2097152 | tf_op jit(solution)/shard_map/all_to_all | solution.py:390
  54.4 6.6 %shard_map.153 = (bf16[16,2,16,512]{3,2,1,0:T(8,128)(2,1)}, bf16[512,512]{1,0:T(8,128)(2,1)S(1)}, bf16[512,768]{1,0:T(8,128)(2,1)S(1)}, bf16[512,256]{1,0:T(8,12...) custom-call(bf16[16,2,2,16,512]{4,3,2,1,0:T(8,128)(2,1)S(1)} %all_to_all.25.recv, ...), custom_call_target="tpu_custom_call" | custom-call | flops 2000000000 | bytes 6000000 | tf_op jit(solution)/shard_map/pallas_call | solution.py:34
  61.0 0.8 copy-done.3
  61.8 0.7 copy-done.5
  62.5 6.1 %all-to-all-start.1 = ((bf16[16,2,16,512]{3,2,1,0:T(8,128)(2,1)}), bf16[16,2,16,512]{3,2,1,0:T(8,128)(2,1)S(1)}, u32[]{:S(2)}, u32[]{:S(2)}) async-start(bf16[16,2,16,512]{3,2,1,0:T(8,128)(2,1)} %get-tuple-element.21), calls=%async_computation.1 | async-start | bytes 1048576 | tf_op jit(solution)/shard_map/all_to_all | solution.py:414
  68.6 1.0 copy-done.4
  69.6 0.9 copy-done.6
  70.6 0.8 shard_map.155.kept
  71.4 2.1 %collective-permute-start.4 = (bf16[16,128,128]{2,1,0:T(8,128)(2,1)S(1)}, bf16[16,128,128]{2,1,0:T(8,128)(2,1)S(1)}, u32[]{:S(2)}, u32[]{:S(2)}) collective-permute-start(bf16[16,128,128]{2,1,0:T(8,128)(2,1)S(1)} %slice_bitcast_fusion), channel_id=1, source_target_pairs={{0,1},{1,0},{2,3},{3,2},{4,5},{5,4},{6,7},{7,6},{8,9},{9,8},{10,11... | collective-permute-start | bytes 1572872 | tf_op jit(solution)/shard_map/ppermute | solution.py:424
  73.5 1.9 %collective-permute-done.4.got = bf16[16,128,128]{2,1,0:T(8,128)(2,1)S(1)} collective-permute-done((bf16[16,128,128]{2,1,0:T(8,128)(2,1)S(1)}, bf16[16,128,128]{2,1,0:T(8,128)(2,1)S(1)}, u32[]{:S(2)}, u32[]{:S(2)}) %collective-permute-start.4) | collective-permute-done | bytes 524320 | tf_op jit(solution)/shard_map/ppermute | solution.py:424
  75.4 3.0 %all-to-all-done.1.ret = bf16[16,2,16,512]{3,2,1,0:T(8,128)(2,1)S(1)} async-done(((bf16[16,2,16,512]{3,2,1,0:T(8,128)(2,1)}), bf16[16,2,16,512]{3,2,1,0:T(8,128)(2,1)S(1)}, u32[]{:S(2)}, u32[]{:S(2)}) %all-to-all-start.1) | async-done | bytes 524320 | tf_op jit(solution)/shard_map/all_to_all | solution.py:414
  78.4 1.4 shard_map.156
  79.8 21.1 %all_to_all.26.recv = bf16[16,144,128]{2,1,0:T(8,128)(2,1)S(1)} all-to-all(bf16[16,144,128]{2,1,0:T(8,128)(2,1)S(1)} %shard_map.156), channel_id=1, replica_groups=mesh['sweep'=16,'azim'=32] {'sweep'}, dimensions={0} | all-to-all | bytes 1179648 | tf_op jit(solution)/shard_map/all_to_all | solution.py:439
  101.0 0.1 shard_map.157
  101.1 23.4 %all_to_all.27.recv = bf16[32,16,128]{2,1,0:T(8,128)(2,1)S(1)} all-to-all(bf16[32,16,128]{2,1,0:T(8,128)(2,1)S(1)} %shard_map.157), channel_id=1, replica_groups=mesh['sweep'=16,'azim'=32] {'azim'}, dimensions={0} | all-to-all | bytes 262144 | tf_op jit(solution)/shard_map/all_to_all | solution.py:453
  124.5 0.7 shard_map.158
  125.2 5.5 %all-to-all-start.4 = ((f32[16,16,128]{2,1,0:T(8,128)}), f32[16,16,128]{2,1,0:T(8,128)S(1)}, u32[]{:S(2)}, u32[]{:S(2)}) async-start(f32[16,16,128]{2,1,0:T(8,128)} %shard_map.158), calls=%async_computation.4 | async-start | bytes 262144 | tf_op jit(solution)/shard_map/all_to_all | solution.py:457
  130.7 0.1 fusion
  130.8 1.9 %collective-permute-start.2 = (bf16[2,8,512]{2,1,0:T(8,128)(2,1)S(1)}, bf16[2,8,512]{2,1,0:T(8,128)(2,1)S(1)}, u32[]{:S(2)}, u32[]{:S(2)}) collective-permute-start(bf16[2,8,512]{2,1,0:T(8,128)(2,1)S(1)} %bitcast.27), channel_id=1, source_target_pairs={{0,1},{1,2},{2,3},{3,4},{4,5},{5,6},{6,7},{7,8},{8,9},{9,10},{10,1... | collective-permute-start | bytes 49160 | tf_op jit(solution)/shard_map/ppermute | solution.py:428
  132.7 9.7 %collective-permute-start.3 = (bf16[2,8,512]{2,1,0:T(8,128)(2,1)S(1)}, bf16[2,8,512]{2,1,0:T(8,128)(2,1)S(1)}, u32[]{:S(2)}, u32[]{:S(2)}) collective-permute-start(bf16[2,8,512]{2,1,0:T(8,128)(2,1)S(1)} %bitcast.28), channel_id=1, source_target_pairs={{1,0},{2,1},{3,2},{4,3},{5,4},{6,5},{7,6},{8,7},{9,8},{10,9},{11,1... | collective-permute-start | bytes 49160 | tf_op jit(solution)/shard_map/ppermute | solution.py:429
  142.4 1.4 collective-permute-done.3.back_r
  143.8 2.3 %shard_map.154 = f32[2,8,32,512]{3,2,1,0:T(8,128)} custom-call(bf16[2,8,32,512]{3,2,1,0:T(8,128)(2,1)S(1)} %copy-done, bf16[2,8,32,512]{3,2,1,0:T(8,128)(2,1)S(1)} %copy-done.2, bf16[16,2,16,512]{3,2,1,0:T(8,128)(2,1)S(1)} %all-to-all-done.1.ret, bf16[2,2,8,512]{3,2,1,0:T(8,128)(2,1)S(1)} %collective-permute-done.left, ...), custom_call_target="tpu_custom_call" | custom-call | flops 10000000 | bytes 4000000 | tf_op jit(solution)/shard_map/pallas_call | solution.py:34
  146.1 0.7 shard_map.159
  (31 shorter events, 0.2 us)
Async XLA Ops:
  0.6 29.4 %copy-start = (bf16[2,8,32,512]{3,2,1,0:T(8,128)(2,1)S(1)}, bf16[2,8,32,512]{3,2,1,0:T(8,128)(2,1)}, u32[]{:S(2)}) copy-start(bf16[2,8,32,512]{3,2,1,0:T(8,128)(2,1)} %lat.5) | copy-start | bytes 1572868
  2.8 17.6 %collective-permute-start.1 = (bf16[2,2,8,512]{3,2,1,0:T(8,128)(2,1)S(1)}, bf16[2,2,8,512]{3,2,1,0:T(8,128)(2,1)S(1)}, u32[]{:S(2)}, u32[]{:S(2)}) collective-permute-start(bf16[2,2,8,512]{3,2,1,0:T(8,128)(2,1)S(1)} %pad_maximum_fusion.1), channel_id=1, source_target_pairs={{1,0},{2,1},{3,2},{4,3},{5,4},{6,5},{7,6},{8,7},{9,8},{10,9},{11,1... | collective-permute-start | bytes 98312 | tf_op jit(solution)/shard_map/ppermute | solution.py:380
  18.5 11.5 %copy-start.7 = (f32[9,512]{1,0:T(8,128)S(1)}, f32[9,512]{1,0:T(8,128)}, u32[]{:S(2)}) copy-start(f32[9,512]{1,0:T(8,128)} %taps.3) | copy-start | bytes 55300
  18.5 11.5 %copy-start.8 = (f32[512]{0:T(512)S(1)}, f32[512]{0:T(512)}, u32[]{:S(2)}) copy-start(f32[512]{0:T(512)} %param.12) | copy-start | bytes 6148
  18.5 11.5 %collective-permute-start = (bf16[2,2,8,512]{3,2,1,0:T(8,128)(2,1)S(1)}, bf16[2,2,8,512]{3,2,1,0:T(8,128)(2,1)S(1)}, u32[]{:S(2)}, u32[]{:S(2)}) collective-permute-start(bf16[2,2,8,512]{3,2,1,0:T(8,128)(2,1)S(1)} %pad_maximum_fusion), channel_id=1, source_target_pairs={{0,1},{1,2},{2,3},{3,4},{4,5},{5,6},{6,7},{7,8},{8,9},{9,10},{10,1... | collective-permute-start | bytes 98312 | tf_op jit(solution)/shard_map/ppermute | solution.py:379
  30.0 1.0 copy-start.1
  32.3 22.1 %copy-start.9 = (bf16[512,256]{1,0:T(8,128)(2,1)S(1)}, bf16[512,256]{1,0:T(8,128)(2,1)}, u32[]{:S(2)}) copy-start(bf16[512,256]{1,0:T(8,128)(2,1)} %w_query.1) | copy-start | bytes 786436
  32.3 22.1 %copy-start.10 = (bf16[512,256]{1,0:T(8,128)(2,1)S(1)}, bf16[512,256]{1,0:T(8,128)(2,1)}, u32[]{:S(2)}) copy-start(bf16[512,256]{1,0:T(8,128)(2,1)} %w_key.1) | copy-start | bytes 786436
  32.3 22.1 %copy-start.11 = (bf16[512,256]{1,0:T(8,128)(2,1)S(1)}, bf16[512,256]{1,0:T(8,128)(2,1)}, u32[]{:S(2)}) copy-start(bf16[512,256]{1,0:T(8,128)(2,1)} %w_value.1) | copy-start | bytes 786436
  32.3 22.1 %copy-start.12 = (bf16[512,256]{1,0:T(8,128)(2,1)S(1)}, bf16[512,256]{1,0:T(8,128)(2,1)}, u32[]{:S(2)}) copy-start(bf16[512,256]{1,0:T(8,128)(2,1)} %w_output.1) | copy-start | bytes 786436
  32.3 22.1 %copy-start.13 = (f32[512]{0:T(512)S(1)}, f32[512]{0:T(512)}, u32[]{:S(2)}) copy-start(f32[512]{0:T(512)} %param.13) | copy-start | bytes 6148
  61.0 0.8 copy-start.3
  61.8 0.7 copy-start.5
  62.5 15.9 %all-to-all-start.1 = ((bf16[16,2,16,512]{3,2,1,0:T(8,128)(2,1)}), bf16[16,2,16,512]{3,2,1,0:T(8,128)(2,1)S(1)}, u32[]{:S(2)}, u32[]{:S(2)}) async-start(bf16[16,2,16,512]{3,2,1,0:T(8,128)(2,1)} %get-tuple-element.21), calls=%async_computation.1 | async-start | bytes 1048576 | tf_op jit(solution)/shard_map/all_to_all | solution.py:414
  68.6 1.0 copy-start.4
  69.6 0.9 copy-start.6
  71.4 7.0 %copy-start.2 = (bf16[2,8,32,512]{3,2,1,0:T(8,128)(2,1)S(1)}, bf16[2,8,32,512]{3,2,1,0:T(8,128)(2,1)}, u32[]{:S(2)}) copy-start(bf16[2,8,32,512]{3,2,1,0:T(8,128)(2,1)} %cot.5) | copy-start | bytes 1572868
  71.4 3.9 %collective-permute-start.4 = (bf16[16,128,128]{2,1,0:T(8,128)(2,1)S(1)}, bf16[16,128,128]{2,1,0:T(8,128)(2,1)S(1)}, u32[]{:S(2)}, u32[]{:S(2)}) collective-permute-start(bf16[16,128,128]{2,1,0:T(8,128)(2,1)S(1)} %slice_bitcast_fusion), channel_id=1, source_target_pairs={{0,1},{1,0},{2,3},{3,2},{4,5},{5,4},{6,7},{7,6},{8,9},{9,8},{10,11... | collective-permute-start | bytes 1572872 | tf_op jit(solution)/shard_map/ppermute | solution.py:424
  125.2 21.0 %all-to-all-start.4 = ((f32[16,16,128]{2,1,0:T(8,128)}), f32[16,16,128]{2,1,0:T(8,128)S(1)}, u32[]{:S(2)}, u32[]{:S(2)}) async-start(f32[16,16,128]{2,1,0:T(8,128)} %shard_map.158), calls=%async_computation.4 | async-start | bytes 262144 | tf_op jit(solution)/shard_map/all_to_all | solution.py:457
  130.8 11.6 %collective-permute-start.2 = (bf16[2,8,512]{2,1,0:T(8,128)(2,1)S(1)}, bf16[2,8,512]{2,1,0:T(8,128)(2,1)S(1)}, u32[]{:S(2)}, u32[]{:S(2)}) collective-permute-start(bf16[2,8,512]{2,1,0:T(8,128)(2,1)S(1)} %bitcast.27), channel_id=1, source_target_pairs={{0,1},{1,2},{2,3},{3,4},{4,5},{5,6},{6,7},{7,8},{8,9},{9,10},{10,1... | collective-permute-start | bytes 49160 | tf_op jit(solution)/shard_map/ppermute | solution.py:428
  132.7 11.1 %collective-permute-start.3 = (bf16[2,8,512]{2,1,0:T(8,128)(2,1)S(1)}, bf16[2,8,512]{2,1,0:T(8,128)(2,1)S(1)}, u32[]{:S(2)}, u32[]{:S(2)}) collective-permute-start(bf16[2,8,512]{2,1,0:T(8,128)(2,1)S(1)} %bitcast.28), channel_id=1, source_target_pairs={{1,0},{2,1},{3,2},{4,3},{5,4},{6,5},{7,6},{8,7},{9,8},{10,9},{11,1... | collective-permute-start | bytes 49160 | tf_op jit(solution)/shard_map/ppermute | solution.py:429

commit v2 on v1

--- a/solution.py
+++ b/solution.py
@@ -81,7 +81,21 @@
     return below, value, above
 
 
-def forward_kernel(lat, cot, left, right, taps, bias, out, edge_l, edge_r):
+def start_kernel(lat, cot, packed, first, last, edges):
+    for which, ref in enumerate((lat, cot)):
+        for s in range(SL):
+            for h in range(H):
+                edges[0, which, s, h : h + 1, :] = ref[s, h, :PX, :].astype(F32)[:1]
+                edges[1, which, s, h : h + 1, :] = ref[s, h, PX:, :].astype(F32)[PX - 1 :]
+    first[...] = edges[0].astype(BF16)
+    last[...] = edges[1].astype(BF16)
+    for s in range(SL):
+        for h in range(H):
+            packed[2 * h, s] = cot[s, h, :PX, :]
+            packed[2 * h + 1, s] = cot[s, h, PX:, :]
+
+
+def forward_kernel(lat, left, right, taps, bias, out, edge_l, edge_r):
     for s in range(SL):
         shifted = row_shifts(silu(left[0, s].astype(F32)))
         edge_l[s] = sum(taps[3 * a : 3 * a + 1, :] * shifted[a] for a in range(3))
@@ -111,11 +125,8 @@
                 rows == WL - 1, edge_r[s, h : h + 1, here], pltpu.roll(cols[2], WL - 1, 0)
             )
             y = (values[h] + (cols[1] + from_left + from_right) + base).astype(BF16)
-            out[2 * h, 0, s, :, here] = y[:PX]
-            out[2 * h + 1, 0, s, :, here] = y[PX:]
-            moved = cot[s, h, :, here]
-            out[2 * h, 1, s, :, here] = moved[:PX]
-            out[2 * h + 1, 1, s, :, here] = moved[PX:]
+            out[2 * h, s, :, here] = y[:PX]
+            out[2 * h + 1, s, :, here] = y[PX:]
 
 
 def pair_up(first, second):
@@ -127,18 +138,18 @@
 
 
 def attend_kernel(
-    recv, w_query, w_key, w_value, w_output, gain,
-    out, normed, stacked, attended, cot, gain_sum,
-    y_rows, inv_rows, qkv, gatt, gnorm,
+    predivide, core, recv, recv_cot, w_query, w_key, w_value, w_output, gain,
+    out, halves, gain_sum,
+    normed, stacked, attended, cot, y_rows, inv_rows, qkv, gatt, gnorm,
 ):
     rows_each = GROUPS * 8
     scale = 1.0 / math.sqrt(DH)
     for tile in range(2):
         y_two = [
-            recv[:, 0, s].astype(F32)[:, 8 * tile : 8 * tile + 8, :] for s in range(SL)
+            recv[:, s].astype(F32)[:, 8 * tile : 8 * tile + 8, :] for s in range(SL)
         ]
         cot_two = [
-            recv[:, 1, s].astype(F32)[:, 8 * tile : 8 * tile + 8, :] for s in range(SL)
+            recv_cot[:, s].astype(F32)[:, 8 * tile : 8 * tile + 8, :] for s in range(SL)
         ]
         for half, (y, c) in enumerate(zip(pair_up(*y_two), pair_up(*cot_two))):
             at = pl.ds((2 * tile + half) * rows_each, rows_each)
@@ -201,7 +212,7 @@
     )
     total = jnp.zeros((8, C), F32)
     for tile in range(2):
-        halves = []
+        results = []
         for half in range(2):
             at = pl.ds((2 * tile + half) * rows_each, rows_each)
             y = y_rows[at, :]
@@ -211,13 +222,11 @@
             gained = grad * gain[...]
             mean = jnp.sum(gained * y, axis=-1, keepdims=True) * (1.0 / C)
             result = inverse * (gained - y * (mean * inverse * inverse))
-            halves.append(result.reshape(GROUPS, 8, C))
-        for s, whole in enumerate(pair_up(*halves)):
+            results.append(result.reshape(GROUPS, 8, C))
+        for s, whole in enumerate(pair_up(*results)):
             out[:, s, 8 * tile : 8 * tile + 8, :] = whole.astype(BF16)
     gain_sum[...] = jnp.sum(total, axis=0, keepdims=True)
 
-
-def weights_kernel(predivide, core, normed, stacked, attended, cot, out):
     mine = core[0]
     for m in range(4):
         if m < 3:
@@ -230,10 +239,13 @@
             for high in range(2):
                 for side in range(2):
                     piece = tiles[:, which, high, :, side * LANES : (side + 1) * LANES]
-                    out[slot, 4 * m + 2 * high + side] = piece.reshape(LANES, LANES).astype(BF16)
-
-
-def taps_kernel(predivide, lat, left, right, cot, ret, gain_sum, kept, got, out, edge_l, edge_r, tiles):
+                    halves[slot, 4 * m + 2 * high + side] = piece.reshape(LANES, LANES).astype(BF16)
+
+
+def taps_kernel(
+    predivide, lat, left, right, cot, ret, gain_sum, kept, got,
+    out, first, last, edge_l, edge_r, tiles, edges,
+):
     tiles[...] = jnp.zeros_like(tiles)
     for s in range(SL):
         edge_l[s] = silu(left[0, s].astype(F32))
@@ -273,6 +285,12 @@
             tiles[4 * part + r // 3, pl.ds(r % 3, 1), :] = jnp.sum(sums[r], axis=0, keepdims=True)
         tiles[4 * part + 3, pl.ds(1, 1), :] = gain_sum[:, here]
 
+    for s in range(SL):
+        for h in range(H):
+            edges[0, s, h : h + 1, :] = ret[2 * h, s].astype(F32)[:1]
+            edges[1, s, h : h + 1, :] = ret[2 * h + 1, s].astype(F32)[PX - 1 :]
+    first[...] = edges[0].astype(BF16)
+    last[...] = edges[1].astype(BF16)
     whole = tiles[...] * predivide
     high = whole.astype(BF16).astype(F32)
     out[:, LANES:, :] = jnp.concatenate([high, whole - high], axis=1).astype(BF16)
@@ -374,69 +392,67 @@
     gain_row = norm_gain.reshape(1, C)
     edge = pltpu.VMEM((SL, H, C), F32)
 
-    last = jnp.stack([latents[:, :, WL - 1, :], cotangent[:, :, WL - 1, :]])
-    first = jnp.stack([latents[:, :, 0, :], cotangent[:, :, 0, :]])
+    both_edges = struct((2, SL, H, C), BF16)
+    cot_sent, first, last = call(
+        start_kernel,
+        (struct((GROUPS, SL, PX, C), BF16), both_edges, both_edges),
+        16,
+        moved=1_500_000,
+        scratch=[pltpu.VMEM((2, 2, SL, H, C), F32)],
+    )(latents, cotangent)
     left = lax.ppermute(last, "azim", up)
     right = lax.ppermute(first, "azim", down)
-
-    sent = call(
+    recv_cot = lax.all_to_all(cot_sent, "sweep", split_axis=0, concat_axis=0, tiled=True)
+
+    y_sent = call(
         forward_kernel,
-        struct((GROUPS, 2, SL, PX, C), BF16),
+        struct((GROUPS, SL, PX, C), BF16),
         16,
         flops=10_000_000,
-        moved=2_000_000,
+        moved=1_000_000,
         scratch=[edge, edge],
-    )(latents, cotangent, left, right, conv_kernel, bias_row)
-    recv = lax.all_to_all(sent, "sweep", split_axis=0, concat_axis=0, tiled=True)
+    )(latents, left, right, conv_kernel, bias_row)
+    recv = lax.all_to_all(y_sent, "sweep", split_axis=0, concat_axis=0, tiled=True)
 
     rows = GROUPS * SL * PX
-    grad_attn, normed, stacked, attended, cot_rows, gain_sum = call(
-        attend_kernel,
+    grad_attn, halves, gain_sum = call(
+        functools.partial(attend_kernel, predivide),
         (
             struct((GROUPS, SL, PX, C), BF16),
-            struct((rows, C), BF16),
-            struct((rows, 3 * HD), BF16),
-            struct((rows, HD), BF16),
-            struct((rows, C), BF16),
+            struct((2, GROUPS, LANES, LANES), BF16),
             struct((1, C), F32),
         ),
         32,
         flops=2_000_000_000,
         moved=6_000_000,
+        smem=1,
         scratch=[
+            pltpu.VMEM((rows, C), BF16),
+            pltpu.VMEM((rows, 3 * HD), BF16),
+            pltpu.VMEM((rows, HD), BF16),
+            pltpu.VMEM((rows, C), BF16),
             pltpu.VMEM((rows, C), F32),
             pltpu.VMEM((rows, LANES), F32),
             pltpu.VMEM((rows, 3 * HD), BF16),
             pltpu.VMEM((rows, HD), BF16),
             pltpu.VMEM((rows, C), F32),
         ],
-    )(recv, w_query, w_key, w_value, w_output, gain_row)
+    )(core, recv, recv_cot, w_query, w_key, w_value, w_output, gain_row)
     ret = lax.all_to_all(grad_attn, "sweep", split_axis=0, concat_axis=0, tiled=True)
-
-    halves = call(
-        functools.partial(weights_kernel, predivide),
-        struct((2, GROUPS, LANES, LANES), BF16),
-        24,
-        flops=600_000_000,
-        moved=4_000_000,
-        smem=1,
-    )(core, normed, stacked, attended, cot_rows)
     got = lax.ppermute(halves[1], "azim", pair)
 
-    back_last = ret[1::2, :, PX - 1, :].transpose(1, 0, 2)
-    back_first = ret[0::2, :, 0, :].transpose(1, 0, 2)
-    back_l = lax.ppermute(back_last, "azim", up)
-    back_r = lax.ppermute(back_first, "azim", down)
-
-    first_sent = call(
+    one_edge = struct((SL, H, C), BF16)
+    first_sent, back_first, back_last = call(
         functools.partial(taps_kernel, predivide),
-        struct((GROUPS, LANES + 16, LANES), BF16),
+        (struct((GROUPS, LANES + 16, LANES), BF16), one_edge, one_edge),
         16,
         flops=10_000_000,
         moved=3_000_000,
-        scratch=[edge, edge, pltpu.VMEM((GROUPS, 8, LANES), F32)],
+        scratch=[edge, edge, pltpu.VMEM((GROUPS, 8, LANES), F32), pltpu.VMEM((2, SL, H, C), F32)],
     )(latents, left, right, cotangent, ret, gain_sum, halves, got)
     first_recv = lax.all_to_all(first_sent, "sweep", split_axis=0, concat_axis=0, tiled=True)
+    back_l = lax.ppermute(back_last, "azim", up)
+    back_r = lax.ppermute(back_first, "azim", down)
 
     grad_latents = call(
         latents_kernel,
@@ -446,6 +462,7 @@
         moved=4_000_000,
         scratch=[edge, edge],
     )(latents, cotangent, ret, left, right, back_l, back_r, conv_kernel)
+    first_recv, grad_latents = lax.optimization_barrier((first_recv, grad_latents))
 
     second_sent = call(
         second_kernel, struct((strips, 16, LANES), BF16), 16, moved=1_000_000, smem=1

time: 148 us -> 141 us (0.953)
  the two profiles are of different devices: /device:TPU:2 before, /device:TPU:1 now
where the time goes in v2:
time: 141 us; the launch traced here: 140 us
  starting transfers between devices  53 us (38%)
  blocking collectives  44.8 us (32%)
  waiting for transfers between devices  22.7 us (16%)
  Pallas kernels  15.2 us (11%)
  local copies, waits for them, and re-layouts  3.1 us (2%)
    all_to_all x1, blocking collectives, on_device(): lax.all_to_all(second_sent, 'azim', split_axis=0, concat_axis=0, tiled=True)  34.5 us
    pallas_call x8, Pallas kernels, run(): pl.pallas_call(kernel, out_shape=outs, in_specs=specs, out_specs=jax.tree...  15.2 us
    ppermute x1, starting transfers between devices, on_device(): got = lax.ppermute(halves[1], 'azim', pair)  14.1 us
    all_to_all x1, waiting for transfers between devices, on_device(): lax.all_to_all(y_sent, 'sweep', split_axis=0, concat_axis=0, tiled=True)  11.1 us
    all_to_all x1, blocking collectives, on_device(): lax.all_to_all(third_sent, 'sweep', split_axis=0, concat_axis=0, tiled=True)  10.3 us
    all_to_all x1, starting transfers between devices, on_device(): lax.all_to_all(cot_sent, 'sweep', split_axis=0, concat_axis=0, tiled=True)  8.12 us
    all_to_all x1, starting transfers between devices, on_device(): lax.all_to_all(first_sent, 'sweep', split_axis=0, concat_axis=0, tiled=True)  7.17 us
    ppermute x1, starting transfers between devices, on_device(): back_l = lax.ppermute(back_last, 'azim', up)  6.35 us
  transfers between devices with their start and end apart: 9, of which 6 were waited for; matrix products, arithmetic and copies ran while one was open for 0% of the time, Pallas kernels for 3%

profile of v2, /device:TPU:1, one launch (start us, length us, event | category | flops | bytes accessed | tf_op | source)
XLA Modules:
  0.0 139.6 jit_solution(6616669923516577917)
XLA Ops:
  0.6 0.0 copy-start
  0.6 1.0 copy-done
  1.7 1.0 copy-done.2
  2.7 0.9 shard_map.152
  3.6 8.1 %all-to-all-start.1 = ((bf16[16,2,16,512]{3,2,1,0:T(8,128)(2,1)}), bf16[16,2,16,512]{3,2,1,0:T(8,128)(2,1)S(1)}, u32[]{:S(2)}, u32[]{:S(2)}) async-start(bf16[16,2,16,512]{3,2,1,0:T(8,128)(2,1)} %get-tuple-element.28), calls=%async_computation.1 | async-start | bytes 1048576 | tf_op jit(solution)/shard_map/all_to_all | solution.py:405
  11.7 0.0 copy-start.5
  11.7 4.8 %collective-permute-start = (bf16[2,2,8,512]{3,2,1,0:T(8,128)(2,1)S(1)}, bf16[2,2,8,512]{3,2,1,0:T(8,128)(2,1)S(1)}, u32[]{:S(2)}, u32[]{:S(2)}) collective-permute-start(bf16[2,2,8,512]{3,2,1,0:T(8,128)(2,1)S(1)} %get-tuple-element.26), channel_id=1, source_target_pairs={{0,1},{1,2},{2,3},{3,4},{4,5},{5,6},{6,7},{7,8},{8,9},{9,10},{10,1... | collective-permute-start | bytes 98312 | tf_op jit(solution)/shard_map/ppermute | solution.py:403
  16.6 1.9 %collective-permute-start.1 = (bf16[2,2,8,512]{3,2,1,0:T(8,128)(2,1)S(1)}, bf16[2,2,8,512]{3,2,1,0:T(8,128)(2,1)S(1)}, u32[]{:S(2)}, u32[]{:S(2)}) collective-permute-start(bf16[2,2,8,512]{3,2,1,0:T(8,128)(2,1)S(1)} %get-tuple-element.27), channel_id=1, source_target_pairs={{1,0},{2,1},{3,2},{4,3},{5,4},{6,5},{7,6},{8,7},{9,8},{10,9},{11,1... | collective-permute-start | bytes 98312 | tf_op jit(solution)/shard_map/ppermute | solution.py:404
  18.5 3.6 %collective-permute-done.1.right = bf16[2,2,8,512]{3,2,1,0:T(8,128)(2,1)S(1)} collective-permute-done((bf16[2,2,8,512]{3,2,1,0:T(8,128)(2,1)S(1)}, bf16[2,2,8,512]{3,2,1,0:T(8,128)(2,1)S(1)}, u32[]{:S(2)}, u32[]{:S(2)}) %collective-permute-start.1) | collective-permute-done | bytes 32800 | tf_op jit(solution)/shard_map/ppermute | solution.py:404
  22.1 2.0 %shard_map.153 = bf16[16,2,16,512]{3,2,1,0:T(8,128)(2,1)} custom-call(bf16[2,8,32,512]{3,2,1,0:T(8,128)(2,1)S(1)} %copy-done.1, bf16[2,2,8,512]{3,2,1,0:T(8,128)(2,1)S(1)} %collective-permute-done.left, bf16[2,2,8,512]{3,2,1,0:T(8,128)(2,1)S(1)} %collective-permute-done.1.right, f32[9,512]{1,0:T(8,128)S(1)} %copy-done.4, f32[1,512]{1,0:T(1,128)S(1)} %bitcast.7), custom_call_target="tpu_custom_call" | custom-call | flops 10000000 | bytes 1000000 | tf_op jit(solution)/shard_map/pallas_call | solution.py:34
  24.1 3.0 %all-to-all-done.1.recv_cot = bf16[16,2,16,512]{3,2,1,0:T(8,128)(2,1)S(1)} async-done(((bf16[16,2,16,512]{3,2,1,0:T(8,128)(2,1)}), bf16[16,2,16,512]{3,2,1,0:T(8,128)(2,1)S(1)}, u32[]{:S(2)}, u32[]{:S(2)}) %all-to-all-start.1) | async-done | bytes 524320 | tf_op jit(solution)/shard_map/all_to_all | solution.py:405
  27.1 4.4 %all-to-all-start = ((bf16[16,2,16,512]{3,2,1,0:T(8,128)(2,1)}), bf16[16,2,16,512]{3,2,1,0:T(8,128)(2,1)S(1)}, u32[]{:S(2)}, u32[]{:S(2)}) async-start(bf16[16,2,16,512]{3,2,1,0:T(8,128)(2,1)} %shard_map.153), calls=%async_computation | async-start | bytes 1048576 | tf_op jit(solution)/shard_map/all_to_all | solution.py:415
  31.5 0.0 copy-start.10
  31.5 11.1 %all-to-all-done.recv = bf16[16,2,16,512]{3,2,1,0:T(8,128)(2,1)S(1)} async-done(((bf16[16,2,16,512]{3,2,1,0:T(8,128)(2,1)}), bf16[16,2,16,512]{3,2,1,0:T(8,128)(2,1)S(1)}, u32[]{:S(2)}, u32[]{:S(2)}) %all-to-all-start) | async-done | bytes 524320 | tf_op jit(solution)/shard_map/all_to_all | solution.py:415
  42.7 0.0 copy-start.9
  42.7 0.9 copy-done.9
  43.6 6.8 %shard_map.154 = (bf16[16,2,16,512]{3,2,1,0:T(8,128)(2,1)}, bf16[2,16,128,128]{3,2,1,0:T(8,128)(2,1)S(1)}, f32[1,512]{1,0:T(1,128)S(1)}) custom-call(s32[1]{0:T(128)} %bitcast.core, bf16[16,2,16,512]{3,2,1,0:T(8,128)(2,1)S(1)} %all-to-all-done.recv, bf16[16,2,16,512]{3,2,1,0:T(8,128)(2,1)S(1)} %all-to-all-done.1.recv_cot, bf16[512,256]{1,0:T(8,128)(2,1)S(1)} %copy-done.6, ...), custom_call_target="tpu_custom_call" | custom-call | flops 2000000000 | bytes 6000000 | tf_op jit(solution)/shard_map/pallas_call | solution.py:34
  50.4 3.6 %all-to-all-start.2 = ((bf16[16,2,16,512]{3,2,1,0:T(8,128)(2,1)}), bf16[16,2,16,512]{3,2,1,0:T(8,128)(2,1)S(1)}, u32[]{:S(2)}, u32[]{:S(2)}) async-start(bf16[16,2,16,512]{3,2,1,0:T(8,128)(2,1)} %get-tuple-element.29), calls=%async_computation.2 | async-start | bytes 1048576 | tf_op jit(solution)/shard_map/all_to_all | solution.py:441
  54.0 0.0 copy-start.3
  54.1 14.1 %collective-permute-start.2 = (bf16[16,128,128]{2,1,0:T(8,128)(2,1)S(1)}, bf16[16,128,128]{2,1,0:T(8,128)(2,1)S(1)}, u32[]{:S(2)}, u32[]{:S(2)}) collective-permute-start(bf16[16,128,128]{2,1,0:T(8,128)(2,1)S(1)} %slice_bitcast_fusion), channel_id=1, source_target_pairs={{0,1},{1,0},{2,3},{3,2},{4,5},{5,4},{6,7},{7,6},{8,9},{9,8},{10,11... | collective-permute-start | bytes 1572872 | tf_op jit(solution)/shard_map/ppermute | solution.py:442
  68.2 1.5 %collective-permute-done.2.got = bf16[16,128,128]{2,1,0:T(8,128)(2,1)S(1)} collective-permute-done((bf16[16,128,128]{2,1,0:T(8,128)(2,1)S(1)}, bf16[16,128,128]{2,1,0:T(8,128)(2,1)S(1)}, u32[]{:S(2)}, u32[]{:S(2)}) %collective-permute-start.2) | collective-permute-done | bytes 524320 | tf_op jit(solution)/shard_map/ppermute | solution.py:442
  69.7 2.4 %shard_map.155 = (bf16[16,144,128]{2,1,0:T(8,128)(2,1)}, bf16[2,8,512]{2,1,0:T(8,128)(2,1)S(1)}, bf16[2,8,512]{2,1,0:T(8,128)(2,1)S(1)}) custom-call(bf16[2,8,32,512]{3,2,1,0:T(8,128)(2,1)S(1)} %copy-done.1, bf16[2,2,8,512]{3,2,1,0:T(8,128)(2,1)S(1)} %collective-permute-done.left, bf16[2,2,8,512]{3,2,1,0:T(8,128)(2,1)S(1)} %collective-permute-done.1.right, ...), custom_call_target="tpu_custom_call" | custom-call | flops 10000000 | bytes 3000000 | tf_op jit(solution)/shard_map/pallas_call | solution.py:34
  72.1 7.2 %all-to-all-start.3 = ((bf16[16,144,128]{2,1,0:T(8,128)(2,1)}), bf16[16,144,128]{2,1,0:T(8,128)(2,1)S(1)}, u32[]{:S(2)}, u32[]{:S(2)}) async-start(bf16[16,144,128]{2,1,0:T(8,128)(2,1)} %get-tuple-element.32), calls=%async_computation.3 | async-start | bytes 1179648 | tf_op jit(solution)/shard_map/all_to_all | solution.py:453
  79.3 6.3 %collective-permute-start.3 = (bf16[2,8,512]{2,1,0:T(8,128)(2,1)S(1)}, bf16[2,8,512]{2,1,0:T(8,128)(2,1)S(1)}, u32[]{:S(2)}, u32[]{:S(2)}) collective-permute-start(bf16[2,8,512]{2,1,0:T(8,128)(2,1)S(1)} %get-tuple-element.33), channel_id=1, source_target_pairs={{0,1},{1,2},{2,3},{3,4},{4,5},{5,6},{6,7},{7,8},{8,9},{9,10},{10,1... | collective-permute-start | bytes 49160 | tf_op jit(solution)/shard_map/ppermute | solution.py:454
  85.7 2.5 %collective-permute-start.4 = (bf16[2,8,512]{2,1,0:T(8,128)(2,1)S(1)}, bf16[2,8,512]{2,1,0:T(8,128)(2,1)S(1)}, u32[]{:S(2)}, u32[]{:S(2)}) collective-permute-start(bf16[2,8,512]{2,1,0:T(8,128)(2,1)S(1)} %get-tuple-element.34), channel_id=1, source_target_pairs={{1,0},{2,1},{3,2},{4,3},{5,4},{6,5},{7,6},{8,7},{9,8},{10,9},{11,1... | collective-permute-start | bytes 49160 | tf_op jit(solution)/shard_map/ppermute | solution.py:455
  88.2 2.8 %collective-permute-done.4.back_r = bf16[2,8,512]{2,1,0:T(8,128)(2,1)S(1)} collective-permute-done((bf16[2,8,512]{2,1,0:T(8,128)(2,1)S(1)}, bf16[2,8,512]{2,1,0:T(8,128)(2,1)S(1)}, u32[]{:S(2)}, u32[]{:S(2)}) %collective-permute-start.4) | collective-permute-done | bytes 16416 | tf_op jit(solution)/shard_map/ppermute | solution.py:455
  91.0 2.3 %shard_map.156 = f32[2,8,32,512]{3,2,1,0:T(8,128)} custom-call(bf16[2,8,32,512]{3,2,1,0:T(8,128)(2,1)S(1)} %copy-done.1, bf16[2,8,32,512]{3,2,1,0:T(8,128)(2,1)S(1)} %copy-done.3, bf16[16,2,16,512]{3,2,1,0:T(8,128)(2,1)S(1)} %all-to-all-done.2.ret, bf16[2,2,8,512]{3,2,1,0:T(8,128)(2,1)S(1)} %collective-permute-done.left, ...), custom_call_target="tpu_custom_call" | custom-call | flops 10000000 | bytes 4000000 | tf_op jit(solution)/shard_map/pallas_call | solution.py:34
  93.4 0.6 all-to-all-done.3.recv
  94.0 0.1 shard_map.157
  94.1 34.5 %all_to_all.30.recv = bf16[32,16,128]{2,1,0:T(8,128)(2,1)S(1)} all-to-all(bf16[32,16,128]{2,1,0:T(8,128)(2,1)S(1)} %shard_map.157), channel_id=1, replica_groups=mesh['sweep'=16,'azim'=32] {'azim'}, dimensions={0} | all-to-all | bytes 262144 | tf_op jit(solution)/shard_map/all_to_all | solution.py:470
  128.7 10.3 %all_to_all.31.recv = f32[16,16,128]{2,1,0:T(8,128)S(1)} all-to-all(f32[16,16,128]{2,1,0:T(8,128)S(1)} %shard_map.158), channel_id=1, replica_groups=mesh['sweep'=16,'azim'=32] {'sweep'}, dimensions={0} | all-to-all | bytes 262144 | tf_op jit(solution)/shard_map/all_to_all | solution.py:474
  138.9 0.7 shard_map.159
  (19 shorter events, 0.1 us)
Async XLA Ops:
  0.6 1.0 copy-start
  1.7 1.0 copy-start.2
  3.6 18.5 %copy-start.1 = (bf16[2,8,32,512]{3,2,1,0:T(8,128)(2,1)S(1)}, bf16[2,8,32,512]{3,2,1,0:T(8,128)(2,1)}, u32[]{:S(2)}) copy-start(bf16[2,8,32,512]{3,2,1,0:T(8,128)(2,1)} %lat.7) | copy-start | bytes 1572868
  3.6 18.5 %copy-start.4 = (f32[9,512]{1,0:T(8,128)S(1)}, f32[9,512]{1,0:T(8,128)}, u32[]{:S(2)}) copy-start(f32[9,512]{1,0:T(8,128)} %taps.3) | copy-start | bytes 55300
  3.6 23.5 %all-to-all-start.1 = ((bf16[16,2,16,512]{3,2,1,0:T(8,128)(2,1)}), bf16[16,2,16,512]{3,2,1,0:T(8,128)(2,1)S(1)}, u32[]{:S(2)}, u32[]{:S(2)}) async-start(bf16[16,2,16,512]{3,2,1,0:T(8,128)(2,1)} %get-tuple-element.28), calls=%async_computation.1 | async-start | bytes 1048576 | tf_op jit(solution)/shard_map/all_to_all | solution.py:405
  11.7 10.4 %copy-start.5 = (f32[512]{0:T(512)S(1)}, f32[512]{0:T(512)}, u32[]{:S(2)}) copy-start(f32[512]{0:T(512)} %param.12) | copy-start | bytes 6148
  11.7 6.8 %collective-permute-start = (bf16[2,2,8,512]{3,2,1,0:T(8,128)(2,1)S(1)}, bf16[2,2,8,512]{3,2,1,0:T(8,128)(2,1)S(1)}, u32[]{:S(2)}, u32[]{:S(2)}) collective-permute-start(bf16[2,2,8,512]{3,2,1,0:T(8,128)(2,1)S(1)} %get-tuple-element.26), channel_id=1, source_target_pairs={{0,1},{1,2},{2,3},{3,4},{4,5},{5,6},{6,7},{7,8},{8,9},{9,10},{10,1... | collective-permute-start | bytes 98312 | tf_op jit(solution)/shard_map/ppermute | solution.py:403
  16.6 5.5 %collective-permute-start.1 = (bf16[2,2,8,512]{3,2,1,0:T(8,128)(2,1)S(1)}, bf16[2,2,8,512]{3,2,1,0:T(8,128)(2,1)S(1)}, u32[]{:S(2)}, u32[]{:S(2)}) collective-permute-start(bf16[2,2,8,512]{3,2,1,0:T(8,128)(2,1)S(1)} %get-tuple-element.27), channel_id=1, source_target_pairs={{1,0},{2,1},{3,2},{4,3},{5,4},{6,5},{7,6},{8,7},{9,8},{10,9},{11,1... | collective-permute-start | bytes 98312 | tf_op jit(solution)/shard_map/ppermute | solution.py:404
  24.1 18.5 %copy-start.6 = (bf16[512,256]{1,0:T(8,128)(2,1)S(1)}, bf16[512,256]{1,0:T(8,128)(2,1)}, u32[]{:S(2)}) copy-start(bf16[512,256]{1,0:T(8,128)(2,1)} %w_query.1) | copy-start | bytes 786436
  24.1 18.5 %copy-start.7 = (bf16[512,256]{1,0:T(8,128)(2,1)S(1)}, bf16[512,256]{1,0:T(8,128)(2,1)}, u32[]{:S(2)}) copy-start(bf16[512,256]{1,0:T(8,128)(2,1)} %w_key.1) | copy-start | bytes 786436
  24.1 18.5 %copy-start.8 = (bf16[512,256]{1,0:T(8,128)(2,1)S(1)}, bf16[512,256]{1,0:T(8,128)(2,1)}, u32[]{:S(2)}) copy-start(bf16[512,256]{1,0:T(8,128)(2,1)} %w_value.1) | copy-start | bytes 786436
  27.1 15.5 %all-to-all-start = ((bf16[16,2,16,512]{3,2,1,0:T(8,128)(2,1)}), bf16[16,2,16,512]{3,2,1,0:T(8,128)(2,1)S(1)}, u32[]{:S(2)}, u32[]{:S(2)}) async-start(bf16[16,2,16,512]{3,2,1,0:T(8,128)(2,1)} %shard_map.153), calls=%async_computation | async-start | bytes 1048576 | tf_op jit(solution)/shard_map/all_to_all | solution.py:415
  31.5 11.2 %copy-start.10 = (f32[512]{0:T(512)S(1)}, f32[512]{0:T(512)}, u32[]{:S(2)}) copy-start(f32[512]{0:T(512)} %param.13) | copy-start | bytes 6148
  42.7 1.0 copy-start.9
  50.4 19.3 %all-to-all-start.2 = ((bf16[16,2,16,512]{3,2,1,0:T(8,128)(2,1)}), bf16[16,2,16,512]{3,2,1,0:T(8,128)(2,1)S(1)}, u32[]{:S(2)}, u32[]{:S(2)}) async-start(bf16[16,2,16,512]{3,2,1,0:T(8,128)(2,1)} %get-tuple-element.29), calls=%async_computation.2 | async-start | bytes 1048576 | tf_op jit(solution)/shard_map/all_to_all | solution.py:441
  54.0 15.7 %copy-start.3 = (bf16[2,8,32,512]{3,2,1,0:T(8,128)(2,1)S(1)}, bf16[2,8,32,512]{3,2,1,0:T(8,128)(2,1)}, u32[]{:S(2)}) copy-start(bf16[2,8,32,512]{3,2,1,0:T(8,128)(2,1)} %cot.5) | copy-start | bytes 1572868
  54.1 15.6 %collective-permute-start.2 = (bf16[16,128,128]{2,1,0:T(8,128)(2,1)S(1)}, bf16[16,128,128]{2,1,0:T(8,128)(2,1)S(1)}, u32[]{:S(2)}, u32[]{:S(2)}) collective-permute-start(bf16[16,128,128]{2,1,0:T(8,128)(2,1)S(1)} %slice_bitcast_fusion), channel_id=1, source_target_pairs={{0,1},{1,0},{2,3},{3,2},{4,5},{5,4},{6,7},{7,6},{8,9},{9,8},{10,11... | collective-permute-start | bytes 1572872 | tf_op jit(solution)/shard_map/ppermute | solution.py:442
  72.1 21.9 %all-to-all-start.3 = ((bf16[16,144,128]{2,1,0:T(8,128)(2,1)}), bf16[16,144,128]{2,1,0:T(8,128)(2,1)S(1)}, u32[]{:S(2)}, u32[]{:S(2)}) async-start(bf16[16,144,128]{2,1,0:T(8,128)(2,1)} %get-tuple-element.32), calls=%async_computation.3 | async-start | bytes 1179648 | tf_op jit(solution)/shard_map/all_to_all | solution.py:453
  79.3 8.9 %collective-permute-start.3 = (bf16[2,8,512]{2,1,0:T(8,128)(2,1)S(1)}, bf16[2,8,512]{2,1,0:T(8,128)(2,1)S(1)}, u32[]{:S(2)}, u32[]{:S(2)}) collective-permute-start(bf16[2,8,512]{2,1,0:T(8,128)(2,1)S(1)} %get-tuple-element.33), channel_id=1, source_target_pairs={{0,1},{1,2},{2,3},{3,4},{4,5},{5,6},{6,7},{7,8},{8,9},{9,10},{10,1... | collective-permute-start | bytes 49160 | tf_op jit(solution)/shard_map/ppermute | solution.py:454
  85.7 5.4 %collective-permute-start.4 = (bf16[2,8,512]{2,1,0:T(8,128)(2,1)S(1)}, bf16[2,8,512]{2,1,0:T(8,128)(2,1)S(1)}, u32[]{:S(2)}, u32[]{:S(2)}) collective-permute-start(bf16[2,8,512]{2,1,0:T(8,128)(2,1)S(1)} %get-tuple-element.34), channel_id=1, source_target_pairs={{1,0},{2,1},{3,2},{4,3},{5,4},{6,5},{7,6},{8,7},{9,8},{10,9},{11,1... | collective-permute-start | bytes 49160 | tf_op jit(solution)/shard_map/ppermute | solution.py:455

commit v3 on v2

--- a/solution.py
+++ b/solution.py
@@ -26,11 +26,13 @@
     return pltpu.CompilerParams(vmem_limit_bytes=mib * 1024 * 1024)
 
 
-def call(kernel, outs, mib, flops=0, moved=0, scratch=(), smem=0):
+def call(kernel, outs, mib, flops=0, moved=0, scratch=(), smem=0, hbm=()):
     vmem = pl.BlockSpec(memory_space=pltpu.VMEM)
 
     def run(*args):
         specs = [pl.BlockSpec(memory_space=pltpu.SMEM)] * smem + [vmem] * (len(args) - smem)
+        for at in hbm:
+            specs[at] = pl.BlockSpec(memory_space=pltpu.HBM)
         return pl.pallas_call(
             kernel,
             out_shape=outs,
@@ -81,8 +83,15 @@
     return below, value, above
 
 
-def start_kernel(lat, cot, packed, first, last, edges):
+def start_kernel(lat_far, cot_far, packed, first, last, lat, cot, edges, sems):
+    copies = [
+        pltpu.make_async_copy(lat_far, lat, sems.at[0]),
+        pltpu.make_async_copy(cot_far, cot, sems.at[1]),
+    ]
+    for copy in copies:
+        copy.start()
     for which, ref in enumerate((lat, cot)):
+        copies[which].wait()
         for s in range(SL):
             for h in range(H):
                 edges[0, which, s, h : h + 1, :] = ref[s, h, :PX, :].astype(F32)[:1]
@@ -244,7 +253,7 @@
 
 def taps_kernel(
     predivide, lat, left, right, cot, ret, gain_sum, kept, got,
-    out, first, last, edge_l, edge_r, tiles, edges,
+    out, edge_l, edge_r, tiles,
 ):
     tiles[...] = jnp.zeros_like(tiles)
     for s in range(SL):
@@ -285,16 +294,20 @@
             tiles[4 * part + r // 3, pl.ds(r % 3, 1), :] = jnp.sum(sums[r], axis=0, keepdims=True)
         tiles[4 * part + 3, pl.ds(1, 1), :] = gain_sum[:, here]
 
+    whole = tiles[...] * predivide
+    high = whole.astype(BF16).astype(F32)
+    out[:, LANES:, :] = jnp.concatenate([high, whole - high], axis=1).astype(BF16)
+    out[:, :LANES, :] = (kept[0].astype(F32) + got[...].astype(F32)).astype(BF16)
+
+
+def edges_kernel(after, ret, first, last, edges):
+    del after
     for s in range(SL):
         for h in range(H):
             edges[0, s, h : h + 1, :] = ret[2 * h, s].astype(F32)[:1]
             edges[1, s, h : h + 1, :] = ret[2 * h + 1, s].astype(F32)[PX - 1 :]
     first[...] = edges[0].astype(BF16)
     last[...] = edges[1].astype(BF16)
-    whole = tiles[...] * predivide
-    high = whole.astype(BF16).astype(F32)
-    out[:, LANES:, :] = jnp.concatenate([high, whole - high], axis=1).astype(BF16)
-    out[:, :LANES, :] = (kept[0].astype(F32) + got[...].astype(F32)).astype(BF16)
 
 
 def latents_kernel(lat, cot, ret, left, right, back_l, back_r, taps, out, edge_l, edge_r):
@@ -396,14 +409,21 @@
     cot_sent, first, last = call(
         start_kernel,
         (struct((GROUPS, SL, PX, C), BF16), both_edges, both_edges),
-        16,
+        56,
         moved=1_500_000,
-        scratch=[pltpu.VMEM((2, 2, SL, H, C), F32)],
+        hbm=(0, 1),
+        scratch=[
+            pltpu.VMEM((SL, H, WL, C), BF16),
+            pltpu.VMEM((SL, H, WL, C), BF16),
+            pltpu.VMEM((2, 2, SL, H, C), F32),
+            pltpu.SemaphoreType.DMA((2,)),
+        ],
     )(latents, cotangent)
     left = lax.ppermute(last, "azim", up)
     right = lax.ppermute(first, "azim", down)
     recv_cot = lax.all_to_all(cot_sent, "sweep", split_axis=0, concat_axis=0, tiled=True)
 
+    rows = GROUPS * SL * PX
     y_sent = call(
         forward_kernel,
         struct((GROUPS, SL, PX, C), BF16),
@@ -414,7 +434,6 @@
     )(latents, left, right, conv_kernel, bias_row)
     recv = lax.all_to_all(y_sent, "sweep", split_axis=0, concat_axis=0, tiled=True)
 
-    rows = GROUPS * SL * PX
     grad_attn, halves, gain_sum = call(
         functools.partial(attend_kernel, predivide),
         (
@@ -441,18 +460,27 @@
     ret = lax.all_to_all(grad_attn, "sweep", split_axis=0, concat_axis=0, tiled=True)
     got = lax.ppermute(halves[1], "azim", pair)
 
-    one_edge = struct((SL, H, C), BF16)
-    first_sent, back_first, back_last = call(
+    first_sent = call(
         functools.partial(taps_kernel, predivide),
-        (struct((GROUPS, LANES + 16, LANES), BF16), one_edge, one_edge),
+        struct((GROUPS, LANES + 16, LANES), BF16),
         16,
         flops=10_000_000,
         moved=3_000_000,
-        scratch=[edge, edge, pltpu.VMEM((GROUPS, 8, LANES), F32), pltpu.VMEM((2, SL, H, C), F32)],
+        scratch=[edge, edge, pltpu.VMEM((GROUPS, 8, LANES), F32)],
     )(latents, left, right, cotangent, ret, gain_sum, halves, got)
     first_recv = lax.all_to_all(first_sent, "sweep", split_axis=0, concat_axis=0, tiled=True)
+    one_edge = struct((SL, H, C), BF16)
+    back_first, back_last = call(
+        edges_kernel,
+        (one_edge, one_edge),
+        16,
+        moved=100_000,
+        hbm=(0,),
+        scratch=[pltpu.VMEM((2, SL, H, C), F32)],
+    )(first_sent, ret)
     back_l = lax.ppermute(back_last, "azim", up)
     back_r = lax.ppermute(back_first, "azim", down)
+    first_recv, back_l, back_r = lax.optimization_barrier((first_recv, back_l, back_r))
 
     grad_latents = call(
         latents_kernel,
@@ -462,12 +490,12 @@
         moved=4_000_000,
         scratch=[edge, edge],
     )(latents, cotangent, ret, left, right, back_l, back_r, conv_kernel)
-    first_recv, grad_latents = lax.optimization_barrier((first_recv, grad_latents))
 
     second_sent = call(
         second_kernel, struct((strips, 16, LANES), BF16), 16, moved=1_000_000, smem=1
     )(core, first_recv)
     second_recv = lax.all_to_all(second_sent, "azim", split_axis=0, concat_axis=0, tiled=True)
+    second_recv, grad_latents = lax.optimization_barrier((second_recv, grad_latents))
     third_sent = call(third_kernel, struct((GROUPS, 16, LANES), F32), 16, moved=300_000)(
         second_recv
     )

time: 141 us -> 140 us (level)
  blocking collectives: 44.8 us -> 10.1 us
  starting transfers between devices: 53 us -> 75.6 us
  waiting for transfers between devices: 22.7 us -> 34.7 us
  local copies, waits for them, and re-layouts: 3.1 us -> 1.04 us
  Pallas kernels: 15.2 us -> 16.9 us
    all_to_all x1 -> x0, blocking collectives: 34.5 us -> none  [on_device(): lax.all_to_all(second_sent, 'azim', split_axis=0, concat_axis=0, tiled=True)]
    all_to_all x0 -> x1, starting transfers between devices: none -> 22.7 us  [on_device(): lax.all_to_all(second_sent, 'azim', split_axis=0, concat_axis=0, tiled=True)]
    all_to_all x0 -> x1, waiting for transfers between devices: none -> 9.73 us  [on_device(): lax.all_to_all(second_sent, 'azim', split_axis=0, concat_axis=0, tiled=True)]
    all_to_all x1, waiting for transfers between devices: 0.63 us -> 2.89 us  [on_device(): lax.all_to_all(first_sent, 'sweep', split_axis=0, concat_axis=0, tiled=True)]
    unnamed x22, local copies, waits for them, and re-layouts: 3.06 us -> 1 us
    pallas_call x8 -> x9, Pallas kernels: 15.2 us -> 16.9 us  [run(): pl.pallas_call(kernel, out_shape=outs, in_specs=specs, out_specs=jax.tree...]
  transfers between devices with their start and end apart: 9 -> 10, of which waited for: 6 -> 7; matrix products, arithmetic and copies ran while one was open for 0% -> 0% of each run, Pallas kernels for 3% -> 3%
where the time goes in v3:
time: 140 us; the launch traced here: 139 us
  starting transfers between devices  75.6 us (54%)
  waiting for transfers between devices  34.7 us (25%)
  Pallas kernels  16.9 us (12%)
  blocking collectives  10.1 us (7%)
    all_to_all x1, starting transfers between devices, on_device(): lax.all_to_all(second_sent, 'azim', split_axis=0, concat_axis=0, tiled=True)  22.7 us
    pallas_call x9, Pallas kernels, run(): pl.pallas_call(kernel, out_shape=outs, in_specs=specs, out_specs=jax.tree...  16.9 us
    ppermute x1, starting transfers between devices, on_device(): got = lax.ppermute(halves[1], 'azim', pair)  14.1 us
    all_to_all x1, waiting for transfers between devices, on_device(): lax.all_to_all(y_sent, 'sweep', split_axis=0, concat_axis=0, tiled=True)  11.1 us
    all_to_all x1, blocking collectives, on_device(): lax.all_to_all(third_sent, 'sweep', split_axis=0, concat_axis=0, tiled=True)  10.1 us
    all_to_all x1, waiting for transfers between devices, on_device(): lax.all_to_all(second_sent, 'azim', split_axis=0, concat_axis=0, tiled=True)  9.73 us
    all_to_all x1, starting transfers between devices, on_device(): lax.all_to_all(cot_sent, 'sweep', split_axis=0, concat_axis=0, tiled=True)  8.14 us
    all_to_all x1, starting transfers between devices, on_device(): lax.all_to_all(first_sent, 'sweep', split_axis=0, concat_axis=0, tiled=True)  7.17 us
  transfers between devices with their start and end apart: 10, of which 7 were waited for; matrix products, arithmetic and copies ran while one was open for 0% of the time, Pallas kernels for 3%

profile of v3, /device:TPU:1, one launch (start us, length us, event | category | flops | bytes accessed | tf_op | source)
XLA Modules:
  0.0 139.2 jit_solution(3516230966809140937)
XLA Ops:
  0.6 2.1 %shard_map.152 = (bf16[16,2,16,512]{3,2,1,0:T(8,128)(2,1)}, bf16[2,2,8,512]{3,2,1,0:T(8,128)(2,1)}, bf16[2,2,8,512]{3,2,1,0:T(8,128)(2,1)}) custom-call(bf16[2,8,32,512]{3,2,1,0:T(8,128)(2,1)} %lat.5, bf16[2,8,32,512]{3,2,1,0:T(8,128)(2,1)} %cot.3), custom_call_target="tpu_custom_call" | custom-call | bytes 1500000 | tf_op jit(solution)/shard_map/pallas_call | solution.py:36
  2.7 0.0 copy-start.9
  2.7 0.0 copy-start
  2.7 0.0 copy-start.2
  2.8 8.1 %all-to-all-start.1 = ((bf16[16,2,16,512]{3,2,1,0:T(8,128)(2,1)}), bf16[16,2,16,512]{3,2,1,0:T(8,128)(2,1)S(1)}, u32[]{:S(2)}, u32[]{:S(2)}) async-start(bf16[16,2,16,512]{3,2,1,0:T(8,128)(2,1)} %get-tuple-element.30), calls=%async_computation.1 | async-start | bytes 1048576 | tf_op jit(solution)/shard_map/all_to_all | solution.py:424
  10.9 0.0 copy-start.3
  10.9 4.8 %collective-permute-start = (bf16[2,2,8,512]{3,2,1,0:T(8,128)(2,1)S(1)}, bf16[2,2,8,512]{3,2,1,0:T(8,128)(2,1)S(1)}, u32[]{:S(2)}, u32[]{:S(2)}) collective-permute-start(bf16[2,2,8,512]{3,2,1,0:T(8,128)(2,1)S(1)} %copy-done.10), channel_id=1, source_target_pairs={{0,1},{1,2},{2,3},{3,4},{4,5},{5,6},{6,7},{7,8},{8,9},{9,10},{10,1... | collective-permute-start | bytes 98312 | tf_op jit(solution)/shard_map/ppermute | solution.py:422
  15.8 1.9 %collective-permute-start.1 = (bf16[2,2,8,512]{3,2,1,0:T(8,128)(2,1)S(1)}, bf16[2,2,8,512]{3,2,1,0:T(8,128)(2,1)S(1)}, u32[]{:S(2)}, u32[]{:S(2)}) collective-permute-start(bf16[2,2,8,512]{3,2,1,0:T(8,128)(2,1)S(1)} %copy-done.9), channel_id=1, source_target_pairs={{1,0},{2,1},{3,2},{4,3},{5,4},{6,5},{7,6},{8,7},{9,8},{10,9},{11,1... | collective-permute-start | bytes 98312 | tf_op jit(solution)/shard_map/ppermute | solution.py:423
  17.7 3.6 %collective-permute-done.1.right = bf16[2,2,8,512]{3,2,1,0:T(8,128)(2,1)S(1)} collective-permute-done((bf16[2,2,8,512]{3,2,1,0:T(8,128)(2,1)S(1)}, bf16[2,2,8,512]{3,2,1,0:T(8,128)(2,1)S(1)}, u32[]{:S(2)}, u32[]{:S(2)}) %collective-permute-start.1) | collective-permute-done | bytes 32800 | tf_op jit(solution)/shard_map/ppermute | solution.py:423
  21.3 2.0 %shard_map.153 = bf16[16,2,16,512]{3,2,1,0:T(8,128)(2,1)} custom-call(bf16[2,8,32,512]{3,2,1,0:T(8,128)(2,1)S(1)} %copy-done, bf16[2,2,8,512]{3,2,1,0:T(8,128)(2,1)S(1)} %collective-permute-done.left, bf16[2,2,8,512]{3,2,1,0:T(8,128)(2,1)S(1)} %collective-permute-done.1.right, f32[9,512]{1,0:T(8,128)S(1)} %copy-done.2, f32[1,512]{1,0:T(1,128)S(1)} %bitcast.7), custom_call_target="tpu_custom_call" | custom-call | flops 10000000 | bytes 1000000 | tf_op jit(solution)/shard_map/pallas_call | solution.py:36
  23.3 3.0 %all-to-all-done.1.recv_cot = bf16[16,2,16,512]{3,2,1,0:T(8,128)(2,1)S(1)} async-done(((bf16[16,2,16,512]{3,2,1,0:T(8,128)(2,1)}), bf16[16,2,16,512]{3,2,1,0:T(8,128)(2,1)S(1)}, u32[]{:S(2)}, u32[]{:S(2)}) %all-to-all-start.1) | async-done | bytes 524320 | tf_op jit(solution)/shard_map/all_to_all | solution.py:424
  26.3 4.4 %all-to-all-start = ((bf16[16,2,16,512]{3,2,1,0:T(8,128)(2,1)}), bf16[16,2,16,512]{3,2,1,0:T(8,128)(2,1)S(1)}, u32[]{:S(2)}, u32[]{:S(2)}) async-start(bf16[16,2,16,512]{3,2,1,0:T(8,128)(2,1)} %shard_map.153), calls=%async_computation | async-start | bytes 1048576 | tf_op jit(solution)/shard_map/all_to_all | solution.py:435
  30.7 0.0 copy-start.8
  30.7 11.1 %all-to-all-done.recv = bf16[16,2,16,512]{3,2,1,0:T(8,128)(2,1)S(1)} async-done(((bf16[16,2,16,512]{3,2,1,0:T(8,128)(2,1)}), bf16[16,2,16,512]{3,2,1,0:T(8,128)(2,1)S(1)}, u32[]{:S(2)}, u32[]{:S(2)}) %all-to-all-start) | async-done | bytes 524320 | tf_op jit(solution)/shard_map/all_to_all | solution.py:435
  41.9 0.9 copy-done.7
  42.8 6.8 %shard_map.154 = (bf16[16,2,16,512]{3,2,1,0:T(8,128)(2,1)}, bf16[2,16,128,128]{3,2,1,0:T(8,128)(2,1)S(1)}, f32[1,512]{1,0:T(1,128)S(1)}) custom-call(s32[1]{0:T(128)} %bitcast.core, bf16[16,2,16,512]{3,2,1,0:T(8,128)(2,1)S(1)} %all-to-all-done.recv, bf16[16,2,16,512]{3,2,1,0:T(8,128)(2,1)S(1)} %all-to-all-done.1.recv_cot, bf16[512,256]{1,0:T(8,128)(2,1)S(1)} %copy-done.4, ...), custom_call_target="tpu_custom_call" | custom-call | flops 2000000000 | bytes 6000000 | tf_op jit(solution)/shard_map/pallas_call | solution.py:36
  49.6 3.6 %all-to-all-start.2 = ((bf16[16,2,16,512]{3,2,1,0:T(8,128)(2,1)}), bf16[16,2,16,512]{3,2,1,0:T(8,128)(2,1)S(1)}, u32[]{:S(2)}, u32[]{:S(2)}) async-start(bf16[16,2,16,512]{3,2,1,0:T(8,128)(2,1)} %get-tuple-element.31), calls=%async_computation.2 | async-start | bytes 1048576 | tf_op jit(solution)/shard_map/all_to_all | solution.py:460
  53.3 14.1 %collective-permute-start.2 = (bf16[16,128,128]{2,1,0:T(8,128)(2,1)S(1)}, bf16[16,128,128]{2,1,0:T(8,128)(2,1)S(1)}, u32[]{:S(2)}, u32[]{:S(2)}) collective-permute-start(bf16[16,128,128]{2,1,0:T(8,128)(2,1)S(1)} %slice_bitcast_fusion), channel_id=1, source_target_pairs={{0,1},{1,0},{2,3},{3,2},{4,5},{5,4},{6,7},{7,6},{8,9},{9,8},{10,11... | collective-permute-start | bytes 1572872 | tf_op jit(solution)/shard_map/ppermute | solution.py:461
  67.3 1.5 %collective-permute-done.2.got = bf16[16,128,128]{2,1,0:T(8,128)(2,1)S(1)} collective-permute-done((bf16[16,128,128]{2,1,0:T(8,128)(2,1)S(1)}, bf16[16,128,128]{2,1,0:T(8,128)(2,1)S(1)}, u32[]{:S(2)}, u32[]{:S(2)}) %collective-permute-start.2) | collective-permute-done | bytes 524320 | tf_op jit(solution)/shard_map/ppermute | solution.py:461
  68.9 2.2 %shard_map.155.after = bf16[16,144,128]{2,1,0:T(8,128)(2,1)} custom-call(bf16[2,8,32,512]{3,2,1,0:T(8,128)(2,1)S(1)} %copy-done, bf16[2,2,8,512]{3,2,1,0:T(8,128)(2,1)S(1)} %collective-permute-done.left, bf16[2,2,8,512]{3,2,1,0:T(8,128)(2,1)S(1)} %collective-permute-done.1.right, bf16[2,8,32,512]{3,2,1,0:T(8,128)(2,1)S(1)} %copy-done.1, ...), custom_call_target="tpu_custom_call" | custom-call | flops 10000000 | bytes 3000000 | tf_op jit(solution)/shard_map/pallas_call | solution.py:36
  71.1 7.2 %all-to-all-start.3 = ((bf16[16,144,128]{2,1,0:T(8,128)(2,1)}), bf16[16,144,128]{2,1,0:T(8,128)(2,1)S(1)}, u32[]{:S(2)}, u32[]{:S(2)}) async-start(bf16[16,144,128]{2,1,0:T(8,128)(2,1)} %shard_map.155.after), calls=%async_computation.3 | async-start | bytes 1179648 | tf_op jit(solution)/shard_map/all_to_all | solution.py:471
  78.3 0.1 shard_map.156
  78.3 6.4 %collective-permute-start.3 = (bf16[2,8,512]{2,1,0:T(8,128)(2,1)S(1)}, bf16[2,8,512]{2,1,0:T(8,128)(2,1)S(1)}, u32[]{:S(2)}, u32[]{:S(2)}) collective-permute-start(bf16[2,8,512]{2,1,0:T(8,128)(2,1)S(1)} %get-tuple-element.34), channel_id=1, source_target_pairs={{0,1},{1,2},{2,3},{3,4},{4,5},{5,6},{6,7},{7,8},{8,9},{9,10},{10,1... | collective-permute-start | bytes 49160 | tf_op jit(solution)/shard_map/ppermute | solution.py:481
  84.7 2.5 %collective-permute-start.4 = (bf16[2,8,512]{2,1,0:T(8,128)(2,1)S(1)}, bf16[2,8,512]{2,1,0:T(8,128)(2,1)S(1)}, u32[]{:S(2)}, u32[]{:S(2)}) collective-permute-start(bf16[2,8,512]{2,1,0:T(8,128)(2,1)S(1)} %get-tuple-element.35), channel_id=1, source_target_pairs={{1,0},{2,1},{3,2},{4,3},{5,4},{6,5},{7,6},{8,7},{9,8},{10,9},{11,1... | collective-permute-start | bytes 49160 | tf_op jit(solution)/shard_map/ppermute | solution.py:482
  87.2 2.8 %collective-permute-done.4.back_r = bf16[2,8,512]{2,1,0:T(8,128)(2,1)S(1)} collective-permute-done((bf16[2,8,512]{2,1,0:T(8,128)(2,1)S(1)}, bf16[2,8,512]{2,1,0:T(8,128)(2,1)S(1)}, u32[]{:S(2)}, u32[]{:S(2)}) %collective-permute-start.4) | collective-permute-done | bytes 16416 | tf_op jit(solution)/shard_map/ppermute | solution.py:482
  90.1 2.9 %all-to-all-done.3.recv = bf16[16,144,128]{2,1,0:T(8,128)(2,1)S(1)} async-done(((bf16[16,144,128]{2,1,0:T(8,128)(2,1)}), bf16[16,144,128]{2,1,0:T(8,128)(2,1)S(1)}, u32[]{:S(2)}, u32[]{:S(2)}) %all-to-all-start.3) | async-done | bytes 589856 | tf_op jit(solution)/shard_map/all_to_all | solution.py:471
  92.9 0.7 shard_map.157
  93.7 22.7 %all-to-all-start.4 = ((bf16[32,16,128]{2,1,0:T(8,128)(2,1)}), bf16[32,16,128]{2,1,0:T(8,128)(2,1)S(1)}, u32[]{:S(2)}, u32[]{:S(2)}) async-start(bf16[32,16,128]{2,1,0:T(8,128)(2,1)} %shard_map.157), calls=%async_computation.4 | async-start | bytes 262144 | tf_op jit(solution)/shard_map/all_to_all | solution.py:497
  116.4 2.3 %shard_map.158 = f32[2,8,32,512]{3,2,1,0:T(8,128)} custom-call(bf16[2,8,32,512]{3,2,1,0:T(8,128)(2,1)S(1)} %copy-done, bf16[2,8,32,512]{3,2,1,0:T(8,128)(2,1)S(1)} %copy-done.1, bf16[16,2,16,512]{3,2,1,0:T(8,128)(2,1)S(1)} %all-to-all-done.2.ret, bf16[2,2,8,512]{3,2,1,0:T(8,128)(2,1)S(1)} %collective-permute-done.left, ...), custom_call_target="tpu_custom_call" | custom-call | flops 10000000 | bytes 4000000 | tf_op jit(solution)/shard_map/pallas_call | solution.py:36
  118.7 9.7 %all-to-all-done.4.recv = bf16[32,16,128]{2,1,0:T(8,128)(2,1)S(1)} async-done(((bf16[32,16,128]{2,1,0:T(8,128)(2,1)}), bf16[32,16,128]{2,1,0:T(8,128)(2,1)S(1)}, u32[]{:S(2)}, u32[]{:S(2)}) %all-to-all-start.4) | async-done | bytes 131104 | tf_op jit(solution)/shard_map/all_to_all | solution.py:497
  128.5 10.1 %all_to_all.30.recv = f32[16,16,128]{2,1,0:T(8,128)S(1)} all-to-all(f32[16,16,128]{2,1,0:T(8,128)S(1)} %shard_map.159), channel_id=1, replica_groups=mesh['sweep'=16,'azim'=32] {'sweep'}, dimensions={0} | all-to-all | bytes 262144 | tf_op jit(solution)/shard_map/all_to_all | solution.py:502
  138.6 0.7 shard_map.160
  (21 shorter events, 0.1 us)
Async XLA Ops:
  2.7 8.2 %copy-start.10 = (bf16[2,2,8,512]{3,2,1,0:T(8,128)(2,1)S(1)}, bf16[2,2,8,512]{3,2,1,0:T(8,128)(2,1)}, u32[]{:S(2)}) copy-start(bf16[2,2,8,512]{3,2,1,0:T(8,128)(2,1)} %get-tuple-element.28) | copy-start | bytes 98308
  2.7 13.1 %copy-start.9 = (bf16[2,2,8,512]{3,2,1,0:T(8,128)(2,1)S(1)}, bf16[2,2,8,512]{3,2,1,0:T(8,128)(2,1)}, u32[]{:S(2)}) copy-start(bf16[2,2,8,512]{3,2,1,0:T(8,128)(2,1)} %get-tuple-element.29) | copy-start | bytes 98308
  2.7 18.6 %copy-start = (bf16[2,8,32,512]{3,2,1,0:T(8,128)(2,1)S(1)}, bf16[2,8,32,512]{3,2,1,0:T(8,128)(2,1)}, u32[]{:S(2)}) copy-start(bf16[2,8,32,512]{3,2,1,0:T(8,128)(2,1)} %lat.5) | copy-start | bytes 1572868
  2.7 18.6 %copy-start.2 = (f32[9,512]{1,0:T(8,128)S(1)}, f32[9,512]{1,0:T(8,128)}, u32[]{:S(2)}) copy-start(f32[9,512]{1,0:T(8,128)} %taps.3) | copy-start | bytes 55300
  2.8 23.6 %all-to-all-start.1 = ((bf16[16,2,16,512]{3,2,1,0:T(8,128)(2,1)}), bf16[16,2,16,512]{3,2,1,0:T(8,128)(2,1)S(1)}, u32[]{:S(2)}, u32[]{:S(2)}) async-start(bf16[16,2,16,512]{3,2,1,0:T(8,128)(2,1)} %get-tuple-element.30), calls=%async_computation.1 | async-start | bytes 1048576 | tf_op jit(solution)/shard_map/all_to_all | solution.py:424
  10.9 10.4 %copy-start.3 = (f32[512]{0:T(512)S(1)}, f32[512]{0:T(512)}, u32[]{:S(2)}) copy-start(f32[512]{0:T(512)} %param.12) | copy-start | bytes 6148
  10.9 6.8 %collective-permute-start = (bf16[2,2,8,512]{3,2,1,0:T(8,128)(2,1)S(1)}, bf16[2,2,8,512]{3,2,1,0:T(8,128)(2,1)S(1)}, u32[]{:S(2)}, u32[]{:S(2)}) collective-permute-start(bf16[2,2,8,512]{3,2,1,0:T(8,128)(2,1)S(1)} %copy-done.10), channel_id=1, source_target_pairs={{0,1},{1,2},{2,3},{3,4},{4,5},{5,6},{6,7},{7,8},{8,9},{9,10},{10,1... | collective-permute-start | bytes 98312 | tf_op jit(solution)/shard_map/ppermute | solution.py:422
  15.8 5.5 %collective-permute-start.1 = (bf16[2,2,8,512]{3,2,1,0:T(8,128)(2,1)S(1)}, bf16[2,2,8,512]{3,2,1,0:T(8,128)(2,1)S(1)}, u32[]{:S(2)}, u32[]{:S(2)}) collective-permute-start(bf16[2,2,8,512]{3,2,1,0:T(8,128)(2,1)S(1)} %copy-done.9), channel_id=1, source_target_pairs={{1,0},{2,1},{3,2},{4,3},{5,4},{6,5},{7,6},{8,7},{9,8},{10,9},{11,1... | collective-permute-start | bytes 98312 | tf_op jit(solution)/shard_map/ppermute | solution.py:423
  23.3 18.5 %copy-start.4 = (bf16[512,256]{1,0:T(8,128)(2,1)S(1)}, bf16[512,256]{1,0:T(8,128)(2,1)}, u32[]{:S(2)}) copy-start(bf16[512,256]{1,0:T(8,128)(2,1)} %w_query.1) | copy-start | bytes 786436
  23.3 18.5 %copy-start.5 = (bf16[512,256]{1,0:T(8,128)(2,1)S(1)}, bf16[512,256]{1,0:T(8,128)(2,1)}, u32[]{:S(2)}) copy-start(bf16[512,256]{1,0:T(8,128)(2,1)} %w_key.1) | copy-start | bytes 786436
  23.3 18.5 %copy-start.6 = (bf16[512,256]{1,0:T(8,128)(2,1)S(1)}, bf16[512,256]{1,0:T(8,128)(2,1)}, u32[]{:S(2)}) copy-start(bf16[512,256]{1,0:T(8,128)(2,1)} %w_value.1) | copy-start | bytes 786436
  26.3 15.6 %all-to-all-start = ((bf16[16,2,16,512]{3,2,1,0:T(8,128)(2,1)}), bf16[16,2,16,512]{3,2,1,0:T(8,128)(2,1)S(1)}, u32[]{:S(2)}, u32[]{:S(2)}) async-start(bf16[16,2,16,512]{3,2,1,0:T(8,128)(2,1)} %shard_map.153), calls=%async_computation | async-start | bytes 1048576 | tf_op jit(solution)/shard_map/all_to_all | solution.py:435
  30.7 11.2 %copy-start.8 = (f32[512]{0:T(512)S(1)}, f32[512]{0:T(512)}, u32[]{:S(2)}) copy-start(f32[512]{0:T(512)} %param.13) | copy-start | bytes 6148
  41.9 1.0 copy-start.7
  49.6 19.2 %all-to-all-start.2 = ((bf16[16,2,16,512]{3,2,1,0:T(8,128)(2,1)}), bf16[16,2,16,512]{3,2,1,0:T(8,128)(2,1)S(1)}, u32[]{:S(2)}, u32[]{:S(2)}) async-start(bf16[16,2,16,512]{3,2,1,0:T(8,128)(2,1)} %get-tuple-element.31), calls=%async_computation.2 | async-start | bytes 1048576 | tf_op jit(solution)/shard_map/all_to_all | solution.py:460
  53.2 15.6 %copy-start.1 = (bf16[2,8,32,512]{3,2,1,0:T(8,128)(2,1)S(1)}, bf16[2,8,32,512]{3,2,1,0:T(8,128)(2,1)}, u32[]{:S(2)}) copy-start(bf16[2,8,32,512]{3,2,1,0:T(8,128)(2,1)} %cot.3) | copy-start | bytes 1572868
  53.3 15.6 %collective-permute-start.2 = (bf16[16,128,128]{2,1,0:T(8,128)(2,1)S(1)}, bf16[16,128,128]{2,1,0:T(8,128)(2,1)S(1)}, u32[]{:S(2)}, u32[]{:S(2)}) collective-permute-start(bf16[16,128,128]{2,1,0:T(8,128)(2,1)S(1)} %slice_bitcast_fusion), channel_id=1, source_target_pairs={{0,1},{1,0},{2,3},{3,2},{4,5},{5,4},{6,7},{7,6},{8,9},{9,8},{10,11... | collective-permute-start | bytes 1572872 | tf_op jit(solution)/shard_map/ppermute | solution.py:461
  71.1 21.9 %all-to-all-start.3 = ((bf16[16,144,128]{2,1,0:T(8,128)(2,1)}), bf16[16,144,128]{2,1,0:T(8,128)(2,1)S(1)}, u32[]{:S(2)}, u32[]{:S(2)}) async-start(bf16[16,144,128]{2,1,0:T(8,128)(2,1)} %shard_map.155.after), calls=%async_computation.3 | async-start | bytes 1179648 | tf_op jit(solution)/shard_map/all_to_all | solution.py:471
  78.3 8.9 %collective-permute-start.3 = (bf16[2,8,512]{2,1,0:T(8,128)(2,1)S(1)}, bf16[2,8,512]{2,1,0:T(8,128)(2,1)S(1)}, u32[]{:S(2)}, u32[]{:S(2)}) collective-permute-start(bf16[2,8,512]{2,1,0:T(8,128)(2,1)S(1)} %get-tuple-element.34), channel_id=1, source_target_pairs={{0,1},{1,2},{2,3},{3,4},{4,5},{5,6},{6,7},{7,8},{8,9},{9,10},{10,1... | collective-permute-start | bytes 49160 | tf_op jit(solution)/shard_map/ppermute | solution.py:481
  84.7 5.4 %collective-permute-start.4 = (bf16[2,8,512]{2,1,0:T(8,128)(2,1)S(1)}, bf16[2,8,512]{2,1,0:T(8,128)(2,1)S(1)}, u32[]{:S(2)}, u32[]{:S(2)}) collective-permute-start(bf16[2,8,512]{2,1,0:T(8,128)(2,1)S(1)} %get-tuple-element.35), channel_id=1, source_target_pairs={{1,0},{2,1},{3,2},{4,3},{5,4},{6,5},{7,6},{8,7},{9,8},{10,9},{11,1... | collective-permute-start | bytes 49160 | tf_op jit(solution)/shard_map/ppermute | solution.py:482
  93.7 34.8 %all-to-all-start.4 = ((bf16[32,16,128]{2,1,0:T(8,128)(2,1)}), bf16[32,16,128]{2,1,0:T(8,128)(2,1)S(1)}, u32[]{:S(2)}, u32[]{:S(2)}) async-start(bf16[32,16,128]{2,1,0:T(8,128)(2,1)} %shard_map.157), calls=%async_computation.4 | async-start | bytes 262144 | tf_op jit(solution)/shard_map/all_to_all | solution.py:497

commit v4 on v1

--- a/solution.py
+++ b/solution.py
@@ -20,17 +20,20 @@
 HD = 256
 LANES = 128
 PARTS = C // LANES
+ROWS = 64
 
 
 def params(mib):
     return pltpu.CompilerParams(vmem_limit_bytes=mib * 1024 * 1024)
 
 
-def call(kernel, outs, mib, flops=0, moved=0, scratch=(), smem=0):
+def call(kernel, outs, mib, flops=0, moved=0, scratch=(), smem=0, hbm=()):
     vmem = pl.BlockSpec(memory_space=pltpu.VMEM)
 
     def run(*args):
         specs = [pl.BlockSpec(memory_space=pltpu.SMEM)] * smem + [vmem] * (len(args) - smem)
+        for at in hbm:
+            specs[at] = pl.BlockSpec(memory_space=pltpu.HBM)
         return pl.pallas_call(
             kernel,
             out_shape=outs,
@@ -81,11 +84,40 @@
     return below, value, above
 
 
-def forward_kernel(lat, cot, left, right, taps, bias, out, edge_l, edge_r):
+def core_of(spot):
+    return spot[0] % 2
+
+
+def side_of(spot):
+    return (spot[0] // 2) % 2
+
+
+def to_partners(spot, first, last):
+    even = core_of(spot) == 0
+    return jnp.where(even, last, first), jnp.where(even, first, last)
+
+
+def from_partners(spot, other_core, other_chip):
+    even = core_of(spot) == 0
+    return jnp.where(even, other_chip, other_core), jnp.where(even, other_core, other_chip)
+
+
+def start_kernel(spot, lat, to_core, to_chip, edges):
     for s in range(SL):
-        shifted = row_shifts(silu(left[0, s].astype(F32)))
+        for h in range(H):
+            edges[0, s, h : h + 1, :] = lat[s, h, :PX, :].astype(F32)[:1]
+            edges[1, s, h : h + 1, :] = lat[s, h, PX:, :].astype(F32)[PX - 1 :]
+    one, two = to_partners(spot, edges[0], edges[1])
+    to_core[...] = one.astype(BF16)
+    to_chip[...] = two.astype(BF16)
+
+
+def forward_kernel(spot, lat, cot, other_core, other_chip, taps, bias, out, edge_l, edge_r):
+    for s in range(SL):
+        left, right = from_partners(spot, other_core[s].astype(F32), other_chip[s].astype(F32))
+        shifted = row_shifts(silu(left))
         edge_l[s] = sum(taps[3 * a : 3 * a + 1, :] * shifted[a] for a in range(3))
-        shifted = row_shifts(silu(right[0, s].astype(F32)))
+        shifted = row_shifts(silu(right))
         edge_r[s] = sum(taps[3 * a + 2 : 3 * a + 3, :] * shifted[a] for a in range(3))
     rows = row_index(WL)
 
@@ -127,9 +159,9 @@
 
 
 def attend_kernel(
-    recv, w_query, w_key, w_value, w_output, gain,
-    out, normed, stacked, attended, cot, gain_sum,
-    y_rows, inv_rows, qkv, gatt, gnorm,
+    predivide, spot, recv, w_query, w_key, w_value, w_output, gain,
+    out, halves, gain_sum,
+    normed, stacked, attended, cot, y_rows, inv_rows, qkv, gatt, gnorm,
 ):
     rows_each = GROUPS * 8
     scale = 1.0 / math.sqrt(DH)
@@ -201,7 +233,7 @@
     )
     total = jnp.zeros((8, C), F32)
     for tile in range(2):
-        halves = []
+        results = []
         for half in range(2):
             at = pl.ds((2 * tile + half) * rows_each, rows_each)
             y = y_rows[at, :]
@@ -211,33 +243,48 @@
             gained = grad * gain[...]
             mean = jnp.sum(gained * y, axis=-1, keepdims=True) * (1.0 / C)
             result = inverse * (gained - y * (mean * inverse * inverse))
-            halves.append(result.reshape(GROUPS, 8, C))
-        for s, whole in enumerate(pair_up(*halves)):
+            results.append(result.reshape(GROUPS, 8, C))
+        for s, whole in enumerate(pair_up(*results)):
             out[:, s, 8 * tile : 8 * tile + 8, :] = whole.astype(BF16)
     gain_sum[...] = jnp.sum(total, axis=0, keepdims=True)
 
-
-def weights_kernel(predivide, core, normed, stacked, attended, cot, out):
-    mine = core[0]
     for m in range(4):
         if m < 3:
             whole = tn(normed[...], stacked[:, m * HD : (m + 1) * HD])
         else:
             whole = tn(cot[...], attended[...])
-        tiles = (whole * predivide).reshape(16, 2, 2, 8, HD)
-        for which in range(2):
-            slot = (mine + which) % 2
-            for high in range(2):
-                for side in range(2):
-                    piece = tiles[:, which, high, :, side * LANES : (side + 1) * LANES]
-                    out[slot, 4 * m + 2 * high + side] = piece.reshape(LANES, LANES).astype(BF16)
-
-
-def taps_kernel(predivide, lat, left, right, cot, ret, gain_sum, kept, got, out, edge_l, edge_r, tiles):
+        tiles = (whole * predivide).reshape(8, 2, 2, 2, 8, HD)
+        for z in range(2):
+            for core in range(2):
+                away_core, away_z = (core_of(spot) + core) % 2, (side_of(spot) + z) % 2
+                for high in range(2):
+                    for side in range(2):
+                        piece = tiles[:, z, core, high, :, side * LANES : (side + 1) * LANES]
+                        halves[away_core, away_z, 4 * m + 2 * high + side] = piece.reshape(
+                            ROWS, LANES
+                        ).astype(BF16)
+
+
+def add_cores_kernel(kept, got, keep, send):
+    keep[...] = (kept[0, 0].astype(F32) + got[0].astype(F32)).astype(BF16)
+    send[...] = (kept[0, 1].astype(F32) + got[1].astype(F32)).astype(BF16)
+
+
+def add_chips_kernel(kept, got, out):
+    out[:, :ROWS, :] = (kept[...].astype(F32) + got[...].astype(F32)).astype(BF16)
+    out[:, ROWS:, :] = jnp.zeros((GROUPS, 16, LANES), BF16)
+
+
+def taps_kernel(
+    predivide, spot, lat, other_core, other_chip, cot, ret, gain_sum, sums_in,
+    out, edge_l, edge_r, tiles, packed, sem,
+):
+    del sums_in
     tiles[...] = jnp.zeros_like(tiles)
     for s in range(SL):
-        edge_l[s] = silu(left[0, s].astype(F32))
-        edge_r[s] = silu(right[0, s].astype(F32))
+        left, right = from_partners(spot, other_core[s].astype(F32), other_chip[s].astype(F32))
+        edge_l[s] = silu(left)
+        edge_r[s] = silu(right)
     rows = row_index(WL)
 
     @pl.loop(0, PARTS)
@@ -275,15 +322,36 @@
 
     whole = tiles[...] * predivide
     high = whole.astype(BF16).astype(F32)
-    out[:, LANES:, :] = jnp.concatenate([high, whole - high], axis=1).astype(BF16)
-    out[:, :LANES, :] = (kept[0].astype(F32) + got[...].astype(F32)).astype(BF16)
-
-
-def latents_kernel(lat, cot, ret, left, right, back_l, back_r, taps, out, edge_l, edge_r):
+    packed[...] = jnp.concatenate([high, whole - high], axis=1).astype(BF16)
+    copy = pltpu.make_async_copy(packed, out.at[:, pl.ds(ROWS, 16), :], sem)
+    copy.start()
+    copy.wait()
+
+
+def edges_kernel(spot, after, cot, ret, to_core, to_chip, edges):
+    del after
     for s in range(SL):
-        below, here, above = row_shifts(left[1, s].astype(F32) + back_l[s].astype(F32))
+        for h in range(H):
+            at = pl.ds(h, 1)
+            edges[0, 0, s, at, :] = cot[s, h, :PX, :].astype(F32)[:1]
+            edges[1, 0, s, at, :] = cot[s, h, PX:, :].astype(F32)[PX - 1 :]
+            edges[0, 1, s, at, :] = ret[2 * h, s].astype(F32)[:1]
+            edges[1, 1, s, at, :] = ret[2 * h + 1, s].astype(F32)[PX - 1 :]
+    one, two = to_partners(spot, edges[0], edges[1])
+    to_core[...] = one.astype(BF16)
+    to_chip[...] = two.astype(BF16)
+
+
+def latents_kernel(spot, lat, cot, ret, other_core, other_chip, taps, out, edge_l, edge_r):
+    for s in range(SL):
+        left, right = from_partners(
+            spot,
+            other_core[0, s].astype(F32) + other_core[1, s].astype(F32),
+            other_chip[0, s].astype(F32) + other_chip[1, s].astype(F32),
+        )
+        below, here, above = row_shifts(left)
         edge_l[s] = taps[2:3, :] * above + taps[5:6, :] * here + taps[8:9, :] * below
-        below, here, above = row_shifts(right[1, s].astype(F32) + back_r[s].astype(F32))
+        below, here, above = row_shifts(right)
         edge_r[s] = taps[0:1, :] * above + taps[3:4, :] * here + taps[6:7, :] * below
     rows = row_index(WL)
 
@@ -318,18 +386,21 @@
             out[s, h, :, here] = grads[h] + total * (sig * (1.0 + value * (1.0 - sig)))
 
 
-def second_kernel(core, recv, out):
+def second_kernel(spot, recv, out):
     total = jnp.sum(recv[...].astype(F32), axis=0)
-    weights = total[:LANES].reshape(16, 8, LANES)
-    taps = total[LANES : LANES + 8] + total[LANES + 8 :]
+    weights = total[:ROWS].reshape(8, 8, LANES)
+    taps = total[ROWS : ROWS + 8] + total[ROWS + 8 :]
     high = taps.astype(BF16).astype(F32)
     low = taps - high
     at = lax.broadcasted_iota(jnp.int32, (8, LANES), 0)
     both = jnp.where(at < 4, high, pltpu.roll(low, 4, 0))
-    for which in range(2):
-        own = jnp.where(core[0] == which, 1.0, 0.0)
-        for z in range(16):
-            out[2 * z + which] = jnp.concatenate([weights[z] * own, both], axis=0).astype(BF16)
+    for z in range(2):
+        for core in range(2):
+            own = jnp.where(jnp.logical_and(core_of(spot) == core, side_of(spot) == z), 1.0, 0.0)
+            for block in range(8):
+                out[4 * block + 2 * z + core] = jnp.concatenate(
+                    [weights[block] * own, both], axis=0
+                ).astype(BF16)
 
 
 def third_kernel(recv, out):
@@ -365,19 +436,27 @@
 ):
     strips = lax.axis_size("azim")
     groups = lax.axis_size("sweep")
-    up = [(i, (i + 1) % strips) for i in range(strips)]
-    down = [(j, i) for i, j in up]
-    pair = [(i, i ^ 1) for i in range(strips)]
-    core = (lax.axis_index("azim") % 2).astype(jnp.int32).reshape(1)
+    cores = [(i, i ^ 1) for i in range(strips)]
+    chips = [(i, (i + 1 if i % 2 else i - 1) % strips) for i in range(strips)]
+    sides = [(i, i ^ 2) for i in range(strips)]
+    strip = lax.axis_index("azim")
+    spot = strip.astype(jnp.int32).reshape(1)
     predivide = 1.0 / math.sqrt(SL * groups * H * WL * strips)
     bias_row = conv_bias.reshape(1, C)
     gain_row = norm_gain.reshape(1, C)
     edge = pltpu.VMEM((SL, H, C), F32)
 
-    last = jnp.stack([latents[:, :, WL - 1, :], cotangent[:, :, WL - 1, :]])
-    first = jnp.stack([latents[:, :, 0, :], cotangent[:, :, 0, :]])
-    left = lax.ppermute(last, "azim", up)
-    right = lax.ppermute(first, "azim", down)
+    one_edge = struct((SL, H, C), BF16)
+    to_core, to_chip = call(
+        start_kernel,
+        (one_edge, one_edge),
+        16,
+        moved=600_000,
+        smem=1,
+        scratch=[pltpu.VMEM((2, SL, H, C), F32)],
+    )(spot, latents)
+    other_chip = lax.ppermute(to_chip, "azim", chips)
+    other_core = lax.ppermute(to_core, "azim", cores)
 
     sent = call(
         forward_kernel,
@@ -385,58 +464,79 @@
         16,
         flops=10_000_000,
         moved=2_000_000,
+        smem=1,
         scratch=[edge, edge],
-    )(latents, cotangent, left, right, conv_kernel, bias_row)
+    )(spot, latents, cotangent, other_core, other_chip, conv_kernel, bias_row)
     recv = lax.all_to_all(sent, "sweep", split_axis=0, concat_axis=0, tiled=True)
 
     rows = GROUPS * SL * PX
-    grad_attn, normed, stacked, attended, cot_rows, gain_sum = call(
-        attend_kernel,
+    grad_attn, halves, gain_sum = call(
+        functools.partial(attend_kernel, predivide),
         (
             struct((GROUPS, SL, PX, C), BF16),
-            struct((rows, C), BF16),
-            struct((rows, 3 * HD), BF16),
-            struct((rows, HD), BF16),
-            struct((rows, C), BF16),
+            struct((2, 2, GROUPS, ROWS, LANES), BF16),
             struct((1, C), F32),
         ),
         32,
         flops=2_000_000_000,
         moved=6_000_000,
+        smem=1,
         scratch=[
+            pltpu.VMEM((rows, C), BF16),
+            pltpu.VMEM((rows, 3 * HD), BF16),
+            pltpu.VMEM((rows, HD), BF16),
+            pltpu.VMEM((rows, C), BF16),
             pltpu.VMEM((rows, C), F32),
             pltpu.VMEM((rows, LANES), F32),
             pltpu.VMEM((rows, 3 * HD), BF16),
             pltpu.VMEM((rows, HD), BF16),
             pltpu.VMEM((rows, C), F32),
         ],
-    )(recv, w_query, w_key, w_value, w_output, gain_row)
+    )(spot, recv, w_query, w_key, w_value, w_output, gain_row)
     ret = lax.all_to_all(grad_attn, "sweep", split_axis=0, concat_axis=0, tiled=True)
-
-    halves = call(
-        functools.partial(weights_kernel, predivide),
-        struct((2, GROUPS, LANES, LANES), BF16),
-        24,
-        flops=600_000_000,
-        moved=4_000_000,
+    from_core = lax.ppermute(halves[1], "azim", cores)
+    piece = struct((GROUPS, ROWS, LANES), BF16)
+    keep, send = call(add_cores_kernel, (piece, piece), 16, moved=2_000_000)(halves, from_core)
+    from_chip = lax.ppermute(send, "azim", sides)
+    payload = struct((GROUPS, ROWS + 16, LANES), BF16)
+    sums = call(add_chips_kernel, payload, 16, moved=1_000_000)(keep, from_chip)
+
+    vmem = pl.BlockSpec(memory_space=pltpu.VMEM)
+    anywhere = pl.BlockSpec(memory_space=pltpu.HBM)
+    first_sent = pl.pallas_call(
+        functools.partial(taps_kernel, predivide),
+        out_shape=payload,
+        in_specs=[pl.BlockSpec(memory_space=pltpu.SMEM)] + [vmem] * 6 + [anywhere],
+        out_specs=anywhere,
+        input_output_aliases={7: 0},
+        scratch_shapes=[
+            edge,
+            edge,
+            pltpu.VMEM((GROUPS, 8, LANES), F32),
+            pltpu.VMEM((GROUPS, 16, LANES), BF16),
+            pltpu.SemaphoreType.DMA,
+        ],
+        compiler_params=params(16),
+        cost_estimate=pl.CostEstimate(
+            flops=10_000_000, bytes_accessed=2_000_000, transcendentals=0
+        ),
+    )(spot, latents, other_core, other_chip, cotangent, ret, gain_sum, sums)
+    first_recv = lax.all_to_all(first_sent, "sweep", split_axis=0, concat_axis=0, tiled=True)
+    both_edges = struct((2, SL, H, C), BF16)
+    back_core, back_chip = call(
+        edges_kernel,
+        (both_edges, both_edges),
+        16,
+        moved=100_000,
         smem=1,
-    )(core, normed, stacked, attended, cot_rows)
-    got = lax.ppermute(halves[1], "azim", pair)
-
-    back_last = ret[1::2, :, PX - 1, :].transpose(1, 0, 2)
-    back_first = ret[0::2, :, 0, :].transpose(1, 0, 2)
-    back_l = lax.ppermute(back_last, "azim", up)
-    back_r = lax.ppermute(back_first, "azim", down)
-
-    first_sent = call(
-        functools.partial(taps_kernel, predivide),
-        struct((GROUPS, LANES + 16, LANES), BF16),
-        16,
-        flops=10_000_000,
-        moved=3_000_000,
-        scratch=[edge, edge, pltpu.VMEM((GROUPS, 8, LANES), F32)],
-    )(latents, left, right, cotangent, ret, gain_sum, halves, got)
-    first_recv = lax.all_to_all(first_sent, "sweep", split_axis=0, concat_axis=0, tiled=True)
+        hbm=(1,),
+        scratch=[pltpu.VMEM((2, 2, SL, H, C), F32)],
+    )(spot, first_sent, cotangent, ret)
+    back_chip = lax.ppermute(back_chip, "azim", chips)
+    back_core = lax.ppermute(back_core, "azim", cores)
+    first_recv, back_chip, back_core = lax.optimization_barrier(
+        (first_recv, back_chip, back_core)
+    )
 
     grad_latents = call(
         latents_kernel,
@@ -444,13 +544,15 @@
         16,
         flops=10_000_000,
         moved=4_000_000,
+        smem=1,
         scratch=[edge, edge],
-    )(latents, cotangent, ret, left, right, back_l, back_r, conv_kernel)
+    )(spot, latents, cotangent, ret, back_core, back_chip, conv_kernel)
 
     second_sent = call(
         second_kernel, struct((strips, 16, LANES), BF16), 16, moved=1_000_000, smem=1
-    )(core, first_recv)
+    )(spot, first_recv)
     second_recv = lax.all_to_all(second_sent, "azim", split_axis=0, concat_axis=0, tiled=True)
+    second_recv, grad_latents = lax.optimization_barrier((second_recv, grad_latents))
     third_sent = call(third_kernel, struct((GROUPS, 16, LANES), F32), 16, moved=300_000)(
         second_recv
     )

time: 148 us -> 136 us (0.919)
  the two profiles are of different devices: /device:TPU:2 before, /device:TPU:1 now
where the time goes in v4:
time: 136 us; the launch traced here: 135 us
  starting transfers between devices  57.9 us (43%)
  blocking collectives  38.4 us (28%)
  waiting for transfers between devices  21.3 us (16%)
  Pallas kernels  14.9 us (11%)
  local copies, waits for them, and re-layouts  1.94 us (1%)
    all_to_all x1, blocking collectives, on_device(): lax.all_to_all(sent, 'sweep', split_axis=0, concat_axis=0, tiled=True)  25.8 us
    pallas_call x10, Pallas kernels, run(): pl.pallas_call(kernel, out_shape=outs, in_specs=specs, out_specs=jax.tree...  12.9 us
    all_to_all x1, blocking collectives, on_device(): lax.all_to_all(third_sent, 'sweep', split_axis=0, concat_axis=0, tiled=True)  12.5 us
    all_to_all x1, starting transfers between devices, on_device(): lax.all_to_all(second_sent, 'azim', split_axis=0, concat_axis=0, tiled=True)  10.6 us
    ppermute x1, starting transfers between devices, on_device(): back_core = lax.ppermute(back_core, 'azim', cores)  10.3 us
    all_to_all x1, waiting for transfers between devices, on_device(): lax.all_to_all(second_sent, 'azim', split_axis=0, concat_axis=0, tiled=True)  9.72 us
    ppermute x1, starting transfers between devices, on_device(): other_core = lax.ppermute(to_core, 'azim', cores)  8.79 us
    all_to_all x1, starting transfers between devices, on_device(): lax.all_to_all(first_sent, 'sweep', split_axis=0, concat_axis=0, tiled=True)  7.18 us
  transfers between devices with their start and end apart: 9, of which 5 were waited for; matrix products, arithmetic and copies ran while one was open for 0% of the time, Pallas kernels for 2%

profile of v4, /device:TPU:1, one launch (start us, length us, event | category | flops | bytes accessed | tf_op | source)
XLA Modules:
  0.0 135.3 jit_solution(16772121444316548386)
XLA Ops:
  0.6 0.0 copy-start.1
  0.7 1.1 copy-done.1
  1.7 0.1 shard_map.152
  1.8 8.8 %collective-permute-start = (bf16[2,8,512]{2,1,0:T(8,128)(2,1)S(1)}, bf16[2,8,512]{2,1,0:T(8,128)(2,1)S(1)}, u32[]{:S(2)}, u32[]{:S(2)}) collective-permute-start(bf16[2,8,512]{2,1,0:T(8,128)(2,1)S(1)} %get-tuple-element.29), channel_id=1, source_target_pairs={{0,1},{1,0},{2,3},{3,2},{4,5},{5,4},{6,7},{7,6},{8,9},{9,8},{10,11... | collective-permute-start | bytes 49160 | tf_op jit(solution)/shard_map/ppermute | solution.py:459
  10.6 1.9 %collective-permute-start.1 = (bf16[2,8,512]{2,1,0:T(8,128)(2,1)S(1)}, bf16[2,8,512]{2,1,0:T(8,128)(2,1)S(1)}, u32[]{:S(2)}, u32[]{:S(2)}) collective-permute-start(bf16[2,8,512]{2,1,0:T(8,128)(2,1)S(1)} %get-tuple-element.30), channel_id=1, source_target_pairs={{0,31},{1,2},{2,1},{3,4},{4,3},{5,6},{6,5},{7,8},{8,7},{9,10},{10,... | collective-permute-start | bytes 49160 | tf_op jit(solution)/shard_map/ppermute | solution.py:458
  12.6 3.1 %collective-permute-done.1.other_chip = bf16[2,8,512]{2,1,0:T(8,128)(2,1)S(1)} collective-permute-done((bf16[2,8,512]{2,1,0:T(8,128)(2,1)S(1)}, bf16[2,8,512]{2,1,0:T(8,128)(2,1)S(1)}, u32[]{:S(2)}, u32[]{:S(2)}) %collective-permute-start.1) | collective-permute-done | bytes 16416 | tf_op jit(solution)/shard_map/ppermute | solution.py:458
  15.7 0.8 copy-done.3
  16.4 1.2 shard_map.153
  17.7 0.0 copy-start.6
  17.7 0.0 copy-start.9
  17.7 0.0 copy-start.10
  17.7 25.8 %all_to_all.25.recv = bf16[16,2,2,16,512]{4,3,2,1,0:T(8,128)(2,1)S(1)} all-to-all(bf16[16,2,2,16,512]{4,3,2,1,0:T(8,128)(2,1)S(1)} %shard_map.153), channel_id=1, replica_groups=mesh['sweep'=16,'azim'=32] {'sweep'}, dimensions={0} | all-to-all | bytes 2097152 | tf_op jit(solution)/shard_map/all_to_all | solution.py:470
  43.6 6.9 %shard_map.154 = (bf16[16,2,16,512]{3,2,1,0:T(8,128)(2,1)}, bf16[2,2,16,64,128]{4,3,2,1,0:T(8,128)(2,1)S(1)}, f32[1,512]{1,0:T(1,128)S(1)}) custom-call(s32[1]{0:T(128)} %bitcast.spot, bf16[16,2,2,16,512]{4,3,2,1,0:T(8,128)(2,1)S(1)} %all_to_all.25.recv, bf16[512,256]{1,0:T(8,128)(2,1)S(1)} %copy-done.6, bf16[512,256]{1,0:T(8,128)(2,1)S(1)} %copy-done.7, ...), custom_call_target="tpu_custom_call" | custom-call | flops 2000000000 | bytes 6000000 | tf_op jit(solution)/shard_map/pallas_call | solution.py:37
  50.4 4.2 %all-to-all-start.1 = ((bf16[16,2,16,512]{3,2,1,0:T(8,128)(2,1)}), bf16[16,2,16,512]{3,2,1,0:T(8,128)(2,1)S(1)}, u32[]{:S(2)}, u32[]{:S(2)}) async-start(bf16[16,2,16,512]{3,2,1,0:T(8,128)(2,1)} %get-tuple-element.31), calls=%async_computation.1 | async-start | bytes 1048576 | tf_op jit(solution)/shard_map/all_to_all | solution.py:496
  54.7 6.8 %collective-permute-start.2 = (bf16[2,16,64,128]{3,2,1,0:T(8,128)(2,1)S(1)}, bf16[2,16,64,128]{3,2,1,0:T(8,128)(2,1)S(1)}, u32[]{:S(2)}, u32[]{:S(2)}) collective-permute-start(bf16[2,16,64,128]{3,2,1,0:T(8,128)(2,1)S(1)} %slice_bitcast_fusion), channel_id=1, source_target_pairs={{0,1},{1,0},{2,3},{3,2},{4,5},{5,4},{6,7},{7,6},{8,9},{9,8},{10,11... | collective-permute-start | bytes 1572872 | tf_op jit(solution)/shard_map/ppermute | solution.py:497
  61.6 1.5 %collective-permute-done.2.got = bf16[2,16,64,128]{3,2,1,0:T(8,128)(2,1)S(1)} collective-permute-done((bf16[2,16,64,128]{3,2,1,0:T(8,128)(2,1)S(1)}, bf16[2,16,64,128]{3,2,1,0:T(8,128)(2,1)S(1)}, u32[]{:S(2)}, u32[]{:S(2)}) %collective-permute-start.2) | collective-permute-done | bytes 524320 | tf_op jit(solution)/shard_map/ppermute | solution.py:497
  63.1 0.1 shard_map.155
  63.2 3.4 %collective-permute-start.3 = (bf16[16,64,128]{2,1,0:T(8,128)(2,1)S(1)}, bf16[16,64,128]{2,1,0:T(8,128)(2,1)S(1)}, u32[]{:S(2)}, u32[]{:S(2)}) collective-permute-start(bf16[16,64,128]{2,1,0:T(8,128)(2,1)S(1)} %get-tuple-element.35), channel_id=1, source_target_pairs={{0,2},{1,3},{2,0},{3,1},{4,6},{5,7},{6,4},{7,5},{8,10},{9,11},{10,... | collective-permute-start | bytes 786440 | tf_op jit(solution)/shard_map/ppermute | solution.py:500
  66.7 6.1 %collective-permute-done.3.got = bf16[16,64,128]{2,1,0:T(8,128)(2,1)S(1)} collective-permute-done((bf16[16,64,128]{2,1,0:T(8,128)(2,1)S(1)}, bf16[16,64,128]{2,1,0:T(8,128)(2,1)S(1)}, u32[]{:S(2)}, u32[]{:S(2)}) %collective-permute-start.3) | collective-permute-done | bytes 262176 | tf_op jit(solution)/shard_map/ppermute | solution.py:500
  72.8 0.8 shard_map.156.sums_in
  73.6 2.0 %shard_map.157.after = bf16[16,80,128]{2,1,0:T(8,128)(2,1)} custom-call(s32[1]{0:T(128)} %bitcast.spot, bf16[2,8,32,512]{3,2,1,0:T(8,128)(2,1)S(1)} %copy-done.2, bf16[2,8,512]{2,1,0:T(8,128)(2,1)S(1)} %collective-permute-done.other_core, bf16[2,8,512]{2,1,0:T(8,128)(2,1)S(1)} %collective-permute-done.1.other_chip, ...), custom_call_target="tpu_custom_call", output_to_operand_aliasing={{}: (7, {})} | custom-call | flops 10000000 | bytes 2000000 | tf_op jit(solution)/shard_map/pallas_call | solution.py:506
  75.6 7.2 %all-to-all-start.2 = ((bf16[16,80,128]{2,1,0:T(8,128)(2,1)}), bf16[16,80,128]{2,1,0:T(8,128)(2,1)S(1)}, u32[]{:S(2)}, u32[]{:S(2)}) async-start(bf16[16,80,128]{2,1,0:T(8,128)(2,1)} %shard_map.157.after), calls=%async_computation.2 | async-start | bytes 655360 | tf_op jit(solution)/shard_map/all_to_all | solution.py:524
  82.7 0.1 shard_map.158
  82.9 4.6 %collective-permute-start.4 = (bf16[2,2,8,512]{3,2,1,0:T(8,128)(2,1)S(1)}, bf16[2,2,8,512]{3,2,1,0:T(8,128)(2,1)S(1)}, u32[]{:S(2)}, u32[]{:S(2)}) collective-permute-start(bf16[2,2,8,512]{3,2,1,0:T(8,128)(2,1)S(1)} %get-tuple-element.36), channel_id=1, source_target_pairs={{0,31},{1,2},{2,1},{3,4},{4,3},{5,6},{6,5},{7,8},{8,7},{9,10},{10,... | collective-permute-start | bytes 98312 | tf_op jit(solution)/shard_map/ppermute | solution.py:535
  87.5 10.3 %collective-permute-start.5 = (bf16[2,2,8,512]{3,2,1,0:T(8,128)(2,1)S(1)}, bf16[2,2,8,512]{3,2,1,0:T(8,128)(2,1)S(1)}, u32[]{:S(2)}, u32[]{:S(2)}) collective-permute-start(bf16[2,2,8,512]{3,2,1,0:T(8,128)(2,1)S(1)} %get-tuple-element.37), channel_id=1, source_target_pairs={{0,1},{1,0},{2,3},{3,2},{4,5},{5,4},{6,7},{7,6},{8,9},{9,8},{10,11... | collective-permute-start | bytes 98312 | tf_op jit(solution)/shard_map/ppermute | solution.py:536
  97.8 0.8 collective-permute-done.5.other_core
  98.6 0.7 shard_map.159
  99.3 10.6 %all-to-all-start.3 = ((bf16[32,16,128]{2,1,0:T(8,128)(2,1)}), bf16[32,16,128]{2,1,0:T(8,128)(2,1)S(1)}, u32[]{:S(2)}, u32[]{:S(2)}) async-start(bf16[32,16,128]{2,1,0:T(8,128)(2,1)} %shard_map.159), calls=%async_computation.3 | async-start | bytes 262144 | tf_op jit(solution)/shard_map/all_to_all | solution.py:554
  110.0 2.4 %shard_map.160 = f32[2,8,32,512]{3,2,1,0:T(8,128)} custom-call(s32[1]{0:T(128)} %bitcast.spot, bf16[2,8,32,512]{3,2,1,0:T(8,128)(2,1)S(1)} %copy-done.2, bf16[2,8,32,512]{3,2,1,0:T(8,128)(2,1)S(1)} %copy-done, bf16[16,2,16,512]{3,2,1,0:T(8,128)(2,1)S(1)} %all-to-all-done.1.ret, bf16[2,2,8,512]{3,2,1,0:T(8,128)(2,1)S(1)} %collective-permute-done.5.other_core, ...), custom_call_target="tpu_custom_call" | custom-call | flops 10000000 | bytes 4000000 | tf_op jit(solution)/shard_map/pallas_call | solution.py:37
  112.3 9.7 %all-to-all-done.3.recv = bf16[32,16,128]{2,1,0:T(8,128)(2,1)S(1)} async-done(((bf16[32,16,128]{2,1,0:T(8,128)(2,1)}), bf16[32,16,128]{2,1,0:T(8,128)(2,1)S(1)}, u32[]{:S(2)}, u32[]{:S(2)}) %all-to-all-start.3) | async-done | bytes 131104 | tf_op jit(solution)/shard_map/all_to_all | solution.py:554
  122.1 12.5 %all_to_all.26.recv = f32[16,16,128]{2,1,0:T(8,128)S(1)} all-to-all(f32[16,16,128]{2,1,0:T(8,128)S(1)} %shard_map.161), channel_id=1, replica_groups=mesh['sweep'=16,'azim'=32] {'sweep'}, dimensions={0} | all-to-all | bytes 262144 | tf_op jit(solution)/shard_map/all_to_all | solution.py:559
  134.6 0.7 shard_map.162
  (22 shorter events, 0.1 us)
Async XLA Ops:
  0.6 15.0 %copy-start = (bf16[2,8,32,512]{3,2,1,0:T(8,128)(2,1)S(1)}, bf16[2,8,32,512]{3,2,1,0:T(8,128)(2,1)}, u32[]{:S(2)}) copy-start(bf16[2,8,32,512]{3,2,1,0:T(8,128)(2,1)} %cot.7) | copy-start | bytes 1572868
  0.6 1.1 copy-start.1
  1.8 13.9 %copy-start.5 = (f32[512]{0:T(512)S(1)}, f32[512]{0:T(512)}, u32[]{:S(2)}) copy-start(f32[512]{0:T(512)} %param.12) | copy-start | bytes 6148
  1.8 10.7 %collective-permute-start = (bf16[2,8,512]{2,1,0:T(8,128)(2,1)S(1)}, bf16[2,8,512]{2,1,0:T(8,128)(2,1)S(1)}, u32[]{:S(2)}, u32[]{:S(2)}) collective-permute-start(bf16[2,8,512]{2,1,0:T(8,128)(2,1)S(1)} %get-tuple-element.29), channel_id=1, source_target_pairs={{0,1},{1,0},{2,3},{3,2},{4,5},{5,4},{6,7},{7,6},{8,9},{9,8},{10,11... | collective-permute-start | bytes 49160 | tf_op jit(solution)/shard_map/ppermute | solution.py:459
  10.6 5.1 %collective-permute-start.1 = (bf16[2,8,512]{2,1,0:T(8,128)(2,1)S(1)}, bf16[2,8,512]{2,1,0:T(8,128)(2,1)S(1)}, u32[]{:S(2)}, u32[]{:S(2)}) collective-permute-start(bf16[2,8,512]{2,1,0:T(8,128)(2,1)S(1)} %get-tuple-element.30), channel_id=1, source_target_pairs={{0,31},{1,2},{2,1},{3,4},{4,3},{5,6},{6,5},{7,8},{8,7},{9,10},{10,... | collective-permute-start | bytes 49160 | tf_op jit(solution)/shard_map/ppermute | solution.py:458
  15.7 0.8 copy-start.3
  17.7 25.9 %copy-start.6 = (bf16[512,256]{1,0:T(8,128)(2,1)S(1)}, bf16[512,256]{1,0:T(8,128)(2,1)}, u32[]{:S(2)}) copy-start(bf16[512,256]{1,0:T(8,128)(2,1)} %w_query.1) | copy-start | bytes 786436
  17.7 25.9 %copy-start.7 = (bf16[512,256]{1,0:T(8,128)(2,1)S(1)}, bf16[512,256]{1,0:T(8,128)(2,1)}, u32[]{:S(2)}) copy-start(bf16[512,256]{1,0:T(8,128)(2,1)} %w_key.1) | copy-start | bytes 786436
  17.7 25.9 %copy-start.8 = (bf16[512,256]{1,0:T(8,128)(2,1)S(1)}, bf16[512,256]{1,0:T(8,128)(2,1)}, u32[]{:S(2)}) copy-start(bf16[512,256]{1,0:T(8,128)(2,1)} %w_value.1) | copy-start | bytes 786436
  17.7 25.9 %copy-start.9 = (bf16[512,256]{1,0:T(8,128)(2,1)S(1)}, bf16[512,256]{1,0:T(8,128)(2,1)}, u32[]{:S(2)}) copy-start(bf16[512,256]{1,0:T(8,128)(2,1)} %w_output.1) | copy-start | bytes 786436
  17.7 25.9 %copy-start.10 = (f32[512]{0:T(512)S(1)}, f32[512]{0:T(512)}, u32[]{:S(2)}) copy-start(f32[512]{0:T(512)} %param.13) | copy-start | bytes 6148
  50.4 23.1 %all-to-all-start.1 = ((bf16[16,2,16,512]{3,2,1,0:T(8,128)(2,1)}), bf16[16,2,16,512]{3,2,1,0:T(8,128)(2,1)S(1)}, u32[]{:S(2)}, u32[]{:S(2)}) async-start(bf16[16,2,16,512]{3,2,1,0:T(8,128)(2,1)} %get-tuple-element.31), calls=%async_computation.1 | async-start | bytes 1048576 | tf_op jit(solution)/shard_map/all_to_all | solution.py:496
  54.7 8.4 %collective-permute-start.2 = (bf16[2,16,64,128]{3,2,1,0:T(8,128)(2,1)S(1)}, bf16[2,16,64,128]{3,2,1,0:T(8,128)(2,1)S(1)}, u32[]{:S(2)}, u32[]{:S(2)}) collective-permute-start(bf16[2,16,64,128]{3,2,1,0:T(8,128)(2,1)S(1)} %slice_bitcast_fusion), channel_id=1, source_target_pairs={{0,1},{1,0},{2,3},{3,2},{4,5},{5,4},{6,7},{7,6},{8,9},{9,8},{10,11... | collective-permute-start | bytes 1572872 | tf_op jit(solution)/shard_map/ppermute | solution.py:497
  63.2 10.4 %copy-start.2 = (bf16[2,8,32,512]{3,2,1,0:T(8,128)(2,1)S(1)}, bf16[2,8,32,512]{3,2,1,0:T(8,128)(2,1)}, u32[]{:S(2)}) copy-start(bf16[2,8,32,512]{3,2,1,0:T(8,128)(2,1)} %lat.7) | copy-start | bytes 1572868
  63.2 9.5 %collective-permute-start.3 = (bf16[16,64,128]{2,1,0:T(8,128)(2,1)S(1)}, bf16[16,64,128]{2,1,0:T(8,128)(2,1)S(1)}, u32[]{:S(2)}, u32[]{:S(2)}) collective-permute-start(bf16[16,64,128]{2,1,0:T(8,128)(2,1)S(1)} %get-tuple-element.35), channel_id=1, source_target_pairs={{0,2},{1,3},{2,0},{3,1},{4,6},{5,7},{6,4},{7,5},{8,10},{9,11},{10,... | collective-permute-start | bytes 786440 | tf_op jit(solution)/shard_map/ppermute | solution.py:500
  75.6 23.1 %all-to-all-start.2 = ((bf16[16,80,128]{2,1,0:T(8,128)(2,1)}), bf16[16,80,128]{2,1,0:T(8,128)(2,1)S(1)}, u32[]{:S(2)}, u32[]{:S(2)}) async-start(bf16[16,80,128]{2,1,0:T(8,128)(2,1)} %shard_map.157.after), calls=%async_computation.2 | async-start | bytes 655360 | tf_op jit(solution)/shard_map/all_to_all | solution.py:524
  82.9 14.9 %collective-permute-start.4 = (bf16[2,2,8,512]{3,2,1,0:T(8,128)(2,1)S(1)}, bf16[2,2,8,512]{3,2,1,0:T(8,128)(2,1)S(1)}, u32[]{:S(2)}, u32[]{:S(2)}) collective-permute-start(bf16[2,2,8,512]{3,2,1,0:T(8,128)(2,1)S(1)} %get-tuple-element.36), channel_id=1, source_target_pairs={{0,31},{1,2},{2,1},{3,4},{4,3},{5,6},{6,5},{7,8},{8,7},{9,10},{10,... | collective-permute-start | bytes 98312 | tf_op jit(solution)/shard_map/ppermute | solution.py:535
  87.5 11.1 %collective-permute-start.5 = (bf16[2,2,8,512]{3,2,1,0:T(8,128)(2,1)S(1)}, bf16[2,2,8,512]{3,2,1,0:T(8,128)(2,1)S(1)}, u32[]{:S(2)}, u32[]{:S(2)}) collective-permute-start(bf16[2,2,8,512]{3,2,1,0:T(8,128)(2,1)S(1)} %get-tuple-element.37), channel_id=1, source_target_pairs={{0,1},{1,0},{2,3},{3,2},{4,5},{5,4},{6,7},{7,6},{8,9},{9,8},{10,11... | collective-permute-start | bytes 98312 | tf_op jit(solution)/shard_map/ppermute | solution.py:536
  99.3 10.6 %copy-start.4 = (f32[9,512]{1,0:T(8,128)S(1)}, f32[9,512]{1,0:T(8,128)}, u32[]{:S(2)}) copy-start(f32[9,512]{1,0:T(8,128)} %taps.3) | copy-start | bytes 55300
  99.3 22.7 %all-to-all-start.3 = ((bf16[32,16,128]{2,1,0:T(8,128)(2,1)}), bf16[32,16,128]{2,1,0:T(8,128)(2,1)S(1)}, u32[]{:S(2)}, u32[]{:S(2)}) async-start(bf16[32,16,128]{2,1,0:T(8,128)(2,1)} %shard_map.159), calls=%async_computation.3 | async-start | bytes 262144 | tf_op jit(solution)/shard_map/all_to_all | solution.py:554

commit v5 on v4

--- a/solution.py
+++ b/solution.py
@@ -92,9 +92,9 @@
     return (spot[0] // 2) % 2
 
 
-def to_partners(spot, first, last):
+def partner_column(spot, for_core, first, last):
     even = core_of(spot) == 0
-    return jnp.where(even, last, first), jnp.where(even, first, last)
+    return jnp.where(even, last, first) if for_core else jnp.where(even, first, last)
 
 
 def from_partners(spot, other_core, other_chip):
@@ -102,17 +102,28 @@
     return jnp.where(even, other_chip, other_core), jnp.where(even, other_core, other_chip)
 
 
-def start_kernel(spot, lat, to_core, to_chip, edges):
+def edge_columns(lat, edges):
     for s in range(SL):
         for h in range(H):
             edges[0, s, h : h + 1, :] = lat[s, h, :PX, :].astype(F32)[:1]
             edges[1, s, h : h + 1, :] = lat[s, h, PX:, :].astype(F32)[PX - 1 :]
-    one, two = to_partners(spot, edges[0], edges[1])
-    to_core[...] = one.astype(BF16)
-    to_chip[...] = two.astype(BF16)
-
-
-def forward_kernel(spot, lat, cot, other_core, other_chip, taps, bias, out, edge_l, edge_r):
+
+
+def chip_edge_kernel(spot, lat, out, edges):
+    edge_columns(lat, edges)
+    out[...] = partner_column(spot, False, edges[0], edges[1]).astype(BF16)
+
+
+def core_edge_kernel(spot, after, lat, taps, bias, out, table, edges):
+    del after
+    edge_columns(lat, edges)
+    out[...] = partner_column(spot, True, edges[0], edges[1]).astype(BF16)
+    table[:9, :] = taps[...]
+    table[9:10, :] = bias[...]
+    table[10:, :] = jnp.zeros((6, C), F32)
+
+
+def forward_kernel(spot, lat, cot, other_core, other_chip, taps, out, edge_l, edge_r):
     for s in range(SL):
         left, right = from_partners(spot, other_core[s].astype(F32), other_chip[s].astype(F32))
         shifted = row_shifts(silu(left))
@@ -126,7 +137,7 @@
         s = step // PARTS
         here = lanes_of(step % PARTS)
         tap = [taps[t : t + 1, here] for t in range(9)]
-        base = bias[:, here]
+        base = taps[9:10, here]
         values = [lat[s, h, :, here].astype(F32) for h in range(H)]
         acts = [silu(v) for v in values]
         for h in range(H):
@@ -328,7 +339,7 @@
     copy.wait()
 
 
-def edges_kernel(spot, after, cot, ret, to_core, to_chip, edges):
+def back_edges_kernel(for_core, spot, after, cot, ret, out, edges):
     del after
     for s in range(SL):
         for h in range(H):
@@ -337,12 +348,11 @@
             edges[1, 0, s, at, :] = cot[s, h, PX:, :].astype(F32)[PX - 1 :]
             edges[0, 1, s, at, :] = ret[2 * h, s].astype(F32)[:1]
             edges[1, 1, s, at, :] = ret[2 * h + 1, s].astype(F32)[PX - 1 :]
-    one, two = to_partners(spot, edges[0], edges[1])
-    to_core[...] = one.astype(BF16)
-    to_chip[...] = two.astype(BF16)
-
-
-def latents_kernel(spot, lat, cot, ret, other_core, other_chip, taps, out, edge_l, edge_r):
+    out[...] = partner_column(spot, for_core, edges[0], edges[1]).astype(BF16)
+
+
+def latents_kernel(spot, after, lat, cot, ret, other_core, other_chip, taps, out, edge_l, edge_r):
+    del after
     for s in range(SL):
         left, right = from_partners(
             spot,
@@ -447,15 +457,20 @@
     edge = pltpu.VMEM((SL, H, C), F32)
 
     one_edge = struct((SL, H, C), BF16)
-    to_core, to_chip = call(
-        start_kernel,
-        (one_edge, one_edge),
+    column = [pltpu.VMEM((2, SL, H, C), F32)]
+    to_chip = call(chip_edge_kernel, one_edge, 16, moved=600_000, smem=1, scratch=column)(
+        spot, latents
+    )
+    other_chip = lax.ppermute(to_chip, "azim", chips)
+    to_core, table = call(
+        core_edge_kernel,
+        (one_edge, struct((16, C), F32)),
         16,
         moved=600_000,
         smem=1,
-        scratch=[pltpu.VMEM((2, SL, H, C), F32)],
-    )(spot, latents)
-    other_chip = lax.ppermute(to_chip, "azim", chips)
+        hbm=(1,),
+        scratch=column,
+    )(spot, to_chip, latents, conv_kernel, bias_row)
     other_core = lax.ppermute(to_core, "azim", cores)
 
     sent = call(
@@ -466,7 +481,7 @@
         moved=2_000_000,
         smem=1,
         scratch=[edge, edge],
-    )(spot, latents, cotangent, other_core, other_chip, conv_kernel, bias_row)
+    )(spot, latents, cotangent, other_core, other_chip, table)
     recv = lax.all_to_all(sent, "sweep", split_axis=0, concat_axis=0, tiled=True)
 
     rows = GROUPS * SL * PX
@@ -523,20 +538,25 @@
     )(spot, latents, other_core, other_chip, cotangent, ret, gain_sum, sums)
     first_recv = lax.all_to_all(first_sent, "sweep", split_axis=0, concat_axis=0, tiled=True)
     both_edges = struct((2, SL, H, C), BF16)
-    back_core, back_chip = call(
-        edges_kernel,
-        (both_edges, both_edges),
-        16,
-        moved=100_000,
-        smem=1,
-        hbm=(1,),
-        scratch=[pltpu.VMEM((2, 2, SL, H, C), F32)],
-    )(spot, first_sent, cotangent, ret)
-    back_chip = lax.ppermute(back_chip, "azim", chips)
-    back_core = lax.ppermute(back_core, "azim", cores)
-    first_recv, back_chip, back_core = lax.optimization_barrier(
-        (first_recv, back_chip, back_core)
-    )
+    second_sent = call(
+        second_kernel, struct((strips, 16, LANES), BF16), 16, moved=1_000_000, smem=1
+    )(spot, first_recv)
+    second_recv = lax.all_to_all(second_sent, "azim", split_axis=0, concat_axis=0, tiled=True)
+
+    def back_edges(for_core, after):
+        return call(
+            functools.partial(back_edges_kernel, for_core),
+            both_edges,
+            16,
+            moved=100_000,
+            smem=1,
+            hbm=(1,),
+            scratch=[pltpu.VMEM((2, 2, SL, H, C), F32)],
+        )(spot, after, cotangent, ret)
+
+    to_chip = back_edges(False, second_sent)
+    back_chip = lax.ppermute(to_chip, "azim", chips)
+    back_core = lax.ppermute(back_edges(True, to_chip), "azim", cores)
 
     grad_latents = call(
         latents_kernel,
@@ -545,13 +565,10 @@
         flops=10_000_000,
         moved=4_000_000,
         smem=1,
+        hbm=(1,),
         scratch=[edge, edge],
-    )(spot, latents, cotangent, ret, back_core, back_chip, conv_kernel)
-
-    second_sent = call(
-        second_kernel, struct((strips, 16, LANES), BF16), 16, moved=1_000_000, smem=1
-    )(spot, first_recv)
-    second_recv = lax.all_to_all(second_sent, "azim", split_axis=0, concat_axis=0, tiled=True)
+    )(spot, second_sent, latents, cotangent, ret, back_core, back_chip, table)
+
     second_recv, grad_latents = lax.optimization_barrier((second_recv, grad_latents))
     third_sent = call(third_kernel, struct((GROUPS, 16, LANES), F32), 16, moved=300_000)(
         second_recv

time: 136 us -> 135 us (level)
  the two profiles are of different devices: /device:TPU:1 before, /device:TPU:40 now
where the time goes in v5:
time: 135 us; the launch traced here: 134 us
  blocking collectives  63 us (47%)
  starting transfers between devices  36.5 us (27%)
  waiting for transfers between devices  18 us (13%)
  Pallas kernels  13.7 us (10%)
  local copies, waits for them, and re-layouts  1.87 us (1%)
    all_to_all x1, blocking collectives, on_device(): lax.all_to_all(sent, 'sweep', split_axis=0, concat_axis=0, tiled=True)  33.6 us
    all_to_all x1, blocking collectives, on_device(): lax.all_to_all(first_sent, 'sweep', split_axis=0, concat_axis=0, tiled=True)  17.4 us
    pallas_call x12, Pallas kernels, run(): pl.pallas_call(kernel, out_shape=outs, in_specs=specs, out_specs=jax.tree...  12.3 us
    all_to_all x1, blocking collectives, on_device(): lax.all_to_all(third_sent, 'sweep', split_axis=0, concat_axis=0, tiled=True)  12 us
    ppermute x1, starting transfers between devices, on_device(): other_chip = lax.ppermute(to_chip, 'azim', chips)  11 us
    ppermute x1, waiting for transfers between devices, on_device(): from_chip = lax.ppermute(send, 'azim', sides)  8.31 us
    all_to_all x1, starting transfers between devices, on_device(): lax.all_to_all(second_sent, 'azim', split_axis=0, concat_axis=0, tiled=True)  7.42 us
    ppermute x1, waiting for transfers between devices, on_device(): back_chip = lax.ppermute(to_chip, 'azim', chips)  6.69 us
  transfers between devices with their start and end apart: 8, of which 4 were waited for; matrix products, arithmetic and copies ran while one was open for 0% of the time, Pallas kernels for 2%

profile of v5, /device:TPU:40, one launch (start us, length us, event | category | flops | bytes accessed | tf_op | source)
XLA Modules:
  0.0 133.9 jit_solution(10965728519855550780)
XLA Ops:
  0.6 1.0 copy-done
  1.7 0.1 shard_map.152.after
  1.7 11.0 %collective-permute-start.1 = (bf16[2,8,512]{2,1,0:T(8,128)(2,1)S(1)}, bf16[2,8,512]{2,1,0:T(8,128)(2,1)S(1)}, u32[]{:S(2)}, u32[]{:S(2)}) collective-permute-start(bf16[2,8,512]{2,1,0:T(8,128)(2,1)S(1)} %shard_map.152.after), channel_id=1, source_target_pairs={{0,31},{1,2},{2,1},{3,4},{4,3},{5,6},{6,5},{7,8},{8,7},{9,10},{10,... | collective-permute-start | bytes 49160 | tf_op jit(solution)/shard_map/ppermute | solution.py:464
  12.7 0.0 copy-start.3
  12.7 0.7 copy-done.3
  13.5 0.1 shard_map.153
  13.5 1.9 %collective-permute-start = (bf16[2,8,512]{2,1,0:T(8,128)(2,1)S(1)}, bf16[2,8,512]{2,1,0:T(8,128)(2,1)S(1)}, u32[]{:S(2)}, u32[]{:S(2)}) collective-permute-start(bf16[2,8,512]{2,1,0:T(8,128)(2,1)S(1)} %get-tuple-element.24), channel_id=1, source_target_pairs={{0,1},{1,0},{2,3},{3,2},{4,5},{5,4},{6,7},{7,6},{8,9},{9,8},{10,11... | collective-permute-start | bytes 49160 | tf_op jit(solution)/shard_map/ppermute | solution.py:474
  15.5 1.1 collective-permute-done.other_core
  16.6 1.2 shard_map.154
  17.9 0.0 copy-start.7
  17.9 0.0 copy-start.8
  17.9 33.6 %all_to_all.25.recv = bf16[16,2,2,16,512]{4,3,2,1,0:T(8,128)(2,1)S(1)} all-to-all(bf16[16,2,2,16,512]{4,3,2,1,0:T(8,128)(2,1)S(1)} %shard_map.154), channel_id=1, replica_groups=mesh['sweep'=16,'azim'=32] {'sweep'}, dimensions={0} | all-to-all | bytes 2097152 | tf_op jit(solution)/shard_map/all_to_all | solution.py:485
  51.6 6.9 %shard_map.155 = (bf16[16,2,16,512]{3,2,1,0:T(8,128)(2,1)}, bf16[2,2,16,64,128]{4,3,2,1,0:T(8,128)(2,1)S(1)}, f32[1,512]{1,0:T(1,128)S(1)}) custom-call(s32[1]{0:T(128)} %bitcast.spot, bf16[16,2,2,16,512]{4,3,2,1,0:T(8,128)(2,1)S(1)} %all_to_all.25.recv, bf16[512,256]{1,0:T(8,128)(2,1)S(1)} %copy-done.5, bf16[512,256]{1,0:T(8,128)(2,1)S(1)} %copy-done.6, ...), custom_call_target="tpu_custom_call" | custom-call | flops 2000000000 | bytes 6000000 | tf_op jit(solution)/shard_map/pallas_call | solution.py:37
  58.4 5.6 %all-to-all-start.1 = ((bf16[16,2,16,512]{3,2,1,0:T(8,128)(2,1)}), bf16[16,2,16,512]{3,2,1,0:T(8,128)(2,1)S(1)}, u32[]{:S(2)}, u32[]{:S(2)}) async-start(bf16[16,2,16,512]{3,2,1,0:T(8,128)(2,1)} %get-tuple-element.26), calls=%async_computation.1 | async-start | bytes 1048576 | tf_op jit(solution)/shard_map/all_to_all | solution.py:511
  64.1 1.9 %collective-permute-start.2 = (bf16[2,16,64,128]{3,2,1,0:T(8,128)(2,1)S(1)}, bf16[2,16,64,128]{3,2,1,0:T(8,128)(2,1)S(1)}, u32[]{:S(2)}, u32[]{:S(2)}) collective-permute-start(bf16[2,16,64,128]{3,2,1,0:T(8,128)(2,1)S(1)} %slice_bitcast_fusion), channel_id=1, source_target_pairs={{0,1},{1,0},{2,3},{3,2},{4,5},{5,4},{6,7},{7,6},{8,9},{9,8},{10,11... | collective-permute-start | bytes 1572872 | tf_op jit(solution)/shard_map/ppermute | solution.py:512
  66.0 1.9 %collective-permute-done.2.got = bf16[2,16,64,128]{3,2,1,0:T(8,128)(2,1)S(1)} collective-permute-done((bf16[2,16,64,128]{3,2,1,0:T(8,128)(2,1)S(1)}, bf16[2,16,64,128]{3,2,1,0:T(8,128)(2,1)S(1)}, u32[]{:S(2)}, u32[]{:S(2)}) %collective-permute-start.2) | collective-permute-done | bytes 524320 | tf_op jit(solution)/shard_map/ppermute | solution.py:512
  67.9 0.1 shard_map.156
  68.0 2.1 %collective-permute-start.3 = (bf16[16,64,128]{2,1,0:T(8,128)(2,1)S(1)}, bf16[16,64,128]{2,1,0:T(8,128)(2,1)S(1)}, u32[]{:S(2)}, u32[]{:S(2)}) collective-permute-start(bf16[16,64,128]{2,1,0:T(8,128)(2,1)S(1)} %get-tuple-element.30), channel_id=1, source_target_pairs={{0,2},{1,3},{2,0},{3,1},{4,6},{5,7},{6,4},{7,5},{8,10},{9,11},{10,... | collective-permute-start | bytes 786440 | tf_op jit(solution)/shard_map/ppermute | solution.py:515
  70.1 8.3 %collective-permute-done.3.got = bf16[16,64,128]{2,1,0:T(8,128)(2,1)S(1)} collective-permute-done((bf16[16,64,128]{2,1,0:T(8,128)(2,1)S(1)}, bf16[16,64,128]{2,1,0:T(8,128)(2,1)S(1)}, u32[]{:S(2)}, u32[]{:S(2)}) %collective-permute-start.3) | collective-permute-done | bytes 262176 | tf_op jit(solution)/shard_map/ppermute | solution.py:515
  78.4 0.1 shard_map.157.sums_in
  78.5 1.3 shard_map.158
  79.8 17.4 %all_to_all.26.recv = bf16[16,80,128]{2,1,0:T(8,128)(2,1)S(1)} all-to-all(bf16[16,80,128]{2,1,0:T(8,128)(2,1)S(1)} %shard_map.158), channel_id=1, replica_groups=mesh['sweep'=16,'azim'=32] {'sweep'}, dimensions={0} | all-to-all | bytes 655360 | tf_op jit(solution)/shard_map/all_to_all | solution.py:539
  97.2 0.7 shard_map.159.after
  97.9 7.4 %all-to-all-start.3 = ((bf16[32,16,128]{2,1,0:T(8,128)(2,1)}), bf16[32,16,128]{2,1,0:T(8,128)(2,1)S(1)}, u32[]{:S(2)}, u32[]{:S(2)}) async-start(bf16[32,16,128]{2,1,0:T(8,128)(2,1)} %shard_map.159.after), calls=%async_computation.3 | async-start | bytes 262144 | tf_op jit(solution)/shard_map/all_to_all | solution.py:544
  105.4 0.1 shard_map.160.after
  105.5 0.1 shard_map.161
  105.6 2.1 %collective-permute-start.4 = (bf16[2,2,8,512]{3,2,1,0:T(8,128)(2,1)S(1)}, bf16[2,2,8,512]{3,2,1,0:T(8,128)(2,1)S(1)}, u32[]{:S(2)}, u32[]{:S(2)}) collective-permute-start(bf16[2,2,8,512]{3,2,1,0:T(8,128)(2,1)S(1)} %shard_map.161), channel_id=1, source_target_pairs={{0,1},{1,0},{2,3},{3,2},{4,5},{5,4},{6,7},{7,6},{8,9},{9,8},{10,11... | collective-permute-start | bytes 98312 | tf_op jit(solution)/shard_map/ppermute | solution.py:559
  107.7 4.5 %collective-permute-start.5 = (bf16[2,2,8,512]{3,2,1,0:T(8,128)(2,1)S(1)}, bf16[2,2,8,512]{3,2,1,0:T(8,128)(2,1)S(1)}, u32[]{:S(2)}, u32[]{:S(2)}) collective-permute-start(bf16[2,2,8,512]{3,2,1,0:T(8,128)(2,1)S(1)} %shard_map.160.after), channel_id=1, source_target_pairs={{0,31},{1,2},{2,1},{3,4},{4,3},{5,6},{6,5},{7,8},{8,7},{9,10},{10,... | collective-permute-start | bytes 98312 | tf_op jit(solution)/shard_map/ppermute | solution.py:558
  112.2 6.7 %collective-permute-done.5.other_chip = bf16[2,2,8,512]{3,2,1,0:T(8,128)(2,1)S(1)} collective-permute-done((bf16[2,2,8,512]{3,2,1,0:T(8,128)(2,1)S(1)}, bf16[2,2,8,512]{3,2,1,0:T(8,128)(2,1)S(1)}, u32[]{:S(2)}, u32[]{:S(2)}) %collective-permute-start.5) | collective-permute-done | bytes 32800 | tf_op jit(solution)/shard_map/ppermute | solution.py:558
  118.9 2.3 %shard_map.162 = f32[2,8,32,512]{3,2,1,0:T(8,128)} custom-call(s32[1]{0:T(128)} %bitcast.spot, bf16[32,16,128]{2,1,0:T(8,128)(2,1)} %shard_map.159.after, bf16[2,8,32,512]{3,2,1,0:T(8,128)(2,1)S(1)} %copy-done.1, bf16[2,8,32,512]{3,2,1,0:T(8,128)(2,1)S(1)} %copy-done.2, bf16[16,2,16,512]{3,2,1,0:T(8,128)(2,1)S(1)} %all-to-all-done.1.ret, ...), custom_call_target="tpu_custom_call" | custom-call | flops 10000000 | bytes 4000000 | tf_op jit(solution)/shard_map/pallas_call | solution.py:37
  121.3 12.0 %all_to_all.27.recv = f32[16,16,128]{2,1,0:T(8,128)S(1)} all-to-all(f32[16,16,128]{2,1,0:T(8,128)S(1)} %shard_map.163), channel_id=1, replica_groups=mesh['sweep'=16,'azim'=32] {'sweep'}, dimensions={0} | all-to-all | bytes 262144 | tf_op jit(solution)/shard_map/all_to_all | solution.py:576
  133.3 0.7 shard_map.164
  (21 shorter events, 0.1 us)
Async XLA Ops:
  0.6 1.0 copy-start
  1.7 11.0 %copy-start.4 = (f32[512]{0:T(512)S(1)}, f32[512]{0:T(512)}, u32[]{:S(2)}) copy-start(f32[512]{0:T(512)} %param.12) | copy-start | bytes 6148
  1.7 14.9 %copy-start.2 = (bf16[2,8,32,512]{3,2,1,0:T(8,128)(2,1)S(1)}, bf16[2,8,32,512]{3,2,1,0:T(8,128)(2,1)}, u32[]{:S(2)}) copy-start(bf16[2,8,32,512]{3,2,1,0:T(8,128)(2,1)} %cot.9) | copy-start | bytes 1572868
  1.7 13.7 %collective-permute-start.1 = (bf16[2,8,512]{2,1,0:T(8,128)(2,1)S(1)}, bf16[2,8,512]{2,1,0:T(8,128)(2,1)S(1)}, u32[]{:S(2)}, u32[]{:S(2)}) collective-permute-start(bf16[2,8,512]{2,1,0:T(8,128)(2,1)S(1)} %shard_map.152.after), channel_id=1, source_target_pairs={{0,31},{1,2},{2,1},{3,4},{4,3},{5,6},{6,5},{7,8},{8,7},{9,10},{10,... | collective-permute-start | bytes 49160 | tf_op jit(solution)/shard_map/ppermute | solution.py:464
  12.7 0.8 copy-start.3
  13.5 3.1 %collective-permute-start = (bf16[2,8,512]{2,1,0:T(8,128)(2,1)S(1)}, bf16[2,8,512]{2,1,0:T(8,128)(2,1)S(1)}, u32[]{:S(2)}, u32[]{:S(2)}) collective-permute-start(bf16[2,8,512]{2,1,0:T(8,128)(2,1)S(1)} %get-tuple-element.24), channel_id=1, source_target_pairs={{0,1},{1,0},{2,3},{3,2},{4,5},{5,4},{6,7},{7,6},{8,9},{9,8},{10,11... | collective-permute-start | bytes 49160 | tf_op jit(solution)/shard_map/ppermute | solution.py:474
  17.8 33.7 %copy-start.5 = (bf16[512,256]{1,0:T(8,128)(2,1)S(1)}, bf16[512,256]{1,0:T(8,128)(2,1)}, u32[]{:S(2)}) copy-start(bf16[512,256]{1,0:T(8,128)(2,1)} %w_query.1) | copy-start | bytes 786436
  17.9 33.7 %copy-start.6 = (bf16[512,256]{1,0:T(8,128)(2,1)S(1)}, bf16[512,256]{1,0:T(8,128)(2,1)}, u32[]{:S(2)}) copy-start(bf16[512,256]{1,0:T(8,128)(2,1)} %w_key.1) | copy-start | bytes 786436
  17.9 33.7 %copy-start.7 = (bf16[512,256]{1,0:T(8,128)(2,1)S(1)}, bf16[512,256]{1,0:T(8,128)(2,1)}, u32[]{:S(2)}) copy-start(bf16[512,256]{1,0:T(8,128)(2,1)} %w_value.1) | copy-start | bytes 786436
  17.9 33.7 %copy-start.8 = (bf16[512,256]{1,0:T(8,128)(2,1)S(1)}, bf16[512,256]{1,0:T(8,128)(2,1)}, u32[]{:S(2)}) copy-start(bf16[512,256]{1,0:T(8,128)(2,1)} %w_output.1) | copy-start | bytes 786436
  17.9 33.7 %copy-start.9 = (f32[512]{0:T(512)S(1)}, f32[512]{0:T(512)}, u32[]{:S(2)}) copy-start(f32[512]{0:T(512)} %param.13) | copy-start | bytes 6148
  58.4 20.1 %all-to-all-start.1 = ((bf16[16,2,16,512]{3,2,1,0:T(8,128)(2,1)}), bf16[16,2,16,512]{3,2,1,0:T(8,128)(2,1)S(1)}, u32[]{:S(2)}, u32[]{:S(2)}) async-start(bf16[16,2,16,512]{3,2,1,0:T(8,128)(2,1)} %get-tuple-element.26), calls=%async_computation.1 | async-start | bytes 1048576 | tf_op jit(solution)/shard_map/all_to_all | solution.py:511
  64.1 3.8 %collective-permute-start.2 = (bf16[2,16,64,128]{3,2,1,0:T(8,128)(2,1)S(1)}, bf16[2,16,64,128]{3,2,1,0:T(8,128)(2,1)S(1)}, u32[]{:S(2)}, u32[]{:S(2)}) collective-permute-start(bf16[2,16,64,128]{3,2,1,0:T(8,128)(2,1)S(1)} %slice_bitcast_fusion), channel_id=1, source_target_pairs={{0,1},{1,0},{2,3},{3,2},{4,5},{5,4},{6,7},{7,6},{8,9},{9,8},{10,11... | collective-permute-start | bytes 1572872 | tf_op jit(solution)/shard_map/ppermute | solution.py:512
  68.0 10.5 %copy-start.1 = (bf16[2,8,32,512]{3,2,1,0:T(8,128)(2,1)S(1)}, bf16[2,8,32,512]{3,2,1,0:T(8,128)(2,1)}, u32[]{:S(2)}) copy-start(bf16[2,8,32,512]{3,2,1,0:T(8,128)(2,1)} %lat.9) | copy-start | bytes 1572868
  68.0 10.4 %collective-permute-start.3 = (bf16[16,64,128]{2,1,0:T(8,128)(2,1)S(1)}, bf16[16,64,128]{2,1,0:T(8,128)(2,1)S(1)}, u32[]{:S(2)}, u32[]{:S(2)}) collective-permute-start(bf16[16,64,128]{2,1,0:T(8,128)(2,1)S(1)} %get-tuple-element.30), channel_id=1, source_target_pairs={{0,2},{1,3},{2,0},{3,1},{4,6},{5,7},{6,4},{7,5},{8,10},{9,11},{10,... | collective-permute-start | bytes 786440 | tf_op jit(solution)/shard_map/ppermute | solution.py:515
  97.9 23.3 %all-to-all-start.3 = ((bf16[32,16,128]{2,1,0:T(8,128)(2,1)}), bf16[32,16,128]{2,1,0:T(8,128)(2,1)S(1)}, u32[]{:S(2)}, u32[]{:S(2)}) async-start(bf16[32,16,128]{2,1,0:T(8,128)(2,1)} %shard_map.159.after), calls=%async_computation.3 | async-start | bytes 262144 | tf_op jit(solution)/shard_map/all_to_all | solution.py:544
  105.6 6.6 %collective-permute-start.4 = (bf16[2,2,8,512]{3,2,1,0:T(8,128)(2,1)S(1)}, bf16[2,2,8,512]{3,2,1,0:T(8,128)(2,1)S(1)}, u32[]{:S(2)}, u32[]{:S(2)}) collective-permute-start(bf16[2,2,8,512]{3,2,1,0:T(8,128)(2,1)S(1)} %shard_map.161), channel_id=1, source_target_pairs={{0,1},{1,0},{2,3},{3,2},{4,5},{5,4},{6,7},{7,6},{8,9},{9,8},{10,11... | collective-permute-start | bytes 98312 | tf_op jit(solution)/shard_map/ppermute | solution.py:559
  107.7 11.3 %collective-permute-start.5 = (bf16[2,2,8,512]{3,2,1,0:T(8,128)(2,1)S(1)}, bf16[2,2,8,512]{3,2,1,0:T(8,128)(2,1)S(1)}, u32[]{:S(2)}, u32[]{:S(2)}) collective-permute-start(bf16[2,2,8,512]{3,2,1,0:T(8,128)(2,1)S(1)} %shard_map.160.after), channel_id=1, source_target_pairs={{0,31},{1,2},{2,1},{3,4},{4,3},{5,6},{6,5},{7,8},{8,7},{9,10},{10,... | collective-permute-start | bytes 98312 | tf_op jit(solution)/shard_map/ppermute | solution.py:558

commit v6 on v5

--- a/solution.py
+++ b/solution.py
@@ -109,7 +109,15 @@
             edges[1, s, h : h + 1, :] = lat[s, h, PX:, :].astype(F32)[PX - 1 :]
 
 
-def chip_edge_kernel(spot, lat, out, edges):
+def pack_kernel(cot, out):
+    for s in range(SL):
+        for h in range(H):
+            out[2 * h, s] = cot[s, h, :PX, :]
+            out[2 * h + 1, s] = cot[s, h, PX:, :]
+
+
+def chip_edge_kernel(spot, after, lat, out, edges):
+    del after
     edge_columns(lat, edges)
     out[...] = partner_column(spot, False, edges[0], edges[1]).astype(BF16)
 
@@ -123,7 +131,7 @@
     table[10:, :] = jnp.zeros((6, C), F32)
 
 
-def forward_kernel(spot, lat, cot, other_core, other_chip, taps, out, edge_l, edge_r):
+def forward_kernel(spot, lat, other_core, other_chip, taps, out, edge_l, edge_r):
     for s in range(SL):
         left, right = from_partners(spot, other_core[s].astype(F32), other_chip[s].astype(F32))
         shifted = row_shifts(silu(left))
@@ -154,11 +162,8 @@
                 rows == WL - 1, edge_r[s, h : h + 1, here], pltpu.roll(cols[2], WL - 1, 0)
             )
             y = (values[h] + (cols[1] + from_left + from_right) + base).astype(BF16)
-            out[2 * h, 0, s, :, here] = y[:PX]
-            out[2 * h + 1, 0, s, :, here] = y[PX:]
-            moved = cot[s, h, :, here]
-            out[2 * h, 1, s, :, here] = moved[:PX]
-            out[2 * h + 1, 1, s, :, here] = moved[PX:]
+            out[2 * h, s, :, here] = y[:PX]
+            out[2 * h + 1, s, :, here] = y[PX:]
 
 
 def pair_up(first, second):
@@ -170,7 +175,7 @@
 
 
 def attend_kernel(
-    predivide, spot, recv, w_query, w_key, w_value, w_output, gain,
+    predivide, spot, recv, recv_cot, w_query, w_key, w_value, w_output, gain,
     out, halves, gain_sum,
     normed, stacked, attended, cot, y_rows, inv_rows, qkv, gatt, gnorm,
 ):
@@ -178,10 +183,10 @@
     scale = 1.0 / math.sqrt(DH)
     for tile in range(2):
         y_two = [
-            recv[:, 0, s].astype(F32)[:, 8 * tile : 8 * tile + 8, :] for s in range(SL)
+            recv[:, s].astype(F32)[:, 8 * tile : 8 * tile + 8, :] for s in range(SL)
         ]
         cot_two = [
-            recv[:, 1, s].astype(F32)[:, 8 * tile : 8 * tile + 8, :] for s in range(SL)
+            recv_cot[:, s].astype(F32)[:, 8 * tile : 8 * tile + 8, :] for s in range(SL)
         ]
         for half, (y, c) in enumerate(zip(pair_up(*y_two), pair_up(*cot_two))):
             at = pl.ds((2 * tile + half) * rows_each, rows_each)
@@ -396,7 +401,8 @@
             out[s, h, :, here] = grads[h] + total * (sig * (1.0 + value * (1.0 - sig)))
 
 
-def second_kernel(spot, recv, out):
+def second_kernel(spot, recv, after_chip, after_core, out):
+    del after_chip, after_core
     total = jnp.sum(recv[...].astype(F32), axis=0)
     weights = total[:ROWS].reshape(8, 8, LANES)
     taps = total[ROWS : ROWS + 8] + total[ROWS + 8 :]
@@ -458,9 +464,12 @@
 
     one_edge = struct((SL, H, C), BF16)
     column = [pltpu.VMEM((2, SL, H, C), F32)]
-    to_chip = call(chip_edge_kernel, one_edge, 16, moved=600_000, smem=1, scratch=column)(
-        spot, latents
-    )
+    packed = struct((GROUPS, SL, PX, C), BF16)
+    cot_sent = call(pack_kernel, packed, 16, moved=1_000_000)(cotangent)
+    recv_cot = lax.all_to_all(cot_sent, "sweep", split_axis=0, concat_axis=0, tiled=True)
+    to_chip = call(
+        chip_edge_kernel, one_edge, 16, moved=600_000, smem=1, hbm=(1,), scratch=column
+    )(spot, cot_sent, latents)
     other_chip = lax.ppermute(to_chip, "azim", chips)
     to_core, table = call(
         core_edge_kernel,
@@ -475,13 +484,13 @@
 
     sent = call(
         forward_kernel,
-        struct((GROUPS, 2, SL, PX, C), BF16),
+        packed,
         16,
         flops=10_000_000,
-        moved=2_000_000,
+        moved=1_000_000,
         smem=1,
         scratch=[edge, edge],
-    )(spot, latents, cotangent, other_core, other_chip, table)
+    )(spot, latents, other_core, other_chip, table)
     recv = lax.all_to_all(sent, "sweep", split_axis=0, concat_axis=0, tiled=True)
 
     rows = GROUPS * SL * PX
@@ -507,7 +516,7 @@
             pltpu.VMEM((rows, HD), BF16),
             pltpu.VMEM((rows, C), F32),
         ],
-    )(spot, recv, w_query, w_key, w_value, w_output, gain_row)
+    )(spot, recv, recv_cot, w_query, w_key, w_value, w_output, gain_row)
     ret = lax.all_to_all(grad_attn, "sweep", split_axis=0, concat_axis=0, tiled=True)
     from_core = lax.ppermute(halves[1], "azim", cores)
     piece = struct((GROUPS, ROWS, LANES), BF16)
@@ -538,10 +547,6 @@
     )(spot, latents, other_core, other_chip, cotangent, ret, gain_sum, sums)
     first_recv = lax.all_to_all(first_sent, "sweep", split_axis=0, concat_axis=0, tiled=True)
     both_edges = struct((2, SL, H, C), BF16)
-    second_sent = call(
-        second_kernel, struct((strips, 16, LANES), BF16), 16, moved=1_000_000, smem=1
-    )(spot, first_recv)
-    second_recv = lax.all_to_all(second_sent, "azim", split_axis=0, concat_axis=0, tiled=True)
 
     def back_edges(for_core, after):
         return call(
@@ -554,9 +559,20 @@
             scratch=[pltpu.VMEM((2, 2, SL, H, C), F32)],
         )(spot, after, cotangent, ret)
 
-    to_chip = back_edges(False, second_sent)
+    to_chip = back_edges(False, first_sent)
     back_chip = lax.ppermute(to_chip, "azim", chips)
-    back_core = lax.ppermute(back_edges(True, to_chip), "azim", cores)
+    to_core = back_edges(True, to_chip)
+    back_core = lax.ppermute(to_core, "azim", cores)
+
+    second_sent = call(
+        second_kernel, struct((strips, 16, LANES), BF16), 16, moved=1_000_000, smem=1, hbm=(2, 3)
+    )(spot, first_recv, back_chip, back_core)
+    second_recv = lax.all_to_all(second_sent, "azim", split_axis=0, concat_axis=0, tiled=True)
+
+    third_sent = call(third_kernel, struct((GROUPS, 16, LANES), F32), 16, moved=300_000)(
+        second_recv
+    )
+    third_recv = lax.all_to_all(third_sent, "sweep", split_axis=0, concat_axis=0, tiled=True)
 
     grad_latents = call(
         latents_kernel,
@@ -567,13 +583,8 @@
         smem=1,
         hbm=(1,),
         scratch=[edge, edge],
-    )(spot, second_sent, latents, cotangent, ret, back_core, back_chip, table)
-
-    second_recv, grad_latents = lax.optimization_barrier((second_recv, grad_latents))
-    third_sent = call(third_kernel, struct((GROUPS, 16, LANES), F32), 16, moved=300_000)(
-        second_recv
-    )
-    third_recv = lax.all_to_all(third_sent, "sweep", split_axis=0, concat_axis=0, tiled=True)
+    )(spot, third_sent, latents, cotangent, ret, back_core, back_chip, table)
+
     share = struct((C // strips, HD), F32)
     line = struct((1, C), F32)
     grad_kernel, grad_bias, grad_gain, *shares = call(

time: 135 us -> 139 us (1.030)
  the two profiles are of different devices: /device:TPU:40 before, /device:TPU:1 now
where the time goes in v6:
time: 139 us; the launch traced here: 138 us
  starting transfers between devices  56 us (40%)
  blocking collectives  43.8 us (32%)
  waiting for transfers between devices  20.1 us (14%)
  Pallas kernels  15.9 us (11%)
    all_to_all x1, blocking collectives, on_device(): lax.all_to_all(second_sent, 'azim', split_axis=0, concat_axis=0, tiled=True)  23.7 us
    all_to_all x1, blocking collectives, on_device(): lax.all_to_all(sent, 'sweep', split_axis=0, concat_axis=0, tiled=True)  20.1 us
    pallas_call x13, Pallas kernels, run(): pl.pallas_call(kernel, out_shape=outs, in_specs=specs, out_specs=jax.tree...  13.9 us
    ppermute x1, starting transfers between devices, on_device(): other_core = lax.ppermute(to_core, 'azim', cores)  10.7 us
    all_to_all x1, starting transfers between devices, on_device(): lax.all_to_all(cot_sent, 'sweep', split_axis=0, concat_axis=0, tiled=True)  8.12 us
    all_to_all x1, starting transfers between devices, on_device(): lax.all_to_all(third_sent, 'sweep', split_axis=0, concat_axis=0, tiled=True)  8.07 us
    ppermute x1, waiting for transfers between devices, on_device(): from_chip = lax.ppermute(send, 'azim', sides)  7.49 us
    all_to_all x1, starting transfers between devices, on_device(): lax.all_to_all(first_sent, 'sweep', split_axis=0, concat_axis=0, tiled=True)  7.18 us
  transfers between devices with their start and end apart: 10, of which 6 were waited for; matrix products, arithmetic and copies ran while one was open for 0% of the time, Pallas kernels for 3%

profile of v6, /device:TPU:1, one launch (start us, length us, event | category | flops | bytes accessed | tf_op | source)
XLA Modules:
  0.0 137.8 jit_solution(8749059906484663101)
XLA Ops:
  0.6 1.0 copy-done
  1.7 0.8 shard_map.152.after
  2.5 8.1 %all-to-all-start.1 = ((bf16[16,2,16,512]{3,2,1,0:T(8,128)(2,1)}), bf16[16,2,16,512]{3,2,1,0:T(8,128)(2,1)S(1)}, u32[]{:S(2)}, u32[]{:S(2)}) async-start(bf16[16,2,16,512]{3,2,1,0:T(8,128)(2,1)} %shard_map.152.after), calls=%async_computation.1 | async-start | bytes 1048576 | tf_op jit(solution)/shard_map/all_to_all | solution.py:469
  10.7 0.1 shard_map.153.after
  10.7 4.8 %collective-permute-start.1 = (bf16[2,8,512]{2,1,0:T(8,128)(2,1)S(1)}, bf16[2,8,512]{2,1,0:T(8,128)(2,1)S(1)}, u32[]{:S(2)}, u32[]{:S(2)}) collective-permute-start(bf16[2,8,512]{2,1,0:T(8,128)(2,1)S(1)} %shard_map.153.after), channel_id=1, source_target_pairs={{0,31},{1,2},{2,1},{3,4},{4,3},{5,6},{6,5},{7,8},{8,7},{9,10},{10,... | collective-permute-start | bytes 49160 | tf_op jit(solution)/shard_map/ppermute | solution.py:473
  15.6 0.1 shard_map.154
  15.7 10.7 %collective-permute-start = (bf16[2,8,512]{2,1,0:T(8,128)(2,1)S(1)}, bf16[2,8,512]{2,1,0:T(8,128)(2,1)S(1)}, u32[]{:S(2)}, u32[]{:S(2)}) collective-permute-start(bf16[2,8,512]{2,1,0:T(8,128)(2,1)S(1)} %get-tuple-element.22), channel_id=1, source_target_pairs={{0,1},{1,0},{2,3},{3,2},{4,5},{5,4},{6,7},{7,6},{8,9},{9,8},{10,11... | collective-permute-start | bytes 49160 | tf_op jit(solution)/shard_map/ppermute | solution.py:483
  26.4 0.8 collective-permute-done.other_core
  27.2 1.2 shard_map.155
  28.5 20.1 %all_to_all.30.recv = bf16[16,2,16,512]{3,2,1,0:T(8,128)(2,1)S(1)} all-to-all(bf16[16,2,16,512]{3,2,1,0:T(8,128)(2,1)S(1)} %shard_map.155), channel_id=1, replica_groups=mesh['sweep'=16,'azim'=32] {'sweep'}, dimensions={0} | all-to-all | bytes 1048576 | tf_op jit(solution)/shard_map/all_to_all | solution.py:494
  48.6 6.9 %shard_map.156 = (bf16[16,2,16,512]{3,2,1,0:T(8,128)(2,1)}, bf16[2,2,16,64,128]{4,3,2,1,0:T(8,128)(2,1)S(1)}, f32[1,512]{1,0:T(1,128)S(1)}) custom-call(s32[1]{0:T(128)} %bitcast.spot, bf16[16,2,16,512]{3,2,1,0:T(8,128)(2,1)S(1)} %all_to_all.30.recv, bf16[16,2,16,512]{3,2,1,0:T(8,128)(2,1)S(1)} %all-to-all-done.1.recv_cot, bf16[512,256]{1,0:T(8,128)(2,1)S(1)} %copy-done.5, ...), custom_call_target="tpu_custom_call" | custom-call | flops 2000000000 | bytes 6000000 | tf_op jit(solution)/shard_map/pallas_call | solution.py:37
  55.5 3.9 %all-to-all-start.2 = ((bf16[16,2,16,512]{3,2,1,0:T(8,128)(2,1)}), bf16[16,2,16,512]{3,2,1,0:T(8,128)(2,1)S(1)}, u32[]{:S(2)}, u32[]{:S(2)}) async-start(bf16[16,2,16,512]{3,2,1,0:T(8,128)(2,1)} %get-tuple-element.24), calls=%async_computation.2 | async-start | bytes 1048576 | tf_op jit(solution)/shard_map/all_to_all | solution.py:520
  59.4 5.8 %collective-permute-start.2 = (bf16[2,16,64,128]{3,2,1,0:T(8,128)(2,1)S(1)}, bf16[2,16,64,128]{3,2,1,0:T(8,128)(2,1)S(1)}, u32[]{:S(2)}, u32[]{:S(2)}) collective-permute-start(bf16[2,16,64,128]{3,2,1,0:T(8,128)(2,1)S(1)} %slice_bitcast_fusion), channel_id=1, source_target_pairs={{0,1},{1,0},{2,3},{3,2},{4,5},{5,4},{6,7},{7,6},{8,9},{9,8},{10,11... | collective-permute-start | bytes 1572872 | tf_op jit(solution)/shard_map/ppermute | solution.py:521
  65.2 1.5 %collective-permute-done.2.got = bf16[2,16,64,128]{3,2,1,0:T(8,128)(2,1)S(1)} collective-permute-done((bf16[2,16,64,128]{3,2,1,0:T(8,128)(2,1)S(1)}, bf16[2,16,64,128]{3,2,1,0:T(8,128)(2,1)S(1)}, u32[]{:S(2)}, u32[]{:S(2)}) %collective-permute-start.2) | collective-permute-done | bytes 524320 | tf_op jit(solution)/shard_map/ppermute | solution.py:521
  66.7 0.1 shard_map.157
  66.9 2.1 %collective-permute-start.3 = (bf16[16,64,128]{2,1,0:T(8,128)(2,1)S(1)}, bf16[16,64,128]{2,1,0:T(8,128)(2,1)S(1)}, u32[]{:S(2)}, u32[]{:S(2)}) collective-permute-start(bf16[16,64,128]{2,1,0:T(8,128)(2,1)S(1)} %get-tuple-element.28), channel_id=1, source_target_pairs={{0,2},{1,3},{2,0},{3,1},{4,6},{5,7},{6,4},{7,5},{8,10},{9,11},{10,... | collective-permute-start | bytes 786440 | tf_op jit(solution)/shard_map/ppermute | solution.py:524
  68.9 7.5 %collective-permute-done.3.got = bf16[16,64,128]{2,1,0:T(8,128)(2,1)S(1)} collective-permute-done((bf16[16,64,128]{2,1,0:T(8,128)(2,1)S(1)}, bf16[16,64,128]{2,1,0:T(8,128)(2,1)S(1)}, u32[]{:S(2)}, u32[]{:S(2)}) %collective-permute-start.3) | collective-permute-done | bytes 262176 | tf_op jit(solution)/shard_map/ppermute | solution.py:524
  76.4 0.8 shard_map.158.sums_in
  77.2 2.0 %shard_map.159.after = bf16[16,80,128]{2,1,0:T(8,128)(2,1)} custom-call(s32[1]{0:T(128)} %bitcast.spot, bf16[2,8,32,512]{3,2,1,0:T(8,128)(2,1)S(1)} %copy-done.2, bf16[2,8,512]{2,1,0:T(8,128)(2,1)S(1)} %collective-permute-done.other_core, bf16[2,8,512]{2,1,0:T(8,128)(2,1)S(1)} %collective-permute-done.1.other_chip, ...), custom_call_target="tpu_custom_call", output_to_operand_aliasing={{}: (7, {})} | custom-call | flops 10000000 | bytes 2000000 | tf_op jit(solution)/shard_map/pallas_call | solution.py:530
  79.2 7.2 %all-to-all-start.3 = ((bf16[16,80,128]{2,1,0:T(8,128)(2,1)}), bf16[16,80,128]{2,1,0:T(8,128)(2,1)S(1)}, u32[]{:S(2)}, u32[]{:S(2)}) async-start(bf16[16,80,128]{2,1,0:T(8,128)(2,1)} %shard_map.159.after), calls=%async_computation.3 | async-start | bytes 655360 | tf_op jit(solution)/shard_map/all_to_all | solution.py:548
  86.4 0.1 shard_map.160.after
  86.5 0.1 shard_map.161
  86.6 3.4 %collective-permute-start.5 = (bf16[2,2,8,512]{3,2,1,0:T(8,128)(2,1)S(1)}, bf16[2,2,8,512]{3,2,1,0:T(8,128)(2,1)S(1)}, u32[]{:S(2)}, u32[]{:S(2)}) collective-permute-start(bf16[2,2,8,512]{3,2,1,0:T(8,128)(2,1)S(1)} %shard_map.161), channel_id=1, source_target_pairs={{0,1},{1,0},{2,3},{3,2},{4,5},{5,4},{6,7},{7,6},{8,9},{9,8},{10,11... | collective-permute-start | bytes 98312 | tf_op jit(solution)/shard_map/ppermute | solution.py:565
  90.0 1.9 %collective-permute-start.4 = (bf16[2,2,8,512]{3,2,1,0:T(8,128)(2,1)S(1)}, bf16[2,2,8,512]{3,2,1,0:T(8,128)(2,1)S(1)}, u32[]{:S(2)}, u32[]{:S(2)}) collective-permute-start(bf16[2,2,8,512]{3,2,1,0:T(8,128)(2,1)S(1)} %shard_map.160.after), channel_id=1, source_target_pairs={{0,31},{1,2},{2,1},{3,4},{4,3},{5,6},{6,5},{7,8},{8,7},{9,10},{10,... | collective-permute-start | bytes 98312 | tf_op jit(solution)/shard_map/ppermute | solution.py:563
  91.9 3.6 %collective-permute-done.4.after_chip.other_chip = bf16[2,2,8,512]{3,2,1,0:T(8,128)(2,1)S(1)} collective-permute-done((bf16[2,2,8,512]{3,2,1,0:T(8,128)(2,1)S(1)}, bf16[2,2,8,512]{3,2,1,0:T(8,128)(2,1)S(1)}, u32[]{:S(2)}, u32[]{:S(2)}) %collective-permute-start.4) | collective-permute-done | bytes 32800 | tf_op jit(solution)/shard_map/ppermute | solution.py:563
  95.5 1.8 %all-to-all-done.3.recv = bf16[16,80,128]{2,1,0:T(8,128)(2,1)S(1)} async-done(((bf16[16,80,128]{2,1,0:T(8,128)(2,1)}), bf16[16,80,128]{2,1,0:T(8,128)(2,1)S(1)}, u32[]{:S(2)}, u32[]{:S(2)}) %all-to-all-start.3) | async-done | bytes 327712 | tf_op jit(solution)/shard_map/all_to_all | solution.py:548
  97.4 23.7 %all_to_all.31.recv = bf16[32,16,128]{2,1,0:T(8,128)(2,1)S(1)} all-to-all(bf16[32,16,128]{2,1,0:T(8,128)(2,1)S(1)} %shard_map.162), channel_id=1, replica_groups=mesh['sweep'=16,'azim'=32] {'azim'}, dimensions={0} | all-to-all | bytes 262144 | tf_op jit(solution)/shard_map/all_to_all | solution.py:570
  121.1 0.7 shard_map.163.after
  121.8 8.1 %all-to-all-start.5 = ((f32[16,16,128]{2,1,0:T(8,128)}), f32[16,16,128]{2,1,0:T(8,128)S(1)}, u32[]{:S(2)}, u32[]{:S(2)}) async-start(f32[16,16,128]{2,1,0:T(8,128)} %shard_map.163.after), calls=%async_computation.5 | async-start | bytes 262144 | tf_op jit(solution)/shard_map/all_to_all | solution.py:575
  129.9 2.4 %shard_map.164 = f32[2,8,32,512]{3,2,1,0:T(8,128)} custom-call(s32[1]{0:T(128)} %bitcast.spot, f32[16,16,128]{2,1,0:T(8,128)} %shard_map.163.after, bf16[2,8,32,512]{3,2,1,0:T(8,128)(2,1)S(1)} %copy-done.2, bf16[2,8,32,512]{3,2,1,0:T(8,128)(2,1)S(1)} %copy-done.1, bf16[16,2,16,512]{3,2,1,0:T(8,128)(2,1)S(1)} %all-to-all-done.2.ret, ...), custom_call_target="tpu_custom_call" | custom-call | flops 10000000 | bytes 4000000 | tf_op jit(solution)/shard_map/pallas_call | solution.py:37
  132.3 4.9 %all-to-all-done.5.recv = f32[16,16,128]{2,1,0:T(8,128)S(1)} async-done(((f32[16,16,128]{2,1,0:T(8,128)}), f32[16,16,128]{2,1,0:T(8,128)S(1)}, u32[]{:S(2)}, u32[]{:S(2)}) %all-to-all-start.5) | async-done | bytes 131104 | tf_op jit(solution)/shard_map/all_to_all | solution.py:575
  137.2 0.7 shard_map.165
  (25 shorter events, 0.2 us)
Async XLA Ops:
  0.6 1.0 copy-start
  2.5 8.1 %copy-start.2 = (bf16[2,8,32,512]{3,2,1,0:T(8,128)(2,1)S(1)}, bf16[2,8,32,512]{3,2,1,0:T(8,128)(2,1)}, u32[]{:S(2)}) copy-start(bf16[2,8,32,512]{3,2,1,0:T(8,128)(2,1)} %lat.9) | copy-start | bytes 1572868
  2.5 25.9 %all-to-all-start.1 = ((bf16[16,2,16,512]{3,2,1,0:T(8,128)(2,1)}), bf16[16,2,16,512]{3,2,1,0:T(8,128)(2,1)S(1)}, u32[]{:S(2)}, u32[]{:S(2)}) async-start(bf16[16,2,16,512]{3,2,1,0:T(8,128)(2,1)} %shard_map.152.after), calls=%async_computation.1 | async-start | bytes 1048576 | tf_op jit(solution)/shard_map/all_to_all | solution.py:469
  10.7 4.9 %copy-start.3 = (f32[9,512]{1,0:T(8,128)S(1)}, f32[9,512]{1,0:T(8,128)}, u32[]{:S(2)}) copy-start(f32[9,512]{1,0:T(8,128)} %taps.1) | copy-start | bytes 55300
  10.7 4.9 %copy-start.4 = (f32[512]{0:T(512)S(1)}, f32[512]{0:T(512)}, u32[]{:S(2)}) copy-start(f32[512]{0:T(512)} %param.12) | copy-start | bytes 6148
  10.7 15.6 %collective-permute-start.1 = (bf16[2,8,512]{2,1,0:T(8,128)(2,1)S(1)}, bf16[2,8,512]{2,1,0:T(8,128)(2,1)S(1)}, u32[]{:S(2)}, u32[]{:S(2)}) collective-permute-start(bf16[2,8,512]{2,1,0:T(8,128)(2,1)S(1)} %shard_map.153.after), channel_id=1, source_target_pairs={{0,31},{1,2},{2,1},{3,4},{4,3},{5,6},{6,5},{7,8},{8,7},{9,10},{10,... | collective-permute-start | bytes 49160 | tf_op jit(solution)/shard_map/ppermute | solution.py:473
  15.7 11.5 %collective-permute-start = (bf16[2,8,512]{2,1,0:T(8,128)(2,1)S(1)}, bf16[2,8,512]{2,1,0:T(8,128)(2,1)S(1)}, u32[]{:S(2)}, u32[]{:S(2)}) collective-permute-start(bf16[2,8,512]{2,1,0:T(8,128)(2,1)S(1)} %get-tuple-element.22), channel_id=1, source_target_pairs={{0,1},{1,0},{2,3},{3,2},{4,5},{5,4},{6,7},{7,6},{8,9},{9,8},{10,11... | collective-permute-start | bytes 49160 | tf_op jit(solution)/shard_map/ppermute | solution.py:483
  27.2 21.4 %copy-start.9 = (f32[512]{0:T(512)S(1)}, f32[512]{0:T(512)}, u32[]{:S(2)}) copy-start(f32[512]{0:T(512)} %param.13) | copy-start | bytes 6148
  28.4 20.2 %copy-start.5 = (bf16[512,256]{1,0:T(8,128)(2,1)S(1)}, bf16[512,256]{1,0:T(8,128)(2,1)}, u32[]{:S(2)}) copy-start(bf16[512,256]{1,0:T(8,128)(2,1)} %w_query.1) | copy-start | bytes 786436
  28.4 20.2 %copy-start.6 = (bf16[512,256]{1,0:T(8,128)(2,1)S(1)}, bf16[512,256]{1,0:T(8,128)(2,1)}, u32[]{:S(2)}) copy-start(bf16[512,256]{1,0:T(8,128)(2,1)} %w_key.1) | copy-start | bytes 786436
  28.4 20.2 %copy-start.7 = (bf16[512,256]{1,0:T(8,128)(2,1)S(1)}, bf16[512,256]{1,0:T(8,128)(2,1)}, u32[]{:S(2)}) copy-start(bf16[512,256]{1,0:T(8,128)(2,1)} %w_value.1) | copy-start | bytes 786436
  28.4 20.1 %copy-start.8 = (bf16[512,256]{1,0:T(8,128)(2,1)S(1)}, bf16[512,256]{1,0:T(8,128)(2,1)}, u32[]{:S(2)}) copy-start(bf16[512,256]{1,0:T(8,128)(2,1)} %w_output.1) | copy-start | bytes 786436
  55.5 21.8 %all-to-all-start.2 = ((bf16[16,2,16,512]{3,2,1,0:T(8,128)(2,1)}), bf16[16,2,16,512]{3,2,1,0:T(8,128)(2,1)S(1)}, u32[]{:S(2)}, u32[]{:S(2)}) async-start(bf16[16,2,16,512]{3,2,1,0:T(8,128)(2,1)} %get-tuple-element.24), calls=%async_computation.2 | async-start | bytes 1048576 | tf_op jit(solution)/shard_map/all_to_all | solution.py:520
  59.4 7.3 %collective-permute-start.2 = (bf16[2,16,64,128]{3,2,1,0:T(8,128)(2,1)S(1)}, bf16[2,16,64,128]{3,2,1,0:T(8,128)(2,1)S(1)}, u32[]{:S(2)}, u32[]{:S(2)}) collective-permute-start(bf16[2,16,64,128]{3,2,1,0:T(8,128)(2,1)S(1)} %slice_bitcast_fusion), channel_id=1, source_target_pairs={{0,1},{1,0},{2,3},{3,2},{4,5},{5,4},{6,7},{7,6},{8,9},{9,8},{10,11... | collective-permute-start | bytes 1572872 | tf_op jit(solution)/shard_map/ppermute | solution.py:521
  66.9 10.4 %copy-start.1 = (bf16[2,8,32,512]{3,2,1,0:T(8,128)(2,1)S(1)}, bf16[2,8,32,512]{3,2,1,0:T(8,128)(2,1)}, u32[]{:S(2)}) copy-start(bf16[2,8,32,512]{3,2,1,0:T(8,128)(2,1)} %cot.9) | copy-start | bytes 1572868
  66.9 9.5 %collective-permute-start.3 = (bf16[16,64,128]{2,1,0:T(8,128)(2,1)S(1)}, bf16[16,64,128]{2,1,0:T(8,128)(2,1)S(1)}, u32[]{:S(2)}, u32[]{:S(2)}) collective-permute-start(bf16[16,64,128]{2,1,0:T(8,128)(2,1)S(1)} %get-tuple-element.28), channel_id=1, source_target_pairs={{0,2},{1,3},{2,0},{3,1},{4,6},{5,7},{6,4},{7,5},{8,10},{9,11},{10,... | collective-permute-start | bytes 786440 | tf_op jit(solution)/shard_map/ppermute | solution.py:524
  79.2 18.2 %all-to-all-start.3 = ((bf16[16,80,128]{2,1,0:T(8,128)(2,1)}), bf16[16,80,128]{2,1,0:T(8,128)(2,1)S(1)}, u32[]{:S(2)}, u32[]{:S(2)}) async-start(bf16[16,80,128]{2,1,0:T(8,128)(2,1)} %shard_map.159.after), calls=%async_computation.3 | async-start | bytes 655360 | tf_op jit(solution)/shard_map/all_to_all | solution.py:548
  86.6 5.3 %collective-permute-start.5 = (bf16[2,2,8,512]{3,2,1,0:T(8,128)(2,1)S(1)}, bf16[2,2,8,512]{3,2,1,0:T(8,128)(2,1)S(1)}, u32[]{:S(2)}, u32[]{:S(2)}) collective-permute-start(bf16[2,2,8,512]{3,2,1,0:T(8,128)(2,1)S(1)} %shard_map.161), channel_id=1, source_target_pairs={{0,1},{1,0},{2,3},{3,2},{4,5},{5,4},{6,7},{7,6},{8,9},{9,8},{10,11... | collective-permute-start | bytes 98312 | tf_op jit(solution)/shard_map/ppermute | solution.py:565
  90.0 5.5 %collective-permute-start.4 = (bf16[2,2,8,512]{3,2,1,0:T(8,128)(2,1)S(1)}, bf16[2,2,8,512]{3,2,1,0:T(8,128)(2,1)S(1)}, u32[]{:S(2)}, u32[]{:S(2)}) collective-permute-start(bf16[2,2,8,512]{3,2,1,0:T(8,128)(2,1)S(1)} %shard_map.160.after), channel_id=1, source_target_pairs={{0,31},{1,2},{2,1},{3,4},{4,3},{5,6},{6,5},{7,8},{8,7},{9,10},{10,... | collective-permute-start | bytes 98312 | tf_op jit(solution)/shard_map/ppermute | solution.py:563
  121.8 15.3 %all-to-all-start.5 = ((f32[16,16,128]{2,1,0:T(8,128)}), f32[16,16,128]{2,1,0:T(8,128)S(1)}, u32[]{:S(2)}, u32[]{:S(2)}) async-start(f32[16,16,128]{2,1,0:T(8,128)} %shard_map.163.after), calls=%async_computation.5 | async-start | bytes 262144 | tf_op jit(solution)/shard_map/all_to_all | solution.py:575

commit v7 on v6

--- a/solution.py
+++ b/solution.py
@@ -569,11 +569,6 @@
     )(spot, first_recv, back_chip, back_core)
     second_recv = lax.all_to_all(second_sent, "azim", split_axis=0, concat_axis=0, tiled=True)
 
-    third_sent = call(third_kernel, struct((GROUPS, 16, LANES), F32), 16, moved=300_000)(
-        second_recv
-    )
-    third_recv = lax.all_to_all(third_sent, "sweep", split_axis=0, concat_axis=0, tiled=True)
-
     grad_latents = call(
         latents_kernel,
         struct((SL, H, WL, C), F32),
@@ -583,7 +578,13 @@
         smem=1,
         hbm=(1,),
         scratch=[edge, edge],
-    )(spot, third_sent, latents, cotangent, ret, back_core, back_chip, table)
+    )(spot, second_sent, latents, cotangent, ret, back_core, back_chip, table)
+    second_recv, grad_latents = lax.optimization_barrier((second_recv, grad_latents))
+
+    third_sent = call(third_kernel, struct((GROUPS, 16, LANES), F32), 16, moved=300_000)(
+        second_recv
+    )
+    third_recv = lax.all_to_all(third_sent, "sweep", split_axis=0, concat_axis=0, tiled=True)
 
     share = struct((C // strips, HD), F32)
     line = struct((1, C), F32)

time: 139 us -> 139 us (level)
  blocking collectives: 43.8 us -> 35.2 us
  waiting for transfers between devices: 20.1 us -> 25 us
  starting transfers between devices: 56 us -> 59.7 us
    all_to_all x1, blocking collectives: 23.7 us -> 15.1 us  [on_device(): lax.all_to_all(third_sent, 'sweep', split_axis=0, concat_axis=0, tiled=True)]
    all_to_all x1, waiting for transfers between devices: 4.9 us -> 9.74 us  [on_device(): lax.all_to_all(second_sent, 'azim', split_axis=0, concat_axis=0, tiled=True)]
    all_to_all x1, starting transfers between devices: 8.07 us -> 11.8 us  [on_device(): lax.all_to_all(second_sent, 'azim', split_axis=0, concat_axis=0, tiled=True)]
where the time goes in v7:
time: 139 us; the launch traced here: 138 us
  starting transfers between devices  59.7 us (43%)
  blocking collectives  35.2 us (25%)
  waiting for transfers between devices  25 us (18%)
  Pallas kernels  15.9 us (11%)
    all_to_all x1, blocking collectives, on_device(): lax.all_to_all(sent, 'sweep', split_axis=0, concat_axis=0, tiled=True)  20.1 us
    all_to_all x1, blocking collectives, on_device(): lax.all_to_all(third_sent, 'sweep', split_axis=0, concat_axis=0, tiled=True)  15.1 us
    pallas_call x13, Pallas kernels, run(): pl.pallas_call(kernel, out_shape=outs, in_specs=specs, out_specs=jax.tree...  13.9 us
    all_to_all x1, starting transfers between devices, on_device(): lax.all_to_all(second_sent, 'azim', split_axis=0, concat_axis=0, tiled=True)  11.8 us
    ppermute x1, starting transfers between devices, on_device(): other_core = lax.ppermute(to_core, 'azim', cores)  10.7 us
    all_to_all x1, waiting for transfers between devices, on_device(): lax.all_to_all(second_sent, 'azim', split_axis=0, concat_axis=0, tiled=True)  9.74 us
    all_to_all x1, starting transfers between devices, on_device(): lax.all_to_all(cot_sent, 'sweep', split_axis=0, concat_axis=0, tiled=True)  8.12 us
    ppermute x1, waiting for transfers between devices, on_device(): from_chip = lax.ppermute(send, 'azim', sides)  7.49 us
  transfers between devices with their start and end apart: 10, of which 6 were waited for; matrix products, arithmetic and copies ran while one was open for 0% of the time, Pallas kernels for 3%

profile of v7, /device:TPU:1, one launch (start us, length us, event | category | flops | bytes accessed | tf_op | source)
XLA Modules:
  0.0 137.8 jit_solution(7836546299423560019)
XLA Ops:
  0.6 1.0 copy-done
  1.7 0.8 shard_map.152.after
  2.5 8.1 %all-to-all-start.1 = ((bf16[16,2,16,512]{3,2,1,0:T(8,128)(2,1)}), bf16[16,2,16,512]{3,2,1,0:T(8,128)(2,1)S(1)}, u32[]{:S(2)}, u32[]{:S(2)}) async-start(bf16[16,2,16,512]{3,2,1,0:T(8,128)(2,1)} %shard_map.152.after), calls=%async_computation.1 | async-start | bytes 1048576 | tf_op jit(solution)/shard_map/all_to_all | solution.py:469
  10.7 0.1 shard_map.153.after
  10.7 4.8 %collective-permute-start.1 = (bf16[2,8,512]{2,1,0:T(8,128)(2,1)S(1)}, bf16[2,8,512]{2,1,0:T(8,128)(2,1)S(1)}, u32[]{:S(2)}, u32[]{:S(2)}) collective-permute-start(bf16[2,8,512]{2,1,0:T(8,128)(2,1)S(1)} %shard_map.153.after), channel_id=1, source_target_pairs={{0,31},{1,2},{2,1},{3,4},{4,3},{5,6},{6,5},{7,8},{8,7},{9,10},{10,... | collective-permute-start | bytes 49160 | tf_op jit(solution)/shard_map/ppermute | solution.py:473
  15.6 0.1 shard_map.154
  15.7 10.7 %collective-permute-start = (bf16[2,8,512]{2,1,0:T(8,128)(2,1)S(1)}, bf16[2,8,512]{2,1,0:T(8,128)(2,1)S(1)}, u32[]{:S(2)}, u32[]{:S(2)}) collective-permute-start(bf16[2,8,512]{2,1,0:T(8,128)(2,1)S(1)} %get-tuple-element.24), channel_id=1, source_target_pairs={{0,1},{1,0},{2,3},{3,2},{4,5},{5,4},{6,7},{7,6},{8,9},{9,8},{10,11... | collective-permute-start | bytes 49160 | tf_op jit(solution)/shard_map/ppermute | solution.py:483
  26.4 0.8 collective-permute-done.other_core
  27.2 1.2 shard_map.155
  28.5 20.1 %all_to_all.30.recv = bf16[16,2,16,512]{3,2,1,0:T(8,128)(2,1)S(1)} all-to-all(bf16[16,2,16,512]{3,2,1,0:T(8,128)(2,1)S(1)} %shard_map.155), channel_id=1, replica_groups=mesh['sweep'=16,'azim'=32] {'sweep'}, dimensions={0} | all-to-all | bytes 1048576 | tf_op jit(solution)/shard_map/all_to_all | solution.py:494
  48.6 6.9 %shard_map.156 = (bf16[16,2,16,512]{3,2,1,0:T(8,128)(2,1)}, bf16[2,2,16,64,128]{4,3,2,1,0:T(8,128)(2,1)S(1)}, f32[1,512]{1,0:T(1,128)S(1)}) custom-call(s32[1]{0:T(128)} %bitcast.spot, bf16[16,2,16,512]{3,2,1,0:T(8,128)(2,1)S(1)} %all_to_all.30.recv, bf16[16,2,16,512]{3,2,1,0:T(8,128)(2,1)S(1)} %all-to-all-done.1.recv_cot, bf16[512,256]{1,0:T(8,128)(2,1)S(1)} %copy-done.5, ...), custom_call_target="tpu_custom_call" | custom-call | flops 2000000000 | bytes 6000000 | tf_op jit(solution)/shard_map/pallas_call | solution.py:37
  55.5 3.9 %all-to-all-start.2 = ((bf16[16,2,16,512]{3,2,1,0:T(8,128)(2,1)}), bf16[16,2,16,512]{3,2,1,0:T(8,128)(2,1)S(1)}, u32[]{:S(2)}, u32[]{:S(2)}) async-start(bf16[16,2,16,512]{3,2,1,0:T(8,128)(2,1)} %get-tuple-element.26), calls=%async_computation.2 | async-start | bytes 1048576 | tf_op jit(solution)/shard_map/all_to_all | solution.py:520
  59.4 5.8 %collective-permute-start.2 = (bf16[2,16,64,128]{3,2,1,0:T(8,128)(2,1)S(1)}, bf16[2,16,64,128]{3,2,1,0:T(8,128)(2,1)S(1)}, u32[]{:S(2)}, u32[]{:S(2)}) collective-permute-start(bf16[2,16,64,128]{3,2,1,0:T(8,128)(2,1)S(1)} %slice_bitcast_fusion), channel_id=1, source_target_pairs={{0,1},{1,0},{2,3},{3,2},{4,5},{5,4},{6,7},{7,6},{8,9},{9,8},{10,11... | collective-permute-start | bytes 1572872 | tf_op jit(solution)/shard_map/ppermute | solution.py:521
  65.2 1.5 %collective-permute-done.2.got = bf16[2,16,64,128]{3,2,1,0:T(8,128)(2,1)S(1)} collective-permute-done((bf16[2,16,64,128]{3,2,1,0:T(8,128)(2,1)S(1)}, bf16[2,16,64,128]{3,2,1,0:T(8,128)(2,1)S(1)}, u32[]{:S(2)}, u32[]{:S(2)}) %collective-permute-start.2) | collective-permute-done | bytes 524320 | tf_op jit(solution)/shard_map/ppermute | solution.py:521
  66.7 0.1 shard_map.157
  66.9 2.1 %collective-permute-start.3 = (bf16[16,64,128]{2,1,0:T(8,128)(2,1)S(1)}, bf16[16,64,128]{2,1,0:T(8,128)(2,1)S(1)}, u32[]{:S(2)}, u32[]{:S(2)}) collective-permute-start(bf16[16,64,128]{2,1,0:T(8,128)(2,1)S(1)} %get-tuple-element.30), channel_id=1, source_target_pairs={{0,2},{1,3},{2,0},{3,1},{4,6},{5,7},{6,4},{7,5},{8,10},{9,11},{10,... | collective-permute-start | bytes 786440 | tf_op jit(solution)/shard_map/ppermute | solution.py:524
  68.9 7.5 %collective-permute-done.3.got = bf16[16,64,128]{2,1,0:T(8,128)(2,1)S(1)} collective-permute-done((bf16[16,64,128]{2,1,0:T(8,128)(2,1)S(1)}, bf16[16,64,128]{2,1,0:T(8,128)(2,1)S(1)}, u32[]{:S(2)}, u32[]{:S(2)}) %collective-permute-start.3) | collective-permute-done | bytes 262176 | tf_op jit(solution)/shard_map/ppermute | solution.py:524
  76.4 0.8 shard_map.158.sums_in
  77.2 2.0 %shard_map.159.after = bf16[16,80,128]{2,1,0:T(8,128)(2,1)} custom-call(s32[1]{0:T(128)} %bitcast.spot, bf16[2,8,32,512]{3,2,1,0:T(8,128)(2,1)S(1)} %copy-done.2, bf16[2,8,512]{2,1,0:T(8,128)(2,1)S(1)} %collective-permute-done.other_core, bf16[2,8,512]{2,1,0:T(8,128)(2,1)S(1)} %collective-permute-done.1.other_chip, ...), custom_call_target="tpu_custom_call", output_to_operand_aliasing={{}: (7, {})} | custom-call | flops 10000000 | bytes 2000000 | tf_op jit(solution)/shard_map/pallas_call | solution.py:530
  79.2 7.2 %all-to-all-start.3 = ((bf16[16,80,128]{2,1,0:T(8,128)(2,1)}), bf16[16,80,128]{2,1,0:T(8,128)(2,1)S(1)}, u32[]{:S(2)}, u32[]{:S(2)}) async-start(bf16[16,80,128]{2,1,0:T(8,128)(2,1)} %shard_map.159.after), calls=%async_computation.3 | async-start | bytes 655360 | tf_op jit(solution)/shard_map/all_to_all | solution.py:548
  86.4 0.1 shard_map.160.after
  86.5 0.1 shard_map.161
  86.6 3.4 %collective-permute-start.5 = (bf16[2,2,8,512]{3,2,1,0:T(8,128)(2,1)S(1)}, bf16[2,2,8,512]{3,2,1,0:T(8,128)(2,1)S(1)}, u32[]{:S(2)}, u32[]{:S(2)}) collective-permute-start(bf16[2,2,8,512]{3,2,1,0:T(8,128)(2,1)S(1)} %shard_map.161), channel_id=1, source_target_pairs={{0,1},{1,0},{2,3},{3,2},{4,5},{5,4},{6,7},{7,6},{8,9},{9,8},{10,11... | collective-permute-start | bytes 98312 | tf_op jit(solution)/shard_map/ppermute | solution.py:565
  90.0 1.9 %collective-permute-start.4 = (bf16[2,2,8,512]{3,2,1,0:T(8,128)(2,1)S(1)}, bf16[2,2,8,512]{3,2,1,0:T(8,128)(2,1)S(1)}, u32[]{:S(2)}, u32[]{:S(2)}) collective-permute-start(bf16[2,2,8,512]{3,2,1,0:T(8,128)(2,1)S(1)} %shard_map.160.after), channel_id=1, source_target_pairs={{0,31},{1,2},{2,1},{3,4},{4,3},{5,6},{6,5},{7,8},{8,7},{9,10},{10,... | collective-permute-start | bytes 98312 | tf_op jit(solution)/shard_map/ppermute | solution.py:563
  91.9 3.6 %collective-permute-done.4.after_chip.other_chip = bf16[2,2,8,512]{3,2,1,0:T(8,128)(2,1)S(1)} collective-permute-done((bf16[2,2,8,512]{3,2,1,0:T(8,128)(2,1)S(1)}, bf16[2,2,8,512]{3,2,1,0:T(8,128)(2,1)S(1)}, u32[]{:S(2)}, u32[]{:S(2)}) %collective-permute-start.4) | collective-permute-done | bytes 32800 | tf_op jit(solution)/shard_map/ppermute | solution.py:563
  95.5 1.8 %all-to-all-done.3.recv = bf16[16,80,128]{2,1,0:T(8,128)(2,1)S(1)} async-done(((bf16[16,80,128]{2,1,0:T(8,128)(2,1)}), bf16[16,80,128]{2,1,0:T(8,128)(2,1)S(1)}, u32[]{:S(2)}, u32[]{:S(2)}) %all-to-all-start.3) | async-done | bytes 327712 | tf_op jit(solution)/shard_map/all_to_all | solution.py:548
  97.4 0.7 shard_map.162.after
  98.1 11.8 %all-to-all-start.4 = ((bf16[32,16,128]{2,1,0:T(8,128)(2,1)}), bf16[32,16,128]{2,1,0:T(8,128)(2,1)S(1)}, u32[]{:S(2)}, u32[]{:S(2)}) async-start(bf16[32,16,128]{2,1,0:T(8,128)(2,1)} %shard_map.162.after), calls=%async_computation.4 | async-start | bytes 262144 | tf_op jit(solution)/shard_map/all_to_all | solution.py:570
  109.9 2.4 %shard_map.163 = f32[2,8,32,512]{3,2,1,0:T(8,128)} custom-call(s32[1]{0:T(128)} %bitcast.spot, bf16[32,16,128]{2,1,0:T(8,128)(2,1)} %shard_map.162.after, bf16[2,8,32,512]{3,2,1,0:T(8,128)(2,1)S(1)} %copy-done.2, bf16[2,8,32,512]{3,2,1,0:T(8,128)(2,1)S(1)} %copy-done.1, bf16[16,2,16,512]{3,2,1,0:T(8,128)(2,1)S(1)} %all-to-all-done.2.ret, ...), custom_call_target="tpu_custom_call" | custom-call | flops 10000000 | bytes 4000000 | tf_op jit(solution)/shard_map/pallas_call | solution.py:37
  112.3 9.7 %all-to-all-done.4.recv = bf16[32,16,128]{2,1,0:T(8,128)(2,1)S(1)} async-done(((bf16[32,16,128]{2,1,0:T(8,128)(2,1)}), bf16[32,16,128]{2,1,0:T(8,128)(2,1)S(1)}, u32[]{:S(2)}, u32[]{:S(2)}) %all-to-all-start.4) | async-done | bytes 131104 | tf_op jit(solution)/shard_map/all_to_all | solution.py:570
  122.1 15.1 %all_to_all.31.recv = f32[16,16,128]{2,1,0:T(8,128)S(1)} all-to-all(f32[16,16,128]{2,1,0:T(8,128)S(1)} %shard_map.164), channel_id=1, replica_groups=mesh['sweep'=16,'azim'=32] {'sweep'}, dimensions={0} | all-to-all | bytes 262144 | tf_op jit(solution)/shard_map/all_to_all | solution.py:587
  137.2 0.7 shard_map.165
  (25 shorter events, 0.1 us)
Async XLA Ops:
  0.6 1.0 copy-start
  2.5 8.1 %copy-start.2 = (bf16[2,8,32,512]{3,2,1,0:T(8,128)(2,1)S(1)}, bf16[2,8,32,512]{3,2,1,0:T(8,128)(2,1)}, u32[]{:S(2)}) copy-start(bf16[2,8,32,512]{3,2,1,0:T(8,128)(2,1)} %lat.9) | copy-start | bytes 1572868
  2.5 25.9 %all-to-all-start.1 = ((bf16[16,2,16,512]{3,2,1,0:T(8,128)(2,1)}), bf16[16,2,16,512]{3,2,1,0:T(8,128)(2,1)S(1)}, u32[]{:S(2)}, u32[]{:S(2)}) async-start(bf16[16,2,16,512]{3,2,1,0:T(8,128)(2,1)} %shard_map.152.after), calls=%async_computation.1 | async-start | bytes 1048576 | tf_op jit(solution)/shard_map/all_to_all | solution.py:469
  10.7 4.9 %copy-start.3 = (f32[9,512]{1,0:T(8,128)S(1)}, f32[9,512]{1,0:T(8,128)}, u32[]{:S(2)}) copy-start(f32[9,512]{1,0:T(8,128)} %taps.1) | copy-start | bytes 55300
  10.7 4.9 %copy-start.4 = (f32[512]{0:T(512)S(1)}, f32[512]{0:T(512)}, u32[]{:S(2)}) copy-start(f32[512]{0:T(512)} %param.12) | copy-start | bytes 6148
  10.7 15.6 %collective-permute-start.1 = (bf16[2,8,512]{2,1,0:T(8,128)(2,1)S(1)}, bf16[2,8,512]{2,1,0:T(8,128)(2,1)S(1)}, u32[]{:S(2)}, u32[]{:S(2)}) collective-permute-start(bf16[2,8,512]{2,1,0:T(8,128)(2,1)S(1)} %shard_map.153.after), channel_id=1, source_target_pairs={{0,31},{1,2},{2,1},{3,4},{4,3},{5,6},{6,5},{7,8},{8,7},{9,10},{10,... | collective-permute-start | bytes 49160 | tf_op jit(solution)/shard_map/ppermute | solution.py:473
  15.7 11.5 %collective-permute-start = (bf16[2,8,512]{2,1,0:T(8,128)(2,1)S(1)}, bf16[2,8,512]{2,1,0:T(8,128)(2,1)S(1)}, u32[]{:S(2)}, u32[]{:S(2)}) collective-permute-start(bf16[2,8,512]{2,1,0:T(8,128)(2,1)S(1)} %get-tuple-element.24), channel_id=1, source_target_pairs={{0,1},{1,0},{2,3},{3,2},{4,5},{5,4},{6,7},{7,6},{8,9},{9,8},{10,11... | collective-permute-start | bytes 49160 | tf_op jit(solution)/shard_map/ppermute | solution.py:483
  27.2 21.4 %copy-start.9 = (f32[512]{0:T(512)S(1)}, f32[512]{0:T(512)}, u32[]{:S(2)}) copy-start(f32[512]{0:T(512)} %param.13) | copy-start | bytes 6148
  28.4 20.2 %copy-start.5 = (bf16[512,256]{1,0:T(8,128)(2,1)S(1)}, bf16[512,256]{1,0:T(8,128)(2,1)}, u32[]{:S(2)}) copy-start(bf16[512,256]{1,0:T(8,128)(2,1)} %w_query.1) | copy-start | bytes 786436
  28.4 20.2 %copy-start.6 = (bf16[512,256]{1,0:T(8,128)(2,1)S(1)}, bf16[512,256]{1,0:T(8,128)(2,1)}, u32[]{:S(2)}) copy-start(bf16[512,256]{1,0:T(8,128)(2,1)} %w_key.1) | copy-start | bytes 786436
  28.4 20.2 %copy-start.7 = (bf16[512,256]{1,0:T(8,128)(2,1)S(1)}, bf16[512,256]{1,0:T(8,128)(2,1)}, u32[]{:S(2)}) copy-start(bf16[512,256]{1,0:T(8,128)(2,1)} %w_value.1) | copy-start | bytes 786436
  28.4 20.1 %copy-start.8 = (bf16[512,256]{1,0:T(8,128)(2,1)S(1)}, bf16[512,256]{1,0:T(8,128)(2,1)}, u32[]{:S(2)}) copy-start(bf16[512,256]{1,0:T(8,128)(2,1)} %w_output.1) | copy-start | bytes 786436
  55.5 21.8 %all-to-all-start.2 = ((bf16[16,2,16,512]{3,2,1,0:T(8,128)(2,1)}), bf16[16,2,16,512]{3,2,1,0:T(8,128)(2,1)S(1)}, u32[]{:S(2)}, u32[]{:S(2)}) async-start(bf16[16,2,16,512]{3,2,1,0:T(8,128)(2,1)} %get-tuple-element.26), calls=%async_computation.2 | async-start | bytes 1048576 | tf_op jit(solution)/shard_map/all_to_all | solution.py:520
  59.4 7.3 %collective-permute-start.2 = (bf16[2,16,64,128]{3,2,1,0:T(8,128)(2,1)S(1)}, bf16[2,16,64,128]{3,2,1,0:T(8,128)(2,1)S(1)}, u32[]{:S(2)}, u32[]{:S(2)}) collective-permute-start(bf16[2,16,64,128]{3,2,1,0:T(8,128)(2,1)S(1)} %slice_bitcast_fusion), channel_id=1, source_target_pairs={{0,1},{1,0},{2,3},{3,2},{4,5},{5,4},{6,7},{7,6},{8,9},{9,8},{10,11... | collective-permute-start | bytes 1572872 | tf_op jit(solution)/shard_map/ppermute | solution.py:521
  66.9 10.4 %copy-start.1 = (bf16[2,8,32,512]{3,2,1,0:T(8,128)(2,1)S(1)}, bf16[2,8,32,512]{3,2,1,0:T(8,128)(2,1)}, u32[]{:S(2)}) copy-start(bf16[2,8,32,512]{3,2,1,0:T(8,128)(2,1)} %cot.9) | copy-start | bytes 1572868
  66.9 9.5 %collective-permute-start.3 = (bf16[16,64,128]{2,1,0:T(8,128)(2,1)S(1)}, bf16[16,64,128]{2,1,0:T(8,128)(2,1)S(1)}, u32[]{:S(2)}, u32[]{:S(2)}) collective-permute-start(bf16[16,64,128]{2,1,0:T(8,128)(2,1)S(1)} %get-tuple-element.30), channel_id=1, source_target_pairs={{0,2},{1,3},{2,0},{3,1},{4,6},{5,7},{6,4},{7,5},{8,10},{9,11},{10,... | collective-permute-start | bytes 786440 | tf_op jit(solution)/shard_map/ppermute | solution.py:524
  79.2 18.2 %all-to-all-start.3 = ((bf16[16,80,128]{2,1,0:T(8,128)(2,1)}), bf16[16,80,128]{2,1,0:T(8,128)(2,1)S(1)}, u32[]{:S(2)}, u32[]{:S(2)}) async-start(bf16[16,80,128]{2,1,0:T(8,128)(2,1)} %shard_map.159.after), calls=%async_computation.3 | async-start | bytes 655360 | tf_op jit(solution)/shard_map/all_to_all | solution.py:548
  86.6 5.3 %collective-permute-start.5 = (bf16[2,2,8,512]{3,2,1,0:T(8,128)(2,1)S(1)}, bf16[2,2,8,512]{3,2,1,0:T(8,128)(2,1)S(1)}, u32[]{:S(2)}, u32[]{:S(2)}) collective-permute-start(bf16[2,2,8,512]{3,2,1,0:T(8,128)(2,1)S(1)} %shard_map.161), channel_id=1, source_target_pairs={{0,1},{1,0},{2,3},{3,2},{4,5},{5,4},{6,7},{7,6},{8,9},{9,8},{10,11... | collective-permute-start | bytes 98312 | tf_op jit(solution)/shard_map/ppermute | solution.py:565
  90.0 5.5 %collective-permute-start.4 = (bf16[2,2,8,512]{3,2,1,0:T(8,128)(2,1)S(1)}, bf16[2,2,8,512]{3,2,1,0:T(8,128)(2,1)S(1)}, u32[]{:S(2)}, u32[]{:S(2)}) collective-permute-start(bf16[2,2,8,512]{3,2,1,0:T(8,128)(2,1)S(1)} %shard_map.160.after), channel_id=1, source_target_pairs={{0,31},{1,2},{2,1},{3,4},{4,3},{5,6},{6,5},{7,8},{8,7},{9,10},{10,... | collective-permute-start | bytes 98312 | tf_op jit(solution)/shard_map/ppermute | solution.py:563
  98.1 23.9 %all-to-all-start.4 = ((bf16[32,16,128]{2,1,0:T(8,128)(2,1)}), bf16[32,16,128]{2,1,0:T(8,128)(2,1)S(1)}, u32[]{:S(2)}, u32[]{:S(2)}) async-start(bf16[32,16,128]{2,1,0:T(8,128)(2,1)} %shard_map.162.after), calls=%async_computation.4 | async-start | bytes 262144 | tf_op jit(solution)/shard_map/all_to_all | solution.py:570

commit v8 on v7

--- a/solution.py
+++ b/solution.py
@@ -212,35 +212,40 @@
             [jnp.where(lane < DH, value, zero), jnp.where(lane >= DH, value, zero)], axis=0
         )
 
-    for group in range(4):
-        at = pl.ds(group * rows_each, rows_each)
-        for pair in range(2):
-            def part(index):
-                return qkv[at, pl.ds(index * HD + pair * LANES, LANES)]
-
-            lanes = pl.ds(pair * LANES, LANES)
-            query, key, value = part(0), part(1), part(2)
-            grad_att = gatt[at, lanes]
-            key2, value2 = split(key), split(value)
-            scores = nt(query, key2)
-            grad_probs = nt(grad_att, value2)
-            lows, grads = [], []
-            for head in range(2):
-                cut = slice(head * rows_each, (head + 1) * rows_each)
-                score = jnp.where(same, scores[:, cut] * scale, MASKED)
-                expon = jnp.exp(score - jnp.max(score, axis=-1, keepdims=True))
-                probs = expon * (1.0 / jnp.sum(expon, axis=-1, keepdims=True))
-                gp = grad_probs[:, cut]
-                weighted = probs * gp
-                total = jnp.sum(weighted, axis=-1, keepdims=True)
-                lows.append(probs.astype(BF16))
-                grads.append(((weighted - probs * total) * scale).astype(BF16))
-            attended[at, lanes] = nn(jnp.concatenate(lows, axis=1), value2).astype(BF16)
-            grad_q = nn(jnp.concatenate(grads, axis=1), key2)
-            grad_k = tn(jnp.concatenate(grads, axis=0), split(query))
-            grad_v = tn(jnp.concatenate(lows, axis=0), split(grad_att))
-            for index, grad in enumerate((grad_q, grad_k, grad_v)):
-                stacked[at, pl.ds(index * HD + pair * LANES, LANES)] = grad.astype(BF16)
+    units = [
+        (pl.ds(group * rows_each, rows_each), pair * LANES)
+        for group in range(4)
+        for pair in range(2)
+    ]
+
+    def part(unit, index):
+        return qkv[unit[0], pl.ds(index * HD + unit[1], LANES)]
+
+    scores = [nt(split(part(unit, 1)), part(unit, 0)) for unit in units]
+    grad_probs = [
+        nt(split(part(unit, 2)), gatt[unit[0], pl.ds(unit[1], LANES)]) for unit in units
+    ]
+    results = []
+    for score2, grad2 in zip(scores, grad_probs):
+        lows, grads = [], []
+        for head in range(2):
+            cut = slice(head * rows_each, (head + 1) * rows_each)
+            score = jnp.where(same, score2[cut] * scale, MASKED)
+            expon = jnp.exp(score - jnp.max(score, axis=0, keepdims=True))
+            probs = expon * (1.0 / jnp.sum(expon, axis=0, keepdims=True))
+            weighted = probs * grad2[cut]
+            total = jnp.sum(weighted, axis=0, keepdims=True)
+            lows.append(probs.astype(BF16))
+            grads.append(((weighted - probs * total) * scale).astype(BF16))
+        results.append((lows, grads))
+    for unit, (lows, grads) in zip(units, results):
+        at, lanes = unit[0], pl.ds(unit[1], LANES)
+        attended[at, lanes] = tn(jnp.concatenate(lows, axis=0), split(part(unit, 2))).astype(BF16)
+        grad_q = tn(jnp.concatenate(grads, axis=0), split(part(unit, 1)))
+        grad_k = nn(jnp.concatenate(grads, axis=1), split(part(unit, 0)))
+        grad_v = nn(jnp.concatenate(lows, axis=1), split(gatt[at, lanes]))
+        for index, grad in enumerate((grad_q, grad_k, grad_v)):
+            stacked[at, pl.ds(index * HD + unit[1], LANES)] = grad.astype(BF16)
 
     gnorm[...] = (
         nt(stacked[:, :HD], w_query[...])
@@ -401,15 +406,17 @@
             out[s, h, :, here] = grads[h] + total * (sig * (1.0 + value * (1.0 - sig)))
 
 
-def second_kernel(spot, recv, after_chip, after_core, out):
-    del after_chip, after_core
+def high_low(value):
+    high = value.astype(BF16).astype(F32)
+    at = lax.broadcasted_iota(jnp.int32, value.shape, 0)
+    return jnp.where(at < 4, high, pltpu.roll(value - high, 4, 0))
+
+
+def second_kernel(spot, recv, out):
     total = jnp.sum(recv[...].astype(F32), axis=0)
     weights = total[:ROWS].reshape(8, 8, LANES)
     taps = total[ROWS : ROWS + 8] + total[ROWS + 8 :]
-    high = taps.astype(BF16).astype(F32)
-    low = taps - high
-    at = lax.broadcasted_iota(jnp.int32, (8, LANES), 0)
-    both = jnp.where(at < 4, high, pltpu.roll(low, 4, 0))
+    both = high_low(taps)
     for z in range(2):
         for core in range(2):
             own = jnp.where(jnp.logical_and(core_of(spot) == core, side_of(spot) == z), 1.0, 0.0)
@@ -422,8 +429,8 @@
 def third_kernel(recv, out):
     total = jnp.sum(recv[...].astype(F32), axis=0)
     both = total[8:]
-    taps = both + pltpu.roll(both, 4, 0)
-    result = jnp.concatenate([total[:8], taps], axis=0)
+    result = jnp.concatenate([total[:8], high_low(both + pltpu.roll(both, 4, 0))], axis=0)
+    result = result.astype(BF16)
     for s in range(GROUPS):
         out[s] = result
 
@@ -431,20 +438,19 @@
 def unpack_kernel(recv, kernel_out, bias_out, gain_out, *outs):
     for part in range(PARTS):
         here = slice(part * LANES, (part + 1) * LANES)
-        for r in range(11):
-            row = recv[4 * part + r // 3, 8 + r % 3 : 9 + r % 3, :]
-            if r < 9:
-                kernel_out[r : r + 1, here] = row
-            elif r == 9:
-                bias_out[:, here] = row
+        for group in range(4):
+            both = recv[4 * part + group].astype(F32)[8:]
+            taps = both + pltpu.roll(both, 4, 0)
+            if group < 3:
+                kernel_out[3 * group : 3 * group + 3, here] = taps[:3]
             else:
-                gain_out[:, here] = row
+                bias_out[:, here] = taps[:1]
+                gain_out[:, here] = taps[1:2]
     for m in range(4):
         for high in range(2):
             for side in range(2):
-                outs[m][8 * high : 8 * high + 8, side * LANES : (side + 1) * LANES] = recv[
-                    4 * m + 2 * high + side, :8, :
-                ]
+                piece = recv[4 * m + 2 * high + side].astype(F32)[:8]
+                outs[m][8 * high : 8 * high + 8, side * LANES : (side + 1) * LANES] = piece
 
 
 def on_device(
@@ -546,6 +552,11 @@
         ),
     )(spot, latents, other_core, other_chip, cotangent, ret, gain_sum, sums)
     first_recv = lax.all_to_all(first_sent, "sweep", split_axis=0, concat_axis=0, tiled=True)
+    second_sent = call(
+        second_kernel, struct((strips, 16, LANES), BF16), 16, moved=1_000_000, smem=1
+    )(spot, first_recv)
+    second_recv = lax.all_to_all(second_sent, "azim", split_axis=0, concat_axis=0, tiled=True)
+
     both_edges = struct((2, SL, H, C), BF16)
 
     def back_edges(for_core, after):
@@ -559,15 +570,10 @@
             scratch=[pltpu.VMEM((2, 2, SL, H, C), F32)],
         )(spot, after, cotangent, ret)
 
-    to_chip = back_edges(False, first_sent)
+    to_chip = back_edges(False, second_sent)
     back_chip = lax.ppermute(to_chip, "azim", chips)
     to_core = back_edges(True, to_chip)
     back_core = lax.ppermute(to_core, "azim", cores)
-
-    second_sent = call(
-        second_kernel, struct((strips, 16, LANES), BF16), 16, moved=1_000_000, smem=1, hbm=(2, 3)
-    )(spot, first_recv, back_chip, back_core)
-    second_recv = lax.all_to_all(second_sent, "azim", split_axis=0, concat_axis=0, tiled=True)
 
     grad_latents = call(
         latents_kernel,
@@ -581,7 +587,7 @@
     )(spot, second_sent, latents, cotangent, ret, back_core, back_chip, table)
     second_recv, grad_latents = lax.optimization_barrier((second_recv, grad_latents))
 
-    third_sent = call(third_kernel, struct((GROUPS, 16, LANES), F32), 16, moved=300_000)(
+    third_sent = call(third_kernel, struct((GROUPS, 16, LANES), BF16), 16, moved=300_000)(
         second_recv
     )
     third_recv = lax.all_to_all(third_sent, "sweep", split_axis=0, concat_axis=0, tiled=True)

time: 139 us -> 131 us (0.942)
  the two profiles are of different devices: /device:TPU:1 before, /device:TPU:32 now
where the time goes in v8:
time: 131 us; the launch traced here: 130 us
  blocking collectives  50.3 us (38%)
  starting transfers between devices  44.3 us (34%)
  waiting for transfers between devices  21.9 us (17%)
  Pallas kernels  11.6 us (9%)
    all_to_all x1, blocking collectives, on_device(): lax.all_to_all(sent, 'sweep', split_axis=0, concat_axis=0, tiled=True)  20.2 us
    all_to_all x1, blocking collectives, on_device(): lax.all_to_all(first_sent, 'sweep', split_axis=0, concat_axis=0, tiled=True)  19 us
    ppermute x1, starting transfers between devices, on_device(): other_chip = lax.ppermute(to_chip, 'azim', chips)  12.3 us
    all_to_all x1, blocking collectives, on_device(): lax.all_to_all(third_sent, 'sweep', split_axis=0, concat_axis=0, tiled=True)  11.1 us
    all_to_all x1, starting transfers between devices, on_device(): lax.all_to_all(second_sent, 'azim', split_axis=0, concat_axis=0, tiled=True)  11 us
    pallas_call x13, Pallas kernels, run(): pl.pallas_call(kernel, out_shape=outs, in_specs=specs, out_specs=jax.tree...  10.3 us
    ppermute x1, waiting for transfers between devices, on_device(): from_chip = lax.ppermute(send, 'azim', sides)  8.31 us
    ppermute x1, waiting for transfers between devices, on_device(): back_chip = lax.ppermute(to_chip, 'azim', chips)  6.69 us
  transfers between devices with their start and end apart: 9, of which 4 were waited for; matrix products, arithmetic and copies ran while one was open for 0% of the time, Pallas kernels for 3%

profile of v8, /device:TPU:32, one launch (start us, length us, event | category | flops | bytes accessed | tf_op | source)
XLA Modules:
  0.0 130.0 jit_solution(3279198163747842757)
XLA Ops:
  0.6 1.0 copy-done.1
  1.7 0.8 shard_map.152.after
  2.5 4.9 %all-to-all-start.1 = ((bf16[16,2,16,512]{3,2,1,0:T(8,128)(2,1)}), bf16[16,2,16,512]{3,2,1,0:T(8,128)(2,1)S(1)}, u32[]{:S(2)}, u32[]{:S(2)}) async-start(bf16[16,2,16,512]{3,2,1,0:T(8,128)(2,1)} %shard_map.152.after), calls=%async_computation.1 | async-start | bytes 1048576 | tf_op jit(solution)/shard_map/all_to_all | solution.py:475
  7.4 0.0 copy-start.3
  7.4 0.0 copy-start.4
  7.4 0.1 shard_map.153.after
  7.5 12.3 %collective-permute-start.1 = (bf16[2,8,512]{2,1,0:T(8,128)(2,1)S(1)}, bf16[2,8,512]{2,1,0:T(8,128)(2,1)S(1)}, u32[]{:S(2)}, u32[]{:S(2)}) collective-permute-start(bf16[2,8,512]{2,1,0:T(8,128)(2,1)S(1)} %shard_map.153.after), channel_id=1, source_target_pairs={{0,31},{1,2},{2,1},{3,4},{4,3},{5,6},{6,5},{7,8},{8,7},{9,10},{10,... | collective-permute-start | bytes 49160 | tf_op jit(solution)/shard_map/ppermute | solution.py:479
  19.9 0.1 shard_map.154
  19.9 1.9 %collective-permute-start = (bf16[2,8,512]{2,1,0:T(8,128)(2,1)S(1)}, bf16[2,8,512]{2,1,0:T(8,128)(2,1)S(1)}, u32[]{:S(2)}, u32[]{:S(2)}) collective-permute-start(bf16[2,8,512]{2,1,0:T(8,128)(2,1)S(1)} %get-tuple-element.24), channel_id=1, source_target_pairs={{0,1},{1,0},{2,3},{3,2},{4,5},{5,4},{6,7},{7,6},{8,9},{9,8},{10,11... | collective-permute-start | bytes 49160 | tf_op jit(solution)/shard_map/ppermute | solution.py:489
  21.9 5.0 %collective-permute-done.1.other_chip = bf16[2,8,512]{2,1,0:T(8,128)(2,1)S(1)} collective-permute-done((bf16[2,8,512]{2,1,0:T(8,128)(2,1)S(1)}, bf16[2,8,512]{2,1,0:T(8,128)(2,1)S(1)}, u32[]{:S(2)}, u32[]{:S(2)}) %collective-permute-start.1) | collective-permute-done | bytes 16416 | tf_op jit(solution)/shard_map/ppermute | solution.py:479
  26.8 1.2 shard_map.155
  28.1 20.2 %all_to_all.30.recv = bf16[16,2,16,512]{3,2,1,0:T(8,128)(2,1)S(1)} all-to-all(bf16[16,2,16,512]{3,2,1,0:T(8,128)(2,1)S(1)} %shard_map.155), channel_id=1, replica_groups=mesh['sweep'=16,'azim'=32] {'sweep'}, dimensions={0} | all-to-all | bytes 1048576 | tf_op jit(solution)/shard_map/all_to_all | solution.py:500
  48.3 4.0 %shard_map.156 = (bf16[16,2,16,512]{3,2,1,0:T(8,128)(2,1)}, bf16[2,2,16,64,128]{4,3,2,1,0:T(8,128)(2,1)S(1)}, f32[1,512]{1,0:T(1,128)S(1)}) custom-call(s32[1]{0:T(128)} %bitcast.spot, bf16[16,2,16,512]{3,2,1,0:T(8,128)(2,1)S(1)} %all_to_all.30.recv, bf16[16,2,16,512]{3,2,1,0:T(8,128)(2,1)S(1)} %all-to-all-done.1.recv_cot, bf16[512,256]{1,0:T(8,128)(2,1)S(1)} %copy-done.5, ...), custom_call_target="tpu_custom_call" | custom-call | flops 2000000000 | bytes 6000000 | tf_op jit(solution)/shard_map/pallas_call | solution.py:37
  52.3 3.6 %all-to-all-start.2 = ((bf16[16,2,16,512]{3,2,1,0:T(8,128)(2,1)}), bf16[16,2,16,512]{3,2,1,0:T(8,128)(2,1)S(1)}, u32[]{:S(2)}, u32[]{:S(2)}) async-start(bf16[16,2,16,512]{3,2,1,0:T(8,128)(2,1)} %get-tuple-element.26), calls=%async_computation.2 | async-start | bytes 1048576 | tf_op jit(solution)/shard_map/all_to_all | solution.py:526
  55.9 1.9 %collective-permute-start.2 = (bf16[2,16,64,128]{3,2,1,0:T(8,128)(2,1)S(1)}, bf16[2,16,64,128]{3,2,1,0:T(8,128)(2,1)S(1)}, u32[]{:S(2)}, u32[]{:S(2)}) collective-permute-start(bf16[2,16,64,128]{3,2,1,0:T(8,128)(2,1)S(1)} %slice_bitcast_fusion), channel_id=1, source_target_pairs={{0,1},{1,0},{2,3},{3,2},{4,5},{5,4},{6,7},{7,6},{8,9},{9,8},{10,11... | collective-permute-start | bytes 1572872 | tf_op jit(solution)/shard_map/ppermute | solution.py:527
  57.8 1.9 %collective-permute-done.2.got = bf16[2,16,64,128]{3,2,1,0:T(8,128)(2,1)S(1)} collective-permute-done((bf16[2,16,64,128]{3,2,1,0:T(8,128)(2,1)S(1)}, bf16[2,16,64,128]{3,2,1,0:T(8,128)(2,1)S(1)}, u32[]{:S(2)}, u32[]{:S(2)}) %collective-permute-start.2) | collective-permute-done | bytes 524320 | tf_op jit(solution)/shard_map/ppermute | solution.py:527
  59.7 0.1 shard_map.157
  59.8 2.1 %collective-permute-start.3 = (bf16[16,64,128]{2,1,0:T(8,128)(2,1)S(1)}, bf16[16,64,128]{2,1,0:T(8,128)(2,1)S(1)}, u32[]{:S(2)}, u32[]{:S(2)}) collective-permute-start(bf16[16,64,128]{2,1,0:T(8,128)(2,1)S(1)} %get-tuple-element.30), channel_id=1, source_target_pairs={{0,2},{1,3},{2,0},{3,1},{4,6},{5,7},{6,4},{7,5},{8,10},{9,11},{10,... | collective-permute-start | bytes 786440 | tf_op jit(solution)/shard_map/ppermute | solution.py:530
  61.9 8.3 %collective-permute-done.3.got = bf16[16,64,128]{2,1,0:T(8,128)(2,1)S(1)} collective-permute-done((bf16[16,64,128]{2,1,0:T(8,128)(2,1)S(1)}, bf16[16,64,128]{2,1,0:T(8,128)(2,1)S(1)}, u32[]{:S(2)}, u32[]{:S(2)}) %collective-permute-start.3) | collective-permute-done | bytes 262176 | tf_op jit(solution)/shard_map/ppermute | solution.py:530
  70.2 0.1 shard_map.158.sums_in
  70.3 1.3 %shard_map.159 = bf16[16,80,128]{2,1,0:T(8,128)(2,1)S(1)} custom-call(s32[1]{0:T(128)} %bitcast.spot, bf16[2,8,32,512]{3,2,1,0:T(8,128)(2,1)S(1)} %copy-done, bf16[2,8,512]{2,1,0:T(8,128)(2,1)S(1)} %collective-permute-done.other_core, bf16[2,8,512]{2,1,0:T(8,128)(2,1)S(1)} %collective-permute-done.1.other_chip, ...), custom_call_target="tpu_custom_call", output_to_operand_aliasing={{}: (7, {})} | custom-call | flops 10000000 | bytes 2000000 | tf_op jit(solution)/shard_map/pallas_call | solution.py:536
  71.6 19.0 %all_to_all.31.recv = bf16[16,80,128]{2,1,0:T(8,128)(2,1)S(1)} all-to-all(bf16[16,80,128]{2,1,0:T(8,128)(2,1)S(1)} %shard_map.159), channel_id=1, replica_groups=mesh['sweep'=16,'azim'=32] {'sweep'}, dimensions={0} | all-to-all | bytes 655360 | tf_op jit(solution)/shard_map/all_to_all | solution.py:554
  90.6 0.7 shard_map.160.after
  91.3 11.0 %all-to-all-start.4 = ((bf16[32,16,128]{2,1,0:T(8,128)(2,1)}), bf16[32,16,128]{2,1,0:T(8,128)(2,1)S(1)}, u32[]{:S(2)}, u32[]{:S(2)}) async-start(bf16[32,16,128]{2,1,0:T(8,128)(2,1)} %shard_map.160.after), calls=%async_computation.4 | async-start | bytes 262144 | tf_op jit(solution)/shard_map/all_to_all | solution.py:558
  102.3 0.1 shard_map.161.after
  102.4 0.1 shard_map.162
  102.5 2.1 %collective-permute-start.4 = (bf16[2,2,8,512]{3,2,1,0:T(8,128)(2,1)S(1)}, bf16[2,2,8,512]{3,2,1,0:T(8,128)(2,1)S(1)}, u32[]{:S(2)}, u32[]{:S(2)}) collective-permute-start(bf16[2,2,8,512]{3,2,1,0:T(8,128)(2,1)S(1)} %shard_map.162), channel_id=1, source_target_pairs={{0,1},{1,0},{2,3},{3,2},{4,5},{5,4},{6,7},{7,6},{8,9},{9,8},{10,11... | collective-permute-start | bytes 98312 | tf_op jit(solution)/shard_map/ppermute | solution.py:576
  104.6 4.5 %collective-permute-start.5 = (bf16[2,2,8,512]{3,2,1,0:T(8,128)(2,1)S(1)}, bf16[2,2,8,512]{3,2,1,0:T(8,128)(2,1)S(1)}, u32[]{:S(2)}, u32[]{:S(2)}) collective-permute-start(bf16[2,2,8,512]{3,2,1,0:T(8,128)(2,1)S(1)} %shard_map.161.after), channel_id=1, source_target_pairs={{0,31},{1,2},{2,1},{3,4},{4,3},{5,6},{6,5},{7,8},{8,7},{9,10},{10,... | collective-permute-start | bytes 98312 | tf_op jit(solution)/shard_map/ppermute | solution.py:574
  109.2 6.7 %collective-permute-done.5.other_chip = bf16[2,2,8,512]{3,2,1,0:T(8,128)(2,1)S(1)} collective-permute-done((bf16[2,2,8,512]{3,2,1,0:T(8,128)(2,1)S(1)}, bf16[2,2,8,512]{3,2,1,0:T(8,128)(2,1)S(1)}, u32[]{:S(2)}, u32[]{:S(2)}) %collective-permute-start.5) | collective-permute-done | bytes 32800 | tf_op jit(solution)/shard_map/ppermute | solution.py:574
  115.9 2.3 %shard_map.163 = f32[2,8,32,512]{3,2,1,0:T(8,128)} custom-call(s32[1]{0:T(128)} %bitcast.spot, bf16[32,16,128]{2,1,0:T(8,128)(2,1)} %shard_map.160.after, bf16[2,8,32,512]{3,2,1,0:T(8,128)(2,1)S(1)} %copy-done, bf16[2,8,32,512]{3,2,1,0:T(8,128)(2,1)S(1)} %copy-done.2, bf16[16,2,16,512]{3,2,1,0:T(8,128)(2,1)S(1)} %all-to-all-done.2.ret, ...), custom_call_target="tpu_custom_call" | custom-call | flops 10000000 | bytes 4000000 | tf_op jit(solution)/shard_map/pallas_call | solution.py:37
  118.3 11.1 %all_to_all.32.recv = bf16[16,16,128]{2,1,0:T(8,128)(2,1)S(1)} all-to-all(bf16[16,16,128]{2,1,0:T(8,128)(2,1)S(1)} %shard_map.164), channel_id=1, replica_groups=mesh['sweep'=16,'azim'=32] {'sweep'}, dimensions={0} | all-to-all | bytes 131072 | tf_op jit(solution)/shard_map/all_to_all | solution.py:593
  129.4 0.7 shard_map.165
  (24 shorter events, 0.1 us)
Async XLA Ops:
  0.6 1.0 copy-start.1
  2.5 4.9 %copy-start = (bf16[2,8,32,512]{3,2,1,0:T(8,128)(2,1)S(1)}, bf16[2,8,32,512]{3,2,1,0:T(8,128)(2,1)}, u32[]{:S(2)}) copy-start(bf16[2,8,32,512]{3,2,1,0:T(8,128)(2,1)} %lat.9) | copy-start | bytes 1572868
  2.5 25.6 %all-to-all-start.1 = ((bf16[16,2,16,512]{3,2,1,0:T(8,128)(2,1)}), bf16[16,2,16,512]{3,2,1,0:T(8,128)(2,1)S(1)}, u32[]{:S(2)}, u32[]{:S(2)}) async-start(bf16[16,2,16,512]{3,2,1,0:T(8,128)(2,1)} %shard_map.152.after), calls=%async_computation.1 | async-start | bytes 1048576 | tf_op jit(solution)/shard_map/all_to_all | solution.py:475
  7.4 12.4 %copy-start.3 = (f32[9,512]{1,0:T(8,128)S(1)}, f32[9,512]{1,0:T(8,128)}, u32[]{:S(2)}) copy-start(f32[9,512]{1,0:T(8,128)} %taps.1) | copy-start | bytes 55300
  7.4 12.4 %copy-start.4 = (f32[512]{0:T(512)S(1)}, f32[512]{0:T(512)}, u32[]{:S(2)}) copy-start(f32[512]{0:T(512)} %param.12) | copy-start | bytes 6148
  7.5 19.3 %collective-permute-start.1 = (bf16[2,8,512]{2,1,0:T(8,128)(2,1)S(1)}, bf16[2,8,512]{2,1,0:T(8,128)(2,1)S(1)}, u32[]{:S(2)}, u32[]{:S(2)}) collective-permute-start(bf16[2,8,512]{2,1,0:T(8,128)(2,1)S(1)} %shard_map.153.after), channel_id=1, source_target_pairs={{0,31},{1,2},{2,1},{3,4},{4,3},{5,6},{6,5},{7,8},{8,7},{9,10},{10,... | collective-permute-start | bytes 49160 | tf_op jit(solution)/shard_map/ppermute | solution.py:479
  19.9 6.9 %collective-permute-start = (bf16[2,8,512]{2,1,0:T(8,128)(2,1)S(1)}, bf16[2,8,512]{2,1,0:T(8,128)(2,1)S(1)}, u32[]{:S(2)}, u32[]{:S(2)}) collective-permute-start(bf16[2,8,512]{2,1,0:T(8,128)(2,1)S(1)} %get-tuple-element.24), channel_id=1, source_target_pairs={{0,1},{1,0},{2,3},{3,2},{4,5},{5,4},{6,7},{7,6},{8,9},{9,8},{10,11... | collective-permute-start | bytes 49160 | tf_op jit(solution)/shard_map/ppermute | solution.py:489
  26.8 21.4 %copy-start.9 = (f32[512]{0:T(512)S(1)}, f32[512]{0:T(512)}, u32[]{:S(2)}) copy-start(f32[512]{0:T(512)} %param.13) | copy-start | bytes 6148
  28.0 20.2 %copy-start.5 = (bf16[512,256]{1,0:T(8,128)(2,1)S(1)}, bf16[512,256]{1,0:T(8,128)(2,1)}, u32[]{:S(2)}) copy-start(bf16[512,256]{1,0:T(8,128)(2,1)} %w_query.1) | copy-start | bytes 786436
  28.1 20.2 %copy-start.6 = (bf16[512,256]{1,0:T(8,128)(2,1)S(1)}, bf16[512,256]{1,0:T(8,128)(2,1)}, u32[]{:S(2)}) copy-start(bf16[512,256]{1,0:T(8,128)(2,1)} %w_key.1) | copy-start | bytes 786436
  28.1 20.2 %copy-start.7 = (bf16[512,256]{1,0:T(8,128)(2,1)S(1)}, bf16[512,256]{1,0:T(8,128)(2,1)}, u32[]{:S(2)}) copy-start(bf16[512,256]{1,0:T(8,128)(2,1)} %w_value.1) | copy-start | bytes 786436
  28.1 20.2 %copy-start.8 = (bf16[512,256]{1,0:T(8,128)(2,1)S(1)}, bf16[512,256]{1,0:T(8,128)(2,1)}, u32[]{:S(2)}) copy-start(bf16[512,256]{1,0:T(8,128)(2,1)} %w_output.1) | copy-start | bytes 786436
  52.3 18.0 %all-to-all-start.2 = ((bf16[16,2,16,512]{3,2,1,0:T(8,128)(2,1)}), bf16[16,2,16,512]{3,2,1,0:T(8,128)(2,1)S(1)}, u32[]{:S(2)}, u32[]{:S(2)}) async-start(bf16[16,2,16,512]{3,2,1,0:T(8,128)(2,1)} %get-tuple-element.26), calls=%async_computation.2 | async-start | bytes 1048576 | tf_op jit(solution)/shard_map/all_to_all | solution.py:526
  55.9 3.8 %collective-permute-start.2 = (bf16[2,16,64,128]{3,2,1,0:T(8,128)(2,1)S(1)}, bf16[2,16,64,128]{3,2,1,0:T(8,128)(2,1)S(1)}, u32[]{:S(2)}, u32[]{:S(2)}) collective-permute-start(bf16[2,16,64,128]{3,2,1,0:T(8,128)(2,1)S(1)} %slice_bitcast_fusion), channel_id=1, source_target_pairs={{0,1},{1,0},{2,3},{3,2},{4,5},{5,4},{6,7},{7,6},{8,9},{9,8},{10,11... | collective-permute-start | bytes 1572872 | tf_op jit(solution)/shard_map/ppermute | solution.py:527
  59.8 10.5 %copy-start.2 = (bf16[2,8,32,512]{3,2,1,0:T(8,128)(2,1)S(1)}, bf16[2,8,32,512]{3,2,1,0:T(8,128)(2,1)}, u32[]{:S(2)}) copy-start(bf16[2,8,32,512]{3,2,1,0:T(8,128)(2,1)} %cot.9) | copy-start | bytes 1572868
  59.8 10.4 %collective-permute-start.3 = (bf16[16,64,128]{2,1,0:T(8,128)(2,1)S(1)}, bf16[16,64,128]{2,1,0:T(8,128)(2,1)S(1)}, u32[]{:S(2)}, u32[]{:S(2)}) collective-permute-start(bf16[16,64,128]{2,1,0:T(8,128)(2,1)S(1)} %get-tuple-element.30), channel_id=1, source_target_pairs={{0,2},{1,3},{2,0},{3,1},{4,6},{5,7},{6,4},{7,5},{8,10},{9,11},{10,... | collective-permute-start | bytes 786440 | tf_op jit(solution)/shard_map/ppermute | solution.py:530
  91.3 26.9 %all-to-all-start.4 = ((bf16[32,16,128]{2,1,0:T(8,128)(2,1)}), bf16[32,16,128]{2,1,0:T(8,128)(2,1)S(1)}, u32[]{:S(2)}, u32[]{:S(2)}) async-start(bf16[32,16,128]{2,1,0:T(8,128)(2,1)} %shard_map.160.after), calls=%async_computation.4 | async-start | bytes 262144 | tf_op jit(solution)/shard_map/all_to_all | solution.py:558
  102.5 6.6 %collective-permute-start.4 = (bf16[2,2,8,512]{3,2,1,0:T(8,128)(2,1)S(1)}, bf16[2,2,8,512]{3,2,1,0:T(8,128)(2,1)S(1)}, u32[]{:S(2)}, u32[]{:S(2)}) collective-permute-start(bf16[2,2,8,512]{3,2,1,0:T(8,128)(2,1)S(1)} %shard_map.162), channel_id=1, source_target_pairs={{0,1},{1,0},{2,3},{3,2},{4,5},{5,4},{6,7},{7,6},{8,9},{9,8},{10,11... | collective-permute-start | bytes 98312 | tf_op jit(solution)/shard_map/ppermute | solution.py:576
  104.6 11.3 %collective-permute-start.5 = (bf16[2,2,8,512]{3,2,1,0:T(8,128)(2,1)S(1)}, bf16[2,2,8,512]{3,2,1,0:T(8,128)(2,1)S(1)}, u32[]{:S(2)}, u32[]{:S(2)}) collective-permute-start(bf16[2,2,8,512]{3,2,1,0:T(8,128)(2,1)S(1)} %shard_map.161.after), channel_id=1, source_target_pairs={{0,31},{1,2},{2,1},{3,4},{4,3},{5,6},{6,5},{7,8},{8,7},{9,10},{10,... | collective-permute-start | bytes 98312 | tf_op jit(solution)/shard_map/ppermute | solution.py:574

commit v9 on v8

--- a/solution.py
+++ b/solution.py
@@ -109,11 +109,22 @@
             edges[1, s, h : h + 1, :] = lat[s, h, PX:, :].astype(F32)[PX - 1 :]
 
 
-def pack_kernel(cot, out):
+def pack_kernel(cot, out, token, sems):
+    token[...] = jnp.zeros_like(token)
+    copies = []
     for s in range(SL):
-        for h in range(H):
-            out[2 * h, s] = cot[s, h, :PX, :]
-            out[2 * h + 1, s] = cot[s, h, PX:, :]
+        for g in range(GROUPS):
+            copies.append(
+                pltpu.make_async_copy(
+                    cot.at[s, g // 2, pl.ds(PX * (g % 2), PX), :],
+                    out.at[g, s],
+                    sems.at[s * GROUPS + g],
+                )
+            )
+    for copy in copies:
+        copy.start()
+    for copy in copies:
+        copy.wait()
 
 
 def chip_edge_kernel(spot, after, lat, out, edges):
@@ -471,11 +482,20 @@
     one_edge = struct((SL, H, C), BF16)
     column = [pltpu.VMEM((2, SL, H, C), F32)]
     packed = struct((GROUPS, SL, PX, C), BF16)
-    cot_sent = call(pack_kernel, packed, 16, moved=1_000_000)(cotangent)
+    far = pl.BlockSpec(memory_space=pltpu.HBM)
+    cot_sent, token = pl.pallas_call(
+        pack_kernel,
+        out_shape=(packed, struct((8, LANES), F32)),
+        in_specs=[far],
+        out_specs=(far, pl.BlockSpec(memory_space=pltpu.VMEM)),
+        scratch_shapes=[pltpu.SemaphoreType.DMA((SL * GROUPS,))],
+        compiler_params=params(56),
+        cost_estimate=pl.CostEstimate(flops=0, bytes_accessed=1_000_000, transcendentals=0),
+    )(cotangent)
     recv_cot = lax.all_to_all(cot_sent, "sweep", split_axis=0, concat_axis=0, tiled=True)
     to_chip = call(
         chip_edge_kernel, one_edge, 16, moved=600_000, smem=1, hbm=(1,), scratch=column
-    )(spot, cot_sent, latents)
+    )(spot, token, latents)
     other_chip = lax.ppermute(to_chip, "azim", chips)
     to_core, table = call(
         core_edge_kernel,
@@ -570,10 +590,10 @@
             scratch=[pltpu.VMEM((2, 2, SL, H, C), F32)],
         )(spot, after, cotangent, ret)
 
-    to_chip = back_edges(False, second_sent)
+    to_core = back_edges(True, second_sent)
+    back_core = lax.ppermute(to_core, "azim", cores)
+    to_chip = back_edges(False, to_core)
     back_chip = lax.ppermute(to_chip, "azim", chips)
-    to_core = back_edges(True, to_chip)
-    back_core = lax.ppermute(to_core, "azim", cores)
 
     grad_latents = call(
         latents_kernel,

time: 131 us -> 147 us (1.12)
  the two profiles are of different devices: /device:TPU:32 before, /device:TPU:1 now
where the time goes in v9:
time: 147 us; the launch traced here: 146 us
  starting transfers between devices  56 us (38%)
  blocking collectives  49 us (33%)
  Pallas kernels  28.6 us (19%)
  waiting for transfers between devices  10.6 us (7%)
    all_to_all x1, blocking collectives, on_device(): lax.all_to_all(sent, 'sweep', split_axis=0, concat_axis=0, tiled=True)  21.2 us
    all_to_all x1, blocking collectives, on_device(): lax.all_to_all(first_sent, 'sweep', split_axis=0, concat_axis=0, tiled=True)  18 us
    pallas_call x1, Pallas kernels, on_device(): pl.pallas_call(pack_kernel, out_shape=(packed, struct((8, LANES), F32)),...  17.9 us
    ppermute x1, starting transfers between devices, on_device(): other_core = lax.ppermute(to_core, 'azim', cores)  10.7 us
    all_to_all x1, starting transfers between devices, on_device(): lax.all_to_all(second_sent, 'azim', split_axis=0, concat_axis=0, tiled=True)  9.97 us
    all_to_all x1, blocking collectives, on_device(): lax.all_to_all(third_sent, 'sweep', split_axis=0, concat_axis=0, tiled=True)  9.76 us
    pallas_call x12, Pallas kernels, run(): pl.pallas_call(kernel, out_shape=outs, in_specs=specs, out_specs=jax.tree...  9.45 us
    ppermute x1, starting transfers between devices, on_device(): back_core = lax.ppermute(to_core, 'azim', cores)  8.16 us
  transfers between devices with their start and end apart: 9, of which 4 were waited for; matrix products, arithmetic and copies ran while one was open for 0% of the time, Pallas kernels for 3%

profile of v9, /device:TPU:1, one launch (start us, length us, event | category | flops | bytes accessed | tf_op | source)
XLA Modules:
  0.0 145.8 jit_solution(18250128124791953594)
XLA Ops:
  0.6 17.9 %shard_map.152 = (bf16[16,2,16,512]{3,2,1,0:T(8,128)(2,1)}, f32[8,128]{1,0:T(8,128)}) custom-call(bf16[2,8,32,512]{3,2,1,0:T(8,128)(2,1)} %cot.9), custom_call_target="tpu_custom_call" | custom-call | bytes 1000000 | tf_op jit(solution)/shard_map/pallas_call | solution.py:486
  18.5 8.1 %all-to-all-start.1 = ((bf16[16,2,16,512]{3,2,1,0:T(8,128)(2,1)}), bf16[16,2,16,512]{3,2,1,0:T(8,128)(2,1)S(1)}, u32[]{:S(2)}, u32[]{:S(2)}) async-start(bf16[16,2,16,512]{3,2,1,0:T(8,128)(2,1)} %get-tuple-element.29), calls=%async_computation.1 | async-start | bytes 1048576 | tf_op jit(solution)/shard_map/all_to_all | solution.py:495
  26.7 0.0 copy-start.3
  26.7 0.7 copy-done.3
  27.4 0.1 shard_map.153.after
  27.4 4.8 %collective-permute-start.1 = (bf16[2,8,512]{2,1,0:T(8,128)(2,1)S(1)}, bf16[2,8,512]{2,1,0:T(8,128)(2,1)S(1)}, u32[]{:S(2)}, u32[]{:S(2)}) collective-permute-start(bf16[2,8,512]{2,1,0:T(8,128)(2,1)S(1)} %shard_map.153.after), channel_id=1, source_target_pairs={{0,31},{1,2},{2,1},{3,4},{4,3},{5,6},{6,5},{7,8},{8,7},{9,10},{10,... | collective-permute-start | bytes 49160 | tf_op jit(solution)/shard_map/ppermute | solution.py:499
  32.3 0.1 shard_map.154
  32.3 10.7 %collective-permute-start = (bf16[2,8,512]{2,1,0:T(8,128)(2,1)S(1)}, bf16[2,8,512]{2,1,0:T(8,128)(2,1)S(1)}, u32[]{:S(2)}, u32[]{:S(2)}) collective-permute-start(bf16[2,8,512]{2,1,0:T(8,128)(2,1)S(1)} %get-tuple-element.27), channel_id=1, source_target_pairs={{0,1},{1,0},{2,3},{3,2},{4,5},{5,4},{6,7},{7,6},{8,9},{9,8},{10,11... | collective-permute-start | bytes 49160 | tf_op jit(solution)/shard_map/ppermute | solution.py:509
  43.1 0.8 collective-permute-done.other_core
  43.9 1.2 shard_map.155
  45.1 0.0 copy-start.5
  45.1 21.2 %all_to_all.30.recv = bf16[16,2,16,512]{3,2,1,0:T(8,128)(2,1)S(1)} all-to-all(bf16[16,2,16,512]{3,2,1,0:T(8,128)(2,1)S(1)} %shard_map.155), channel_id=1, replica_groups=mesh['sweep'=16,'azim'=32] {'sweep'}, dimensions={0} | all-to-all | bytes 1048576 | tf_op jit(solution)/shard_map/all_to_all | solution.py:520
  66.4 4.0 %shard_map.156 = (bf16[16,2,16,512]{3,2,1,0:T(8,128)(2,1)}, bf16[2,2,16,64,128]{4,3,2,1,0:T(8,128)(2,1)S(1)}, f32[1,512]{1,0:T(1,128)S(1)}) custom-call(s32[1]{0:T(128)} %bitcast.spot, bf16[16,2,16,512]{3,2,1,0:T(8,128)(2,1)S(1)} %all_to_all.30.recv, bf16[16,2,16,512]{3,2,1,0:T(8,128)(2,1)S(1)} %all-to-all-done.1.recv_cot, bf16[512,256]{1,0:T(8,128)(2,1)S(1)} %copy-done.5, ...), custom_call_target="tpu_custom_call" | custom-call | flops 2000000000 | bytes 6000000 | tf_op jit(solution)/shard_map/pallas_call | solution.py:37
  70.4 4.1 %all-to-all-start.2 = ((bf16[16,2,16,512]{3,2,1,0:T(8,128)(2,1)}), bf16[16,2,16,512]{3,2,1,0:T(8,128)(2,1)S(1)}, u32[]{:S(2)}, u32[]{:S(2)}) async-start(bf16[16,2,16,512]{3,2,1,0:T(8,128)(2,1)} %get-tuple-element.30), calls=%async_computation.2 | async-start | bytes 1048576 | tf_op jit(solution)/shard_map/all_to_all | solution.py:546
  74.5 4.5 %collective-permute-start.2 = (bf16[2,16,64,128]{3,2,1,0:T(8,128)(2,1)S(1)}, bf16[2,16,64,128]{3,2,1,0:T(8,128)(2,1)S(1)}, u32[]{:S(2)}, u32[]{:S(2)}) collective-permute-start(bf16[2,16,64,128]{3,2,1,0:T(8,128)(2,1)S(1)} %slice_bitcast_fusion), channel_id=1, source_target_pairs={{0,1},{1,0},{2,3},{3,2},{4,5},{5,4},{6,7},{7,6},{8,9},{9,8},{10,11... | collective-permute-start | bytes 1572872 | tf_op jit(solution)/shard_map/ppermute | solution.py:547
  79.0 1.5 %collective-permute-done.2.got = bf16[2,16,64,128]{3,2,1,0:T(8,128)(2,1)S(1)} collective-permute-done((bf16[2,16,64,128]{3,2,1,0:T(8,128)(2,1)S(1)}, bf16[2,16,64,128]{3,2,1,0:T(8,128)(2,1)S(1)}, u32[]{:S(2)}, u32[]{:S(2)}) %collective-permute-start.2) | collective-permute-done | bytes 524320 | tf_op jit(solution)/shard_map/ppermute | solution.py:547
  80.5 0.1 shard_map.157
  80.7 2.1 %collective-permute-start.3 = (bf16[16,64,128]{2,1,0:T(8,128)(2,1)S(1)}, bf16[16,64,128]{2,1,0:T(8,128)(2,1)S(1)}, u32[]{:S(2)}, u32[]{:S(2)}) collective-permute-start(bf16[16,64,128]{2,1,0:T(8,128)(2,1)S(1)} %get-tuple-element.34), channel_id=1, source_target_pairs={{0,2},{1,3},{2,0},{3,1},{4,6},{5,7},{6,4},{7,5},{8,10},{9,11},{10,... | collective-permute-start | bytes 786440 | tf_op jit(solution)/shard_map/ppermute | solution.py:550
  82.7 7.5 %collective-permute-done.3.got = bf16[16,64,128]{2,1,0:T(8,128)(2,1)S(1)} collective-permute-done((bf16[16,64,128]{2,1,0:T(8,128)(2,1)S(1)}, bf16[16,64,128]{2,1,0:T(8,128)(2,1)S(1)}, u32[]{:S(2)}, u32[]{:S(2)}) %collective-permute-start.3) | collective-permute-done | bytes 262176 | tf_op jit(solution)/shard_map/ppermute | solution.py:550
  90.2 0.1 shard_map.158.sums_in
  90.3 1.3 shard_map.159
  91.6 18.0 %all_to_all.31.recv = bf16[16,80,128]{2,1,0:T(8,128)(2,1)S(1)} all-to-all(bf16[16,80,128]{2,1,0:T(8,128)(2,1)S(1)} %shard_map.159), channel_id=1, replica_groups=mesh['sweep'=16,'azim'=32] {'sweep'}, dimensions={0} | all-to-all | bytes 655360 | tf_op jit(solution)/shard_map/all_to_all | solution.py:574
  109.6 0.7 shard_map.160.after
  110.3 10.0 %all-to-all-start.4 = ((bf16[32,16,128]{2,1,0:T(8,128)(2,1)}), bf16[32,16,128]{2,1,0:T(8,128)(2,1)S(1)}, u32[]{:S(2)}, u32[]{:S(2)}) async-start(bf16[32,16,128]{2,1,0:T(8,128)(2,1)} %shard_map.160.after), calls=%async_computation.4 | async-start | bytes 262144 | tf_op jit(solution)/shard_map/all_to_all | solution.py:578
  120.3 0.1 shard_map.161.after
  120.4 0.1 shard_map.162
  120.5 3.5 %collective-permute-start.5 = (bf16[2,2,8,512]{3,2,1,0:T(8,128)(2,1)S(1)}, bf16[2,2,8,512]{3,2,1,0:T(8,128)(2,1)S(1)}, u32[]{:S(2)}, u32[]{:S(2)}) collective-permute-start(bf16[2,2,8,512]{3,2,1,0:T(8,128)(2,1)S(1)} %shard_map.162), channel_id=1, source_target_pairs={{0,31},{1,2},{2,1},{3,4},{4,3},{5,6},{6,5},{7,8},{8,7},{9,10},{10,... | collective-permute-start | bytes 98312 | tf_op jit(solution)/shard_map/ppermute | solution.py:596
  124.0 8.2 %collective-permute-start.4 = (bf16[2,2,8,512]{3,2,1,0:T(8,128)(2,1)S(1)}, bf16[2,2,8,512]{3,2,1,0:T(8,128)(2,1)S(1)}, u32[]{:S(2)}, u32[]{:S(2)}) collective-permute-start(bf16[2,2,8,512]{3,2,1,0:T(8,128)(2,1)S(1)} %shard_map.161.after), channel_id=1, source_target_pairs={{0,1},{1,0},{2,3},{3,2},{4,5},{5,4},{6,7},{7,6},{8,9},{9,8},{10,11... | collective-permute-start | bytes 98312 | tf_op jit(solution)/shard_map/ppermute | solution.py:594
  132.2 0.8 collective-permute-done.4.other_core
  133.0 2.3 %shard_map.163 = f32[2,8,32,512]{3,2,1,0:T(8,128)} custom-call(s32[1]{0:T(128)} %bitcast.spot, bf16[32,16,128]{2,1,0:T(8,128)(2,1)} %shard_map.160.after, bf16[2,8,32,512]{3,2,1,0:T(8,128)(2,1)S(1)} %copy-done, bf16[2,8,32,512]{3,2,1,0:T(8,128)(2,1)S(1)} %copy-done.1, bf16[16,2,16,512]{3,2,1,0:T(8,128)(2,1)S(1)} %all-to-all-done.2.ret, ...), custom_call_target="tpu_custom_call" | custom-call | flops 10000000 | bytes 4000000 | tf_op jit(solution)/shard_map/pallas_call | solution.py:37
  135.4 9.8 %all_to_all.32.recv = bf16[16,16,128]{2,1,0:T(8,128)(2,1)S(1)} all-to-all(bf16[16,16,128]{2,1,0:T(8,128)(2,1)S(1)} %shard_map.164), channel_id=1, replica_groups=mesh['sweep'=16,'azim'=32] {'sweep'}, dimensions={0} | all-to-all | bytes 131072 | tf_op jit(solution)/shard_map/all_to_all | solution.py:613
  145.2 0.7 shard_map.165
  (24 shorter events, 0.1 us)
Async XLA Ops:
  18.5 8.2 %copy-start = (bf16[2,8,32,512]{3,2,1,0:T(8,128)(2,1)S(1)}, bf16[2,8,32,512]{3,2,1,0:T(8,128)(2,1)}, u32[]{:S(2)}) copy-start(bf16[2,8,32,512]{3,2,1,0:T(8,128)(2,1)} %lat.9) | copy-start | bytes 1572868
  18.5 26.6 %all-to-all-start.1 = ((bf16[16,2,16,512]{3,2,1,0:T(8,128)(2,1)}), bf16[16,2,16,512]{3,2,1,0:T(8,128)(2,1)S(1)}, u32[]{:S(2)}, u32[]{:S(2)}) async-start(bf16[16,2,16,512]{3,2,1,0:T(8,128)(2,1)} %get-tuple-element.29), calls=%async_computation.1 | async-start | bytes 1048576 | tf_op jit(solution)/shard_map/all_to_all | solution.py:495
  26.7 0.7 copy-start.3
  27.3 4.9 %copy-start.2 = (f32[9,512]{1,0:T(8,128)S(1)}, f32[9,512]{1,0:T(8,128)}, u32[]{:S(2)}) copy-start(f32[9,512]{1,0:T(8,128)} %taps.1) | copy-start | bytes 55300
  27.3 4.9 %copy-start.4 = (f32[512]{0:T(512)S(1)}, f32[512]{0:T(512)}, u32[]{:S(2)}) copy-start(f32[512]{0:T(512)} %param.12) | copy-start | bytes 6148
  27.4 15.6 %collective-permute-start.1 = (bf16[2,8,512]{2,1,0:T(8,128)(2,1)S(1)}, bf16[2,8,512]{2,1,0:T(8,128)(2,1)S(1)}, u32[]{:S(2)}, u32[]{:S(2)}) collective-permute-start(bf16[2,8,512]{2,1,0:T(8,128)(2,1)S(1)} %shard_map.153.after), channel_id=1, source_target_pairs={{0,31},{1,2},{2,1},{3,4},{4,3},{5,6},{6,5},{7,8},{8,7},{9,10},{10,... | collective-permute-start | bytes 49160 | tf_op jit(solution)/shard_map/ppermute | solution.py:499
  32.3 11.5 %collective-permute-start = (bf16[2,8,512]{2,1,0:T(8,128)(2,1)S(1)}, bf16[2,8,512]{2,1,0:T(8,128)(2,1)S(1)}, u32[]{:S(2)}, u32[]{:S(2)}) collective-permute-start(bf16[2,8,512]{2,1,0:T(8,128)(2,1)S(1)} %get-tuple-element.27), channel_id=1, source_target_pairs={{0,1},{1,0},{2,3},{3,2},{4,5},{5,4},{6,7},{7,6},{8,9},{9,8},{10,11... | collective-permute-start | bytes 49160 | tf_op jit(solution)/shard_map/ppermute | solution.py:509
  43.9 22.5 %copy-start.9 = (f32[512]{0:T(512)S(1)}, f32[512]{0:T(512)}, u32[]{:S(2)}) copy-start(f32[512]{0:T(512)} %param.13) | copy-start | bytes 6148
  45.1 21.3 %copy-start.5 = (bf16[512,256]{1,0:T(8,128)(2,1)S(1)}, bf16[512,256]{1,0:T(8,128)(2,1)}, u32[]{:S(2)}) copy-start(bf16[512,256]{1,0:T(8,128)(2,1)} %w_query.1) | copy-start | bytes 786436
  45.1 21.3 %copy-start.6 = (bf16[512,256]{1,0:T(8,128)(2,1)S(1)}, bf16[512,256]{1,0:T(8,128)(2,1)}, u32[]{:S(2)}) copy-start(bf16[512,256]{1,0:T(8,128)(2,1)} %w_key.1) | copy-start | bytes 786436
  45.1 21.3 %copy-start.7 = (bf16[512,256]{1,0:T(8,128)(2,1)S(1)}, bf16[512,256]{1,0:T(8,128)(2,1)}, u32[]{:S(2)}) copy-start(bf16[512,256]{1,0:T(8,128)(2,1)} %w_value.1) | copy-start | bytes 786436
  45.1 21.3 %copy-start.8 = (bf16[512,256]{1,0:T(8,128)(2,1)S(1)}, bf16[512,256]{1,0:T(8,128)(2,1)}, u32[]{:S(2)}) copy-start(bf16[512,256]{1,0:T(8,128)(2,1)} %w_output.1) | copy-start | bytes 786436
  70.4 19.9 %all-to-all-start.2 = ((bf16[16,2,16,512]{3,2,1,0:T(8,128)(2,1)}), bf16[16,2,16,512]{3,2,1,0:T(8,128)(2,1)S(1)}, u32[]{:S(2)}, u32[]{:S(2)}) async-start(bf16[16,2,16,512]{3,2,1,0:T(8,128)(2,1)} %get-tuple-element.30), calls=%async_computation.2 | async-start | bytes 1048576 | tf_op jit(solution)/shard_map/all_to_all | solution.py:546
  74.5 6.0 %collective-permute-start.2 = (bf16[2,16,64,128]{3,2,1,0:T(8,128)(2,1)S(1)}, bf16[2,16,64,128]{3,2,1,0:T(8,128)(2,1)S(1)}, u32[]{:S(2)}, u32[]{:S(2)}) collective-permute-start(bf16[2,16,64,128]{3,2,1,0:T(8,128)(2,1)S(1)} %slice_bitcast_fusion), channel_id=1, source_target_pairs={{0,1},{1,0},{2,3},{3,2},{4,5},{5,4},{6,7},{7,6},{8,9},{9,8},{10,11... | collective-permute-start | bytes 1572872 | tf_op jit(solution)/shard_map/ppermute | solution.py:547
  80.6 9.6 %copy-start.1 = (bf16[2,8,32,512]{3,2,1,0:T(8,128)(2,1)S(1)}, bf16[2,8,32,512]{3,2,1,0:T(8,128)(2,1)}, u32[]{:S(2)}) copy-start(bf16[2,8,32,512]{3,2,1,0:T(8,128)(2,1)} %cot.9) | copy-start | bytes 1572868
  80.7 9.5 %collective-permute-start.3 = (bf16[16,64,128]{2,1,0:T(8,128)(2,1)S(1)}, bf16[16,64,128]{2,1,0:T(8,128)(2,1)S(1)}, u32[]{:S(2)}, u32[]{:S(2)}) collective-permute-start(bf16[16,64,128]{2,1,0:T(8,128)(2,1)S(1)} %get-tuple-element.34), channel_id=1, source_target_pairs={{0,2},{1,3},{2,0},{3,1},{4,6},{5,7},{6,4},{7,5},{8,10},{9,11},{10,... | collective-permute-start | bytes 786440 | tf_op jit(solution)/shard_map/ppermute | solution.py:550
  110.3 25.1 %all-to-all-start.4 = ((bf16[32,16,128]{2,1,0:T(8,128)(2,1)}), bf16[32,16,128]{2,1,0:T(8,128)(2,1)S(1)}, u32[]{:S(2)}, u32[]{:S(2)}) async-start(bf16[32,16,128]{2,1,0:T(8,128)(2,1)} %shard_map.160.after), calls=%async_computation.4 | async-start | bytes 262144 | tf_op jit(solution)/shard_map/all_to_all | solution.py:578
  120.5 11.7 %collective-permute-start.5 = (bf16[2,2,8,512]{3,2,1,0:T(8,128)(2,1)S(1)}, bf16[2,2,8,512]{3,2,1,0:T(8,128)(2,1)S(1)}, u32[]{:S(2)}, u32[]{:S(2)}) collective-permute-start(bf16[2,2,8,512]{3,2,1,0:T(8,128)(2,1)S(1)} %shard_map.162), channel_id=1, source_target_pairs={{0,31},{1,2},{2,1},{3,4},{4,3},{5,6},{6,5},{7,8},{8,7},{9,10},{10,... | collective-permute-start | bytes 98312 | tf_op jit(solution)/shard_map/ppermute | solution.py:596
  124.0 9.0 %collective-permute-start.4 = (bf16[2,2,8,512]{3,2,1,0:T(8,128)(2,1)S(1)}, bf16[2,2,8,512]{3,2,1,0:T(8,128)(2,1)S(1)}, u32[]{:S(2)}, u32[]{:S(2)}) collective-permute-start(bf16[2,2,8,512]{3,2,1,0:T(8,128)(2,1)S(1)} %shard_map.161.after), channel_id=1, source_target_pairs={{0,1},{1,0},{2,3},{3,2},{4,5},{5,4},{6,7},{7,6},{8,9},{9,8},{10,11... | collective-permute-start | bytes 98312 | tf_op jit(solution)/shard_map/ppermute | solution.py:594

commit v10 on v8

--- a/solution.py
+++ b/solution.py
@@ -361,7 +361,9 @@
     out[...] = partner_column(spot, for_core, edges[0], edges[1]).astype(BF16)
 
 
-def latents_kernel(spot, after, lat, cot, ret, other_core, other_chip, taps, out, edge_l, edge_r):
+def latents_kernel(
+    spot, after, lat, cot, ret, other_core, other_chip, taps, out, edge_l, edge_r, near, sems
+):
     del after
     for s in range(SL):
         left, right = from_partners(
@@ -403,7 +405,16 @@
             total = cols[1] + from_left + from_right
             value = lat[s, h, :, here].astype(F32)
             sig = 1.0 / (1.0 + jnp.exp(-value))
-            out[s, h, :, here] = grads[h] + total * (sig * (1.0 + value * (1.0 - sig)))
+            near[s, h, :, here] = grads[h] + total * (sig * (1.0 + value * (1.0 - sig)))
+        pltpu.make_async_copy(
+            near.at[s, :, :, here], out.at[s, :, :, here], sems.at[step]
+        ).start()
+
+    for step in range(SL * PARTS):
+        s, here = step // PARTS, pl.ds(step % PARTS * LANES, LANES)
+        pltpu.make_async_copy(
+            near.at[s, :, :, here], out.at[s, :, :, here], sems.at[step]
+        ).wait()
 
 
 def high_low(value):
@@ -570,20 +581,22 @@
             scratch=[pltpu.VMEM((2, 2, SL, H, C), F32)],
         )(spot, after, cotangent, ret)
 
-    to_chip = back_edges(False, second_sent)
+    to_core = back_edges(True, second_sent)
+    back_core = lax.ppermute(to_core, "azim", cores)
+    to_chip = back_edges(False, to_core)
     back_chip = lax.ppermute(to_chip, "azim", chips)
-    to_core = back_edges(True, to_chip)
-    back_core = lax.ppermute(to_core, "azim", cores)
-
-    grad_latents = call(
+
+    grad_latents = pl.pallas_call(
         latents_kernel,
-        struct((SL, H, WL, C), F32),
-        16,
-        flops=10_000_000,
-        moved=4_000_000,
-        smem=1,
-        hbm=(1,),
-        scratch=[edge, edge],
+        out_shape=struct((SL, H, WL, C), F32),
+        in_specs=[pl.BlockSpec(memory_space=pltpu.SMEM), anywhere] + [vmem] * 6,
+        out_specs=anywhere,
+        scratch_shapes=[edge, edge]
+        + [pltpu.VMEM((SL, H, WL, C), F32), pltpu.SemaphoreType.DMA((SL * PARTS,))],
+        compiler_params=params(16),
+        cost_estimate=pl.CostEstimate(
+            flops=10_000_000, bytes_accessed=4_000_000, transcendentals=0
+        ),
     )(spot, second_sent, latents, cotangent, ret, back_core, back_chip, table)
     second_recv, grad_latents = lax.optimization_barrier((second_recv, grad_latents))
 

time: 131 us -> 130 us (level)
  the two profiles are of different devices: /device:TPU:32 before, /device:TPU:1 now
where the time goes in v10:
time: 130 us; the launch traced here: 129 us
  starting transfers between devices  57.2 us (44%)
  blocking collectives  47.9 us (37%)
  Pallas kernels  11.3 us (9%)
  waiting for transfers between devices  10.6 us (8%)
    all_to_all x1, blocking collectives, on_device(): lax.all_to_all(sent, 'sweep', split_axis=0, concat_axis=0, tiled=True)  20.1 us
    all_to_all x1, blocking collectives, on_device(): lax.all_to_all(first_sent, 'sweep', split_axis=0, concat_axis=0, tiled=True)  18 us
    ppermute x1, starting transfers between devices, on_device(): other_core = lax.ppermute(to_core, 'azim', cores)  10.7 us
    all_to_all x1, starting transfers between devices, on_device(): lax.all_to_all(second_sent, 'azim', split_axis=0, concat_axis=0, tiled=True)  10.1 us
    all_to_all x1, blocking collectives, on_device(): lax.all_to_all(third_sent, 'sweep', split_axis=0, concat_axis=0, tiled=True)  9.79 us
    ppermute x1, starting transfers between devices, on_device(): back_core = lax.ppermute(to_core, 'azim', cores)  8.16 us
    all_to_all x1, starting transfers between devices, on_device(): lax.all_to_all(cot_sent, 'sweep', split_axis=0, concat_axis=0, tiled=True)  8.12 us
    pallas_call x12, Pallas kernels, run(): pl.pallas_call(kernel, out_shape=outs, in_specs=specs, out_specs=jax.tree...  7.93 us
  transfers between devices with their start and end apart: 9, of which 4 were waited for; matrix products, arithmetic and copies ran while one was open for 0% of the time, Pallas kernels for 3%

profile of v10, /device:TPU:1, one launch (start us, length us, event | category | flops | bytes accessed | tf_op | source)
XLA Modules:
  0.0 129.1 jit_solution(4965710428502594082)
XLA Ops:
  0.6 0.0 copy-start.1
  0.6 1.0 copy-done.1
  1.7 0.8 shard_map.152.after
  2.5 8.1 %all-to-all-start.1 = ((bf16[16,2,16,512]{3,2,1,0:T(8,128)(2,1)}), bf16[16,2,16,512]{3,2,1,0:T(8,128)(2,1)S(1)}, u32[]{:S(2)}, u32[]{:S(2)}) async-start(bf16[16,2,16,512]{3,2,1,0:T(8,128)(2,1)} %shard_map.152.after), calls=%async_computation.1 | async-start | bytes 1048576 | tf_op jit(solution)/shard_map/all_to_all | solution.py:486
  10.7 0.0 copy-start.3
  10.7 0.1 shard_map.153.after
  10.7 4.8 %collective-permute-start.1 = (bf16[2,8,512]{2,1,0:T(8,128)(2,1)S(1)}, bf16[2,8,512]{2,1,0:T(8,128)(2,1)S(1)}, u32[]{:S(2)}, u32[]{:S(2)}) collective-permute-start(bf16[2,8,512]{2,1,0:T(8,128)(2,1)S(1)} %shard_map.153.after), channel_id=1, source_target_pairs={{0,31},{1,2},{2,1},{3,4},{4,3},{5,6},{6,5},{7,8},{8,7},{9,10},{10,... | collective-permute-start | bytes 49160 | tf_op jit(solution)/shard_map/ppermute | solution.py:490
  15.6 0.1 shard_map.154
  15.7 10.7 %collective-permute-start = (bf16[2,8,512]{2,1,0:T(8,128)(2,1)S(1)}, bf16[2,8,512]{2,1,0:T(8,128)(2,1)S(1)}, u32[]{:S(2)}, u32[]{:S(2)}) collective-permute-start(bf16[2,8,512]{2,1,0:T(8,128)(2,1)S(1)} %get-tuple-element.24), channel_id=1, source_target_pairs={{0,1},{1,0},{2,3},{3,2},{4,5},{5,4},{6,7},{7,6},{8,9},{9,8},{10,11... | collective-permute-start | bytes 49160 | tf_op jit(solution)/shard_map/ppermute | solution.py:500
  26.4 0.8 collective-permute-done.other_core
  27.2 1.2 shard_map.155
  28.5 20.1 %all_to_all.30.recv = bf16[16,2,16,512]{3,2,1,0:T(8,128)(2,1)S(1)} all-to-all(bf16[16,2,16,512]{3,2,1,0:T(8,128)(2,1)S(1)} %shard_map.155), channel_id=1, replica_groups=mesh['sweep'=16,'azim'=32] {'sweep'}, dimensions={0} | all-to-all | bytes 1048576 | tf_op jit(solution)/shard_map/all_to_all | solution.py:511
  48.6 4.0 %shard_map.156 = (bf16[16,2,16,512]{3,2,1,0:T(8,128)(2,1)}, bf16[2,2,16,64,128]{4,3,2,1,0:T(8,128)(2,1)S(1)}, f32[1,512]{1,0:T(1,128)S(1)}) custom-call(s32[1]{0:T(128)} %bitcast.spot, bf16[16,2,16,512]{3,2,1,0:T(8,128)(2,1)S(1)} %all_to_all.30.recv, bf16[16,2,16,512]{3,2,1,0:T(8,128)(2,1)S(1)} %all-to-all-done.1.recv_cot, bf16[512,256]{1,0:T(8,128)(2,1)S(1)} %copy-done.5, ...), custom_call_target="tpu_custom_call" | custom-call | flops 2000000000 | bytes 6000000 | tf_op jit(solution)/shard_map/pallas_call | solution.py:37
  52.6 3.9 %all-to-all-start.2 = ((bf16[16,2,16,512]{3,2,1,0:T(8,128)(2,1)}), bf16[16,2,16,512]{3,2,1,0:T(8,128)(2,1)S(1)}, u32[]{:S(2)}, u32[]{:S(2)}) async-start(bf16[16,2,16,512]{3,2,1,0:T(8,128)(2,1)} %get-tuple-element.26), calls=%async_computation.2 | async-start | bytes 1048576 | tf_op jit(solution)/shard_map/all_to_all | solution.py:537
  56.5 5.8 %collective-permute-start.2 = (bf16[2,16,64,128]{3,2,1,0:T(8,128)(2,1)S(1)}, bf16[2,16,64,128]{3,2,1,0:T(8,128)(2,1)S(1)}, u32[]{:S(2)}, u32[]{:S(2)}) collective-permute-start(bf16[2,16,64,128]{3,2,1,0:T(8,128)(2,1)S(1)} %slice_bitcast_fusion), channel_id=1, source_target_pairs={{0,1},{1,0},{2,3},{3,2},{4,5},{5,4},{6,7},{7,6},{8,9},{9,8},{10,11... | collective-permute-start | bytes 1572872 | tf_op jit(solution)/shard_map/ppermute | solution.py:538
  62.3 1.5 %collective-permute-done.2.got = bf16[2,16,64,128]{3,2,1,0:T(8,128)(2,1)S(1)} collective-permute-done((bf16[2,16,64,128]{3,2,1,0:T(8,128)(2,1)S(1)}, bf16[2,16,64,128]{3,2,1,0:T(8,128)(2,1)S(1)}, u32[]{:S(2)}, u32[]{:S(2)}) %collective-permute-start.2) | collective-permute-done | bytes 524320 | tf_op jit(solution)/shard_map/ppermute | solution.py:538
  63.9 0.1 shard_map.157
  64.0 2.1 %collective-permute-start.3 = (bf16[16,64,128]{2,1,0:T(8,128)(2,1)S(1)}, bf16[16,64,128]{2,1,0:T(8,128)(2,1)S(1)}, u32[]{:S(2)}, u32[]{:S(2)}) collective-permute-start(bf16[16,64,128]{2,1,0:T(8,128)(2,1)S(1)} %get-tuple-element.30), channel_id=1, source_target_pairs={{0,2},{1,3},{2,0},{3,1},{4,6},{5,7},{6,4},{7,5},{8,10},{9,11},{10,... | collective-permute-start | bytes 786440 | tf_op jit(solution)/shard_map/ppermute | solution.py:541
  66.0 7.5 %collective-permute-done.3.got = bf16[16,64,128]{2,1,0:T(8,128)(2,1)S(1)} collective-permute-done((bf16[16,64,128]{2,1,0:T(8,128)(2,1)S(1)}, bf16[16,64,128]{2,1,0:T(8,128)(2,1)S(1)}, u32[]{:S(2)}, u32[]{:S(2)}) %collective-permute-start.3) | collective-permute-done | bytes 262176 | tf_op jit(solution)/shard_map/ppermute | solution.py:541
  73.5 0.1 shard_map.158.sums_in
  73.6 1.3 %shard_map.159 = bf16[16,80,128]{2,1,0:T(8,128)(2,1)S(1)} custom-call(s32[1]{0:T(128)} %bitcast.spot, bf16[2,8,32,512]{3,2,1,0:T(8,128)(2,1)S(1)} %copy-done, bf16[2,8,512]{2,1,0:T(8,128)(2,1)S(1)} %collective-permute-done.other_core, bf16[2,8,512]{2,1,0:T(8,128)(2,1)S(1)} %collective-permute-done.1.other_chip, ...), custom_call_target="tpu_custom_call", output_to_operand_aliasing={{}: (7, {})} | custom-call | flops 10000000 | bytes 2000000 | tf_op jit(solution)/shard_map/pallas_call | solution.py:547
  74.9 18.0 %all_to_all.31.recv = bf16[16,80,128]{2,1,0:T(8,128)(2,1)S(1)} all-to-all(bf16[16,80,128]{2,1,0:T(8,128)(2,1)S(1)} %shard_map.159), channel_id=1, replica_groups=mesh['sweep'=16,'azim'=32] {'sweep'}, dimensions={0} | all-to-all | bytes 655360 | tf_op jit(solution)/shard_map/all_to_all | solution.py:565
  92.9 0.7 shard_map.160.after
  93.6 10.1 %all-to-all-start.4 = ((bf16[32,16,128]{2,1,0:T(8,128)(2,1)}), bf16[32,16,128]{2,1,0:T(8,128)(2,1)S(1)}, u32[]{:S(2)}, u32[]{:S(2)}) async-start(bf16[32,16,128]{2,1,0:T(8,128)(2,1)} %shard_map.160.after), calls=%async_computation.4 | async-start | bytes 262144 | tf_op jit(solution)/shard_map/all_to_all | solution.py:569
  103.7 0.1 shard_map.161.after
  103.8 0.1 shard_map.162
  103.9 3.5 %collective-permute-start.5 = (bf16[2,2,8,512]{3,2,1,0:T(8,128)(2,1)S(1)}, bf16[2,2,8,512]{3,2,1,0:T(8,128)(2,1)S(1)}, u32[]{:S(2)}, u32[]{:S(2)}) collective-permute-start(bf16[2,2,8,512]{3,2,1,0:T(8,128)(2,1)S(1)} %shard_map.162), channel_id=1, source_target_pairs={{0,31},{1,2},{2,1},{3,4},{4,3},{5,6},{6,5},{7,8},{8,7},{9,10},{10,... | collective-permute-start | bytes 98312 | tf_op jit(solution)/shard_map/ppermute | solution.py:587
  107.5 8.2 %collective-permute-start.4 = (bf16[2,2,8,512]{3,2,1,0:T(8,128)(2,1)S(1)}, bf16[2,2,8,512]{3,2,1,0:T(8,128)(2,1)S(1)}, u32[]{:S(2)}, u32[]{:S(2)}) collective-permute-start(bf16[2,2,8,512]{3,2,1,0:T(8,128)(2,1)S(1)} %shard_map.161.after), channel_id=1, source_target_pairs={{0,1},{1,0},{2,3},{3,2},{4,5},{5,4},{6,7},{7,6},{8,9},{9,8},{10,11... | collective-permute-start | bytes 98312 | tf_op jit(solution)/shard_map/ppermute | solution.py:585
  115.7 0.8 collective-permute-done.4.other_core
  116.5 2.1 %shard_map.163 = f32[2,8,32,512]{3,2,1,0:T(8,128)} custom-call(s32[1]{0:T(128)} %bitcast.spot, bf16[32,16,128]{2,1,0:T(8,128)(2,1)} %shard_map.160.after, bf16[2,8,32,512]{3,2,1,0:T(8,128)(2,1)S(1)} %copy-done, bf16[2,8,32,512]{3,2,1,0:T(8,128)(2,1)S(1)} %copy-done.2, bf16[16,2,16,512]{3,2,1,0:T(8,128)(2,1)S(1)} %all-to-all-done.2.ret, ...), custom_call_target="tpu_custom_call" | custom-call | flops 10000000 | bytes 4000000 | tf_op jit(solution)/shard_map/pallas_call | solution.py:589
  118.7 9.8 %all_to_all.32.recv = bf16[16,16,128]{2,1,0:T(8,128)(2,1)S(1)} all-to-all(bf16[16,16,128]{2,1,0:T(8,128)(2,1)S(1)} %shard_map.164), channel_id=1, replica_groups=mesh['sweep'=16,'azim'=32] {'sweep'}, dimensions={0} | all-to-all | bytes 131072 | tf_op jit(solution)/shard_map/all_to_all | solution.py:606
  128.4 0.7 shard_map.165
  (24 shorter events, 0.1 us)
Async XLA Ops:
  0.6 1.0 copy-start.1
  2.5 8.1 %copy-start = (bf16[2,8,32,512]{3,2,1,0:T(8,128)(2,1)S(1)}, bf16[2,8,32,512]{3,2,1,0:T(8,128)(2,1)}, u32[]{:S(2)}) copy-start(bf16[2,8,32,512]{3,2,1,0:T(8,128)(2,1)} %lat.9) | copy-start | bytes 1572868
  2.5 25.9 %all-to-all-start.1 = ((bf16[16,2,16,512]{3,2,1,0:T(8,128)(2,1)}), bf16[16,2,16,512]{3,2,1,0:T(8,128)(2,1)S(1)}, u32[]{:S(2)}, u32[]{:S(2)}) async-start(bf16[16,2,16,512]{3,2,1,0:T(8,128)(2,1)} %shard_map.152.after), calls=%async_computation.1 | async-start | bytes 1048576 | tf_op jit(solution)/shard_map/all_to_all | solution.py:486
  10.7 4.9 %copy-start.3 = (f32[9,512]{1,0:T(8,128)S(1)}, f32[9,512]{1,0:T(8,128)}, u32[]{:S(2)}) copy-start(f32[9,512]{1,0:T(8,128)} %taps.1) | copy-start | bytes 55300
  10.7 4.9 %copy-start.4 = (f32[512]{0:T(512)S(1)}, f32[512]{0:T(512)}, u32[]{:S(2)}) copy-start(f32[512]{0:T(512)} %param.12) | copy-start | bytes 6148
  10.7 15.6 %collective-permute-start.1 = (bf16[2,8,512]{2,1,0:T(8,128)(2,1)S(1)}, bf16[2,8,512]{2,1,0:T(8,128)(2,1)S(1)}, u32[]{:S(2)}, u32[]{:S(2)}) collective-permute-start(bf16[2,8,512]{2,1,0:T(8,128)(2,1)S(1)} %shard_map.153.after), channel_id=1, source_target_pairs={{0,31},{1,2},{2,1},{3,4},{4,3},{5,6},{6,5},{7,8},{8,7},{9,10},{10,... | collective-permute-start | bytes 49160 | tf_op jit(solution)/shard_map/ppermute | solution.py:490
  15.7 11.5 %collective-permute-start = (bf16[2,8,512]{2,1,0:T(8,128)(2,1)S(1)}, bf16[2,8,512]{2,1,0:T(8,128)(2,1)S(1)}, u32[]{:S(2)}, u32[]{:S(2)}) collective-permute-start(bf16[2,8,512]{2,1,0:T(8,128)(2,1)S(1)} %get-tuple-element.24), channel_id=1, source_target_pairs={{0,1},{1,0},{2,3},{3,2},{4,5},{5,4},{6,7},{7,6},{8,9},{9,8},{10,11... | collective-permute-start | bytes 49160 | tf_op jit(solution)/shard_map/ppermute | solution.py:500
  27.2 21.4 %copy-start.9 = (f32[512]{0:T(512)S(1)}, f32[512]{0:T(512)}, u32[]{:S(2)}) copy-start(f32[512]{0:T(512)} %param.13) | copy-start | bytes 6148
  28.4 20.2 %copy-start.5 = (bf16[512,256]{1,0:T(8,128)(2,1)S(1)}, bf16[512,256]{1,0:T(8,128)(2,1)}, u32[]{:S(2)}) copy-start(bf16[512,256]{1,0:T(8,128)(2,1)} %w_query.1) | copy-start | bytes 786436
  28.4 20.2 %copy-start.6 = (bf16[512,256]{1,0:T(8,128)(2,1)S(1)}, bf16[512,256]{1,0:T(8,128)(2,1)}, u32[]{:S(2)}) copy-start(bf16[512,256]{1,0:T(8,128)(2,1)} %w_key.1) | copy-start | bytes 786436
  28.4 20.2 %copy-start.7 = (bf16[512,256]{1,0:T(8,128)(2,1)S(1)}, bf16[512,256]{1,0:T(8,128)(2,1)}, u32[]{:S(2)}) copy-start(bf16[512,256]{1,0:T(8,128)(2,1)} %w_value.1) | copy-start | bytes 786436
  28.4 20.1 %copy-start.8 = (bf16[512,256]{1,0:T(8,128)(2,1)S(1)}, bf16[512,256]{1,0:T(8,128)(2,1)}, u32[]{:S(2)}) copy-start(bf16[512,256]{1,0:T(8,128)(2,1)} %w_output.1) | copy-start | bytes 786436
  52.6 21.0 %all-to-all-start.2 = ((bf16[16,2,16,512]{3,2,1,0:T(8,128)(2,1)}), bf16[16,2,16,512]{3,2,1,0:T(8,128)(2,1)S(1)}, u32[]{:S(2)}, u32[]{:S(2)}) async-start(bf16[16,2,16,512]{3,2,1,0:T(8,128)(2,1)} %get-tuple-element.26), calls=%async_computation.2 | async-start | bytes 1048576 | tf_op jit(solution)/shard_map/all_to_all | solution.py:537
  56.5 7.3 %collective-permute-start.2 = (bf16[2,16,64,128]{3,2,1,0:T(8,128)(2,1)S(1)}, bf16[2,16,64,128]{3,2,1,0:T(8,128)(2,1)S(1)}, u32[]{:S(2)}, u32[]{:S(2)}) collective-permute-start(bf16[2,16,64,128]{3,2,1,0:T(8,128)(2,1)S(1)} %slice_bitcast_fusion), channel_id=1, source_target_pairs={{0,1},{1,0},{2,3},{3,2},{4,5},{5,4},{6,7},{7,6},{8,9},{9,8},{10,11... | collective-permute-start | bytes 1572872 | tf_op jit(solution)/shard_map/ppermute | solution.py:538
  64.0 9.6 %copy-start.2 = (bf16[2,8,32,512]{3,2,1,0:T(8,128)(2,1)S(1)}, bf16[2,8,32,512]{3,2,1,0:T(8,128)(2,1)}, u32[]{:S(2)}) copy-start(bf16[2,8,32,512]{3,2,1,0:T(8,128)(2,1)} %cot.9) | copy-start | bytes 1572868
  64.0 9.5 %collective-permute-start.3 = (bf16[16,64,128]{2,1,0:T(8,128)(2,1)S(1)}, bf16[16,64,128]{2,1,0:T(8,128)(2,1)S(1)}, u32[]{:S(2)}, u32[]{:S(2)}) collective-permute-start(bf16[16,64,128]{2,1,0:T(8,128)(2,1)S(1)} %get-tuple-element.30), channel_id=1, source_target_pairs={{0,2},{1,3},{2,0},{3,1},{4,6},{5,7},{6,4},{7,5},{8,10},{9,11},{10,... | collective-permute-start | bytes 786440 | tf_op jit(solution)/shard_map/ppermute | solution.py:541
  93.6 25.0 %all-to-all-start.4 = ((bf16[32,16,128]{2,1,0:T(8,128)(2,1)}), bf16[32,16,128]{2,1,0:T(8,128)(2,1)S(1)}, u32[]{:S(2)}, u32[]{:S(2)}) async-start(bf16[32,16,128]{2,1,0:T(8,128)(2,1)} %shard_map.160.after), calls=%async_computation.4 | async-start | bytes 262144 | tf_op jit(solution)/shard_map/all_to_all | solution.py:569
  103.9 11.7 %collective-permute-start.5 = (bf16[2,2,8,512]{3,2,1,0:T(8,128)(2,1)S(1)}, bf16[2,2,8,512]{3,2,1,0:T(8,128)(2,1)S(1)}, u32[]{:S(2)}, u32[]{:S(2)}) collective-permute-start(bf16[2,2,8,512]{3,2,1,0:T(8,128)(2,1)S(1)} %shard_map.162), channel_id=1, source_target_pairs={{0,31},{1,2},{2,1},{3,4},{4,3},{5,6},{6,5},{7,8},{8,7},{9,10},{10,... | collective-permute-start | bytes 98312 | tf_op jit(solution)/shard_map/ppermute | solution.py:587
  107.5 9.0 %collective-permute-start.4 = (bf16[2,2,8,512]{3,2,1,0:T(8,128)(2,1)S(1)}, bf16[2,2,8,512]{3,2,1,0:T(8,128)(2,1)S(1)}, u32[]{:S(2)}, u32[]{:S(2)}) collective-permute-start(bf16[2,2,8,512]{3,2,1,0:T(8,128)(2,1)S(1)} %shard_map.161.after), channel_id=1, source_target_pairs={{0,1},{1,0},{2,3},{3,2},{4,5},{5,4},{6,7},{7,6},{8,9},{9,8},{10,11... | collective-permute-start | bytes 98312 | tf_op jit(solution)/shard_map/ppermute | solution.py:585

commit v11 on v10

--- a/solution.py
+++ b/solution.py
@@ -110,10 +110,9 @@
 
 
 def pack_kernel(cot, out):
-    for s in range(SL):
-        for h in range(H):
-            out[2 * h, s] = cot[s, h, :PX, :]
-            out[2 * h + 1, s] = cot[s, h, PX:, :]
+    for h in range(H):
+        out[2 * h, 0] = cot[0, h, :PX, :]
+        out[2 * h + 1, 0] = cot[0, h, PX:, :]
 
 
 def chip_edge_kernel(spot, after, lat, out, edges):
@@ -482,7 +481,15 @@
     one_edge = struct((SL, H, C), BF16)
     column = [pltpu.VMEM((2, SL, H, C), F32)]
     packed = struct((GROUPS, SL, PX, C), BF16)
-    cot_sent = call(pack_kernel, packed, 16, moved=1_000_000)(cotangent)
+    cot_sent = pl.pallas_call(
+        pack_kernel,
+        grid=(SL,),
+        out_shape=packed,
+        in_specs=[pl.BlockSpec((1, H, WL, C), lambda s: (s, 0, 0, 0))],
+        out_specs=pl.BlockSpec((GROUPS, 1, PX, C), lambda s: (0, s, 0, 0)),
+        compiler_params=params(56),
+        cost_estimate=pl.CostEstimate(flops=0, bytes_accessed=1_000_000, transcendentals=0),
+    )(cotangent)
     recv_cot = lax.all_to_all(cot_sent, "sweep", split_axis=0, concat_axis=0, tiled=True)
     to_chip = call(
         chip_edge_kernel, one_edge, 16, moved=600_000, smem=1, hbm=(1,), scratch=column

time: 130 us -> 130 us (level)
    pallas_call x0 -> x1, Pallas kernels: none -> 1.77 us  [on_device(): pl.pallas_call(pack_kernel, grid=(SL,), out_shape=packed, in_specs=[pl.Bl...]
    pallas_call x12 -> x11, Pallas kernels: 7.93 us -> 7.1 us  [run(): pl.pallas_call(kernel, out_shape=outs, in_specs=specs, out_specs=jax.tree...]
where the time goes in v11:
time: 130 us; the launch traced here: 129 us
  starting transfers between devices  57.2 us (44%)
  blocking collectives  47.9 us (37%)
  Pallas kernels  12.3 us (9%)
  waiting for transfers between devices  10.6 us (8%)
    all_to_all x1, blocking collectives, on_device(): lax.all_to_all(sent, 'sweep', split_axis=0, concat_axis=0, tiled=True)  20.1 us
    all_to_all x1, blocking collectives, on_device(): lax.all_to_all(first_sent, 'sweep', split_axis=0, concat_axis=0, tiled=True)  18 us
    ppermute x1, starting transfers between devices, on_device(): other_core = lax.ppermute(to_core, 'azim', cores)  10.7 us
    all_to_all x1, starting transfers between devices, on_device(): lax.all_to_all(second_sent, 'azim', split_axis=0, concat_axis=0, tiled=True)  10.1 us
    all_to_all x1, blocking collectives, on_device(): lax.all_to_all(third_sent, 'sweep', split_axis=0, concat_axis=0, tiled=True)  9.79 us
    ppermute x1, starting transfers between devices, on_device(): back_core = lax.ppermute(to_core, 'azim', cores)  8.16 us
    all_to_all x1, starting transfers between devices, on_device(): lax.all_to_all(cot_sent, 'sweep', split_axis=0, concat_axis=0, tiled=True)  8.12 us
    ppermute x1, waiting for transfers between devices, on_device(): from_chip = lax.ppermute(send, 'azim', sides)  7.49 us
  transfers between devices with their start and end apart: 9, of which 4 were waited for; matrix products, arithmetic and copies ran while one was open for 0% of the time, Pallas kernels for 3%

profile of v11, /device:TPU:1, one launch (start us, length us, event | category | flops | bytes accessed | tf_op | source)
XLA Modules:
  0.0 129.0 jit_solution(12881549902018606750)
XLA Ops:
  0.6 1.8 %shard_map.152.after = bf16[16,2,16,512]{3,2,1,0:T(8,128)(2,1)} custom-call(bf16[2,8,32,512]{3,2,1,0:T(8,128)(2,1)} %cot.9), custom_call_target="tpu_custom_call" | custom-call | bytes 1000000 | tf_op jit(solution)/shard_map/pallas_call | solution.py:484
  2.4 8.1 %all-to-all-start.1 = ((bf16[16,2,16,512]{3,2,1,0:T(8,128)(2,1)}), bf16[16,2,16,512]{3,2,1,0:T(8,128)(2,1)S(1)}, u32[]{:S(2)}, u32[]{:S(2)}) async-start(bf16[16,2,16,512]{3,2,1,0:T(8,128)(2,1)} %shard_map.152.after), calls=%async_computation.1 | async-start | bytes 1048576 | tf_op jit(solution)/shard_map/all_to_all | solution.py:493
  10.6 0.0 copy-start.4
  10.6 0.1 shard_map.153.after
  10.6 4.8 %collective-permute-start.1 = (bf16[2,8,512]{2,1,0:T(8,128)(2,1)S(1)}, bf16[2,8,512]{2,1,0:T(8,128)(2,1)S(1)}, u32[]{:S(2)}, u32[]{:S(2)}) collective-permute-start(bf16[2,8,512]{2,1,0:T(8,128)(2,1)S(1)} %shard_map.153.after), channel_id=1, source_target_pairs={{0,31},{1,2},{2,1},{3,4},{4,3},{5,6},{6,5},{7,8},{8,7},{9,10},{10,... | collective-permute-start | bytes 49160 | tf_op jit(solution)/shard_map/ppermute | solution.py:497
  15.5 0.1 shard_map.154
  15.6 10.7 %collective-permute-start = (bf16[2,8,512]{2,1,0:T(8,128)(2,1)S(1)}, bf16[2,8,512]{2,1,0:T(8,128)(2,1)S(1)}, u32[]{:S(2)}, u32[]{:S(2)}) collective-permute-start(bf16[2,8,512]{2,1,0:T(8,128)(2,1)S(1)} %get-tuple-element.24), channel_id=1, source_target_pairs={{0,1},{1,0},{2,3},{3,2},{4,5},{5,4},{6,7},{7,6},{8,9},{9,8},{10,11... | collective-permute-start | bytes 49160 | tf_op jit(solution)/shard_map/ppermute | solution.py:507
  26.3 0.8 collective-permute-done.other_core
  27.1 1.2 shard_map.155
  28.3 0.0 copy-start.5
  28.3 0.0 copy-start.6
  28.4 20.1 %all_to_all.30.recv = bf16[16,2,16,512]{3,2,1,0:T(8,128)(2,1)S(1)} all-to-all(bf16[16,2,16,512]{3,2,1,0:T(8,128)(2,1)S(1)} %shard_map.155), channel_id=1, replica_groups=mesh['sweep'=16,'azim'=32] {'sweep'}, dimensions={0} | all-to-all | bytes 1048576 | tf_op jit(solution)/shard_map/all_to_all | solution.py:518
  48.5 4.0 %shard_map.156 = (bf16[16,2,16,512]{3,2,1,0:T(8,128)(2,1)}, bf16[2,2,16,64,128]{4,3,2,1,0:T(8,128)(2,1)S(1)}, f32[1,512]{1,0:T(1,128)S(1)}) custom-call(s32[1]{0:T(128)} %bitcast.spot, bf16[16,2,16,512]{3,2,1,0:T(8,128)(2,1)S(1)} %all_to_all.30.recv, bf16[16,2,16,512]{3,2,1,0:T(8,128)(2,1)S(1)} %all-to-all-done.1.recv_cot, bf16[512,256]{1,0:T(8,128)(2,1)S(1)} %copy-done.5, ...), custom_call_target="tpu_custom_call" | custom-call | flops 2000000000 | bytes 6000000 | tf_op jit(solution)/shard_map/pallas_call | solution.py:37
  52.5 3.9 %all-to-all-start.2 = ((bf16[16,2,16,512]{3,2,1,0:T(8,128)(2,1)}), bf16[16,2,16,512]{3,2,1,0:T(8,128)(2,1)S(1)}, u32[]{:S(2)}, u32[]{:S(2)}) async-start(bf16[16,2,16,512]{3,2,1,0:T(8,128)(2,1)} %get-tuple-element.26), calls=%async_computation.2 | async-start | bytes 1048576 | tf_op jit(solution)/shard_map/all_to_all | solution.py:544
  56.4 5.8 %collective-permute-start.2 = (bf16[2,16,64,128]{3,2,1,0:T(8,128)(2,1)S(1)}, bf16[2,16,64,128]{3,2,1,0:T(8,128)(2,1)S(1)}, u32[]{:S(2)}, u32[]{:S(2)}) collective-permute-start(bf16[2,16,64,128]{3,2,1,0:T(8,128)(2,1)S(1)} %slice_bitcast_fusion), channel_id=1, source_target_pairs={{0,1},{1,0},{2,3},{3,2},{4,5},{5,4},{6,7},{7,6},{8,9},{9,8},{10,11... | collective-permute-start | bytes 1572872 | tf_op jit(solution)/shard_map/ppermute | solution.py:545
  62.2 1.5 %collective-permute-done.2.got = bf16[2,16,64,128]{3,2,1,0:T(8,128)(2,1)S(1)} collective-permute-done((bf16[2,16,64,128]{3,2,1,0:T(8,128)(2,1)S(1)}, bf16[2,16,64,128]{3,2,1,0:T(8,128)(2,1)S(1)}, u32[]{:S(2)}, u32[]{:S(2)}) %collective-permute-start.2) | collective-permute-done | bytes 524320 | tf_op jit(solution)/shard_map/ppermute | solution.py:545
  63.8 0.1 shard_map.157
  63.9 2.1 %collective-permute-start.3 = (bf16[16,64,128]{2,1,0:T(8,128)(2,1)S(1)}, bf16[16,64,128]{2,1,0:T(8,128)(2,1)S(1)}, u32[]{:S(2)}, u32[]{:S(2)}) collective-permute-start(bf16[16,64,128]{2,1,0:T(8,128)(2,1)S(1)} %get-tuple-element.30), channel_id=1, source_target_pairs={{0,2},{1,3},{2,0},{3,1},{4,6},{5,7},{6,4},{7,5},{8,10},{9,11},{10,... | collective-permute-start | bytes 786440 | tf_op jit(solution)/shard_map/ppermute | solution.py:548
  66.0 7.5 %collective-permute-done.3.got = bf16[16,64,128]{2,1,0:T(8,128)(2,1)S(1)} collective-permute-done((bf16[16,64,128]{2,1,0:T(8,128)(2,1)S(1)}, bf16[16,64,128]{2,1,0:T(8,128)(2,1)S(1)}, u32[]{:S(2)}, u32[]{:S(2)}) %collective-permute-start.3) | collective-permute-done | bytes 262176 | tf_op jit(solution)/shard_map/ppermute | solution.py:548
  73.4 0.1 shard_map.158.sums_in
  73.5 1.3 %shard_map.159 = bf16[16,80,128]{2,1,0:T(8,128)(2,1)S(1)} custom-call(s32[1]{0:T(128)} %bitcast.spot, bf16[2,8,32,512]{3,2,1,0:T(8,128)(2,1)S(1)} %copy-done, bf16[2,8,512]{2,1,0:T(8,128)(2,1)S(1)} %collective-permute-done.other_core, bf16[2,8,512]{2,1,0:T(8,128)(2,1)S(1)} %collective-permute-done.1.other_chip, ...), custom_call_target="tpu_custom_call", output_to_operand_aliasing={{}: (7, {})} | custom-call | flops 10000000 | bytes 2000000 | tf_op jit(solution)/shard_map/pallas_call | solution.py:554
  74.9 18.0 %all_to_all.31.recv = bf16[16,80,128]{2,1,0:T(8,128)(2,1)S(1)} all-to-all(bf16[16,80,128]{2,1,0:T(8,128)(2,1)S(1)} %shard_map.159), channel_id=1, replica_groups=mesh['sweep'=16,'azim'=32] {'sweep'}, dimensions={0} | all-to-all | bytes 655360 | tf_op jit(solution)/shard_map/all_to_all | solution.py:572
  92.8 0.7 shard_map.160.after
  93.5 10.1 %all-to-all-start.4 = ((bf16[32,16,128]{2,1,0:T(8,128)(2,1)}), bf16[32,16,128]{2,1,0:T(8,128)(2,1)S(1)}, u32[]{:S(2)}, u32[]{:S(2)}) async-start(bf16[32,16,128]{2,1,0:T(8,128)(2,1)} %shard_map.160.after), calls=%async_computation.4 | async-start | bytes 262144 | tf_op jit(solution)/shard_map/all_to_all | solution.py:576
  103.6 0.1 shard_map.161.after
  103.7 0.1 shard_map.162
  103.8 3.5 %collective-permute-start.5 = (bf16[2,2,8,512]{3,2,1,0:T(8,128)(2,1)S(1)}, bf16[2,2,8,512]{3,2,1,0:T(8,128)(2,1)S(1)}, u32[]{:S(2)}, u32[]{:S(2)}) collective-permute-start(bf16[2,2,8,512]{3,2,1,0:T(8,128)(2,1)S(1)} %shard_map.162), channel_id=1, source_target_pairs={{0,31},{1,2},{2,1},{3,4},{4,3},{5,6},{6,5},{7,8},{8,7},{9,10},{10,... | collective-permute-start | bytes 98312 | tf_op jit(solution)/shard_map/ppermute | solution.py:594
  107.4 8.2 %collective-permute-start.4 = (bf16[2,2,8,512]{3,2,1,0:T(8,128)(2,1)S(1)}, bf16[2,2,8,512]{3,2,1,0:T(8,128)(2,1)S(1)}, u32[]{:S(2)}, u32[]{:S(2)}) collective-permute-start(bf16[2,2,8,512]{3,2,1,0:T(8,128)(2,1)S(1)} %shard_map.161.after), channel_id=1, source_target_pairs={{0,1},{1,0},{2,3},{3,2},{4,5},{5,4},{6,7},{7,6},{8,9},{9,8},{10,11... | collective-permute-start | bytes 98312 | tf_op jit(solution)/shard_map/ppermute | solution.py:592
  115.6 0.8 collective-permute-done.4.other_core
  116.4 2.1 %shard_map.163 = f32[2,8,32,512]{3,2,1,0:T(8,128)} custom-call(s32[1]{0:T(128)} %bitcast.spot, bf16[32,16,128]{2,1,0:T(8,128)(2,1)} %shard_map.160.after, bf16[2,8,32,512]{3,2,1,0:T(8,128)(2,1)S(1)} %copy-done, bf16[2,8,32,512]{3,2,1,0:T(8,128)(2,1)S(1)} %copy-done.1, bf16[16,2,16,512]{3,2,1,0:T(8,128)(2,1)S(1)} %all-to-all-done.2.ret, ...), custom_call_target="tpu_custom_call" | custom-call | flops 10000000 | bytes 4000000 | tf_op jit(solution)/shard_map/pallas_call | solution.py:596
  118.6 9.8 %all_to_all.32.recv = bf16[16,16,128]{2,1,0:T(8,128)(2,1)S(1)} all-to-all(bf16[16,16,128]{2,1,0:T(8,128)(2,1)S(1)} %shard_map.164), channel_id=1, replica_groups=mesh['sweep'=16,'azim'=32] {'sweep'}, dimensions={0} | all-to-all | bytes 131072 | tf_op jit(solution)/shard_map/all_to_all | solution.py:613
  128.3 0.7 shard_map.165
  (24 shorter events, 0.1 us)
Async XLA Ops:
  2.4 8.1 %copy-start = (bf16[2,8,32,512]{3,2,1,0:T(8,128)(2,1)S(1)}, bf16[2,8,32,512]{3,2,1,0:T(8,128)(2,1)}, u32[]{:S(2)}) copy-start(bf16[2,8,32,512]{3,2,1,0:T(8,128)(2,1)} %lat.9) | copy-start | bytes 1572868
  2.4 8.1 %copy-start.2 = (bf16[16,2,16,512]{3,2,1,0:T(8,128)(2,1)S(1)}, bf16[16,2,16,512]{3,2,1,0:T(8,128)(2,1)}, u32[]{:S(2)}) copy-start(bf16[16,2,16,512]{3,2,1,0:T(8,128)(2,1)} %shard_map.152.after) | copy-start | bytes 1572868
  2.4 25.9 %all-to-all-start.1 = ((bf16[16,2,16,512]{3,2,1,0:T(8,128)(2,1)}), bf16[16,2,16,512]{3,2,1,0:T(8,128)(2,1)S(1)}, u32[]{:S(2)}, u32[]{:S(2)}) async-start(bf16[16,2,16,512]{3,2,1,0:T(8,128)(2,1)} %shard_map.152.after), calls=%async_computation.1 | async-start | bytes 1048576 | tf_op jit(solution)/shard_map/all_to_all | solution.py:493
  10.6 4.9 %copy-start.3 = (f32[9,512]{1,0:T(8,128)S(1)}, f32[9,512]{1,0:T(8,128)}, u32[]{:S(2)}) copy-start(f32[9,512]{1,0:T(8,128)} %taps.1) | copy-start | bytes 55300
  10.6 4.9 %copy-start.4 = (f32[512]{0:T(512)S(1)}, f32[512]{0:T(512)}, u32[]{:S(2)}) copy-start(f32[512]{0:T(512)} %param.12) | copy-start | bytes 6148
  10.6 15.6 %collective-permute-start.1 = (bf16[2,8,512]{2,1,0:T(8,128)(2,1)S(1)}, bf16[2,8,512]{2,1,0:T(8,128)(2,1)S(1)}, u32[]{:S(2)}, u32[]{:S(2)}) collective-permute-start(bf16[2,8,512]{2,1,0:T(8,128)(2,1)S(1)} %shard_map.153.after), channel_id=1, source_target_pairs={{0,31},{1,2},{2,1},{3,4},{4,3},{5,6},{6,5},{7,8},{8,7},{9,10},{10,... | collective-permute-start | bytes 49160 | tf_op jit(solution)/shard_map/ppermute | solution.py:497
  15.6 11.5 %collective-permute-start = (bf16[2,8,512]{2,1,0:T(8,128)(2,1)S(1)}, bf16[2,8,512]{2,1,0:T(8,128)(2,1)S(1)}, u32[]{:S(2)}, u32[]{:S(2)}) collective-permute-start(bf16[2,8,512]{2,1,0:T(8,128)(2,1)S(1)} %get-tuple-element.24), channel_id=1, source_target_pairs={{0,1},{1,0},{2,3},{3,2},{4,5},{5,4},{6,7},{7,6},{8,9},{9,8},{10,11... | collective-permute-start | bytes 49160 | tf_op jit(solution)/shard_map/ppermute | solution.py:507
  27.1 21.4 %copy-start.9 = (f32[512]{0:T(512)S(1)}, f32[512]{0:T(512)}, u32[]{:S(2)}) copy-start(f32[512]{0:T(512)} %param.13) | copy-start | bytes 6148
  28.3 20.2 %copy-start.5 = (bf16[512,256]{1,0:T(8,128)(2,1)S(1)}, bf16[512,256]{1,0:T(8,128)(2,1)}, u32[]{:S(2)}) copy-start(bf16[512,256]{1,0:T(8,128)(2,1)} %w_query.1) | copy-start | bytes 786436
  28.3 20.2 %copy-start.6 = (bf16[512,256]{1,0:T(8,128)(2,1)S(1)}, bf16[512,256]{1,0:T(8,128)(2,1)}, u32[]{:S(2)}) copy-start(bf16[512,256]{1,0:T(8,128)(2,1)} %w_key.1) | copy-start | bytes 786436
  28.3 20.2 %copy-start.7 = (bf16[512,256]{1,0:T(8,128)(2,1)S(1)}, bf16[512,256]{1,0:T(8,128)(2,1)}, u32[]{:S(2)}) copy-start(bf16[512,256]{1,0:T(8,128)(2,1)} %w_value.1) | copy-start | bytes 786436
  28.3 20.1 %copy-start.8 = (bf16[512,256]{1,0:T(8,128)(2,1)S(1)}, bf16[512,256]{1,0:T(8,128)(2,1)}, u32[]{:S(2)}) copy-start(bf16[512,256]{1,0:T(8,128)(2,1)} %w_output.1) | copy-start | bytes 786436
  52.5 21.0 %all-to-all-start.2 = ((bf16[16,2,16,512]{3,2,1,0:T(8,128)(2,1)}), bf16[16,2,16,512]{3,2,1,0:T(8,128)(2,1)S(1)}, u32[]{:S(2)}, u32[]{:S(2)}) async-start(bf16[16,2,16,512]{3,2,1,0:T(8,128)(2,1)} %get-tuple-element.26), calls=%async_computation.2 | async-start | bytes 1048576 | tf_op jit(solution)/shard_map/all_to_all | solution.py:544
  56.4 7.3 %collective-permute-start.2 = (bf16[2,16,64,128]{3,2,1,0:T(8,128)(2,1)S(1)}, bf16[2,16,64,128]{3,2,1,0:T(8,128)(2,1)S(1)}, u32[]{:S(2)}, u32[]{:S(2)}) collective-permute-start(bf16[2,16,64,128]{3,2,1,0:T(8,128)(2,1)S(1)} %slice_bitcast_fusion), channel_id=1, source_target_pairs={{0,1},{1,0},{2,3},{3,2},{4,5},{5,4},{6,7},{7,6},{8,9},{9,8},{10,11... | collective-permute-start | bytes 1572872 | tf_op jit(solution)/shard_map/ppermute | solution.py:545
  63.9 9.6 %copy-start.1 = (bf16[2,8,32,512]{3,2,1,0:T(8,128)(2,1)S(1)}, bf16[2,8,32,512]{3,2,1,0:T(8,128)(2,1)}, u32[]{:S(2)}) copy-start(bf16[2,8,32,512]{3,2,1,0:T(8,128)(2,1)} %cot.9) | copy-start | bytes 1572868
  63.9 9.5 %collective-permute-start.3 = (bf16[16,64,128]{2,1,0:T(8,128)(2,1)S(1)}, bf16[16,64,128]{2,1,0:T(8,128)(2,1)S(1)}, u32[]{:S(2)}, u32[]{:S(2)}) collective-permute-start(bf16[16,64,128]{2,1,0:T(8,128)(2,1)S(1)} %get-tuple-element.30), channel_id=1, source_target_pairs={{0,2},{1,3},{2,0},{3,1},{4,6},{5,7},{6,4},{7,5},{8,10},{9,11},{10,... | collective-permute-start | bytes 786440 | tf_op jit(solution)/shard_map/ppermute | solution.py:548
  93.5 25.0 %all-to-all-start.4 = ((bf16[32,16,128]{2,1,0:T(8,128)(2,1)}), bf16[32,16,128]{2,1,0:T(8,128)(2,1)S(1)}, u32[]{:S(2)}, u32[]{:S(2)}) async-start(bf16[32,16,128]{2,1,0:T(8,128)(2,1)} %shard_map.160.after), calls=%async_computation.4 | async-start | bytes 262144 | tf_op jit(solution)/shard_map/all_to_all | solution.py:576
  103.8 11.7 %collective-permute-start.5 = (bf16[2,2,8,512]{3,2,1,0:T(8,128)(2,1)S(1)}, bf16[2,2,8,512]{3,2,1,0:T(8,128)(2,1)S(1)}, u32[]{:S(2)}, u32[]{:S(2)}) collective-permute-start(bf16[2,2,8,512]{3,2,1,0:T(8,128)(2,1)S(1)} %shard_map.162), channel_id=1, source_target_pairs={{0,31},{1,2},{2,1},{3,4},{4,3},{5,6},{6,5},{7,8},{8,7},{9,10},{10,... | collective-permute-start | bytes 98312 | tf_op jit(solution)/shard_map/ppermute | solution.py:594
  107.4 9.0 %collective-permute-start.4 = (bf16[2,2,8,512]{3,2,1,0:T(8,128)(2,1)S(1)}, bf16[2,2,8,512]{3,2,1,0:T(8,128)(2,1)S(1)}, u32[]{:S(2)}, u32[]{:S(2)}) collective-permute-start(bf16[2,2,8,512]{3,2,1,0:T(8,128)(2,1)S(1)} %shard_map.161.after), channel_id=1, source_target_pairs={{0,1},{1,0},{2,3},{3,2},{4,5},{5,4},{6,7},{7,6},{8,9},{9,8},{10,11... | collective-permute-start | bytes 98312 | tf_op jit(solution)/shard_map/ppermute | solution.py:592
